TPU v7x, 32 devices: a whole 2x2x4 slice. The times are simulated.
32 devices in a mesh: dp: 16 (over z, y, x), tensor: 2 (over core).
Axes of the slice: x: 2, y: 2, z: 4, core: 2. Of those that a mesh axis runs over, the one named last changes fastest.
Arguments:
- hidden_in: bfloat16 [16, 1024, 1536], P('dp', 'tensor'), may hold values from -6 to 6
- text_states: bfloat16 [16, 64, 1536], P('dp'), may hold values from -6 to 6
- norm1_gain: bfloat16 [1536], P('dp'), may hold values from 0.5 to 1.5
- norm1_bias: bfloat16 [1536], P('dp'), may hold values from -3 to 3
- self_query: bfloat16 [1536, 1536], P('tensor', 'dp'), may hold values from -0.15625 to 0.15625
- self_key: bfloat16 [1536, 1536], P('tensor', 'dp'), may hold values from -0.15625 to 0.15625
- self_value: bfloat16 [1536, 1536], P('tensor', 'dp'), may hold values from -0.15625 to 0.15625
- self_out: bfloat16 [1536, 1536], P('dp', 'tensor'), may hold values from -1.25 to 1.25
- norm2_gain: bfloat16 [1536], P('dp'), may hold values from 0.5 to 1.5
- norm2_bias: bfloat16 [1536], P('dp'), may hold values from -3 to 3
- cross_query: bfloat16 [1536, 1536], P('tensor', 'dp'), may hold values from -0.15625 to 0.15625
- cross_key: bfloat16 [1536, 1536], P('tensor', 'dp'), may hold values from -0.15625 to 0.15625
- cross_value: bfloat16 [1536, 1536], P('tensor', 'dp'), may hold values from -0.15625 to 0.15625
- cross_out: bfloat16 [1536, 1536], P('dp', 'tensor'), may hold values from -0.625 to 0.625
- norm3_gain: bfloat16 [1536], P('dp'), may hold values from 0.5 to 1.5
- norm3_bias: bfloat16 [1536], P('dp'), may hold values from -3 to 3
- hidden_up: bfloat16 [6144, 1536], P('tensor', 'dp'), may hold values from -0.15625 to 0.15625
- hidden_down: bfloat16 [1536, 6144], P('dp', 'tensor'), may hold values from -0.15625 to 0.15625
- cotangent: bfloat16 [16, 1024, 1536], P('dp', 'tensor'), may hold values from -6 to 6
Outputs:
- layer_out: bfloat16 [16, 1024, 1536], P('dp', 'tensor')
- grad_input: float32 [16, 1024, 1536], P('dp', 'tensor')
- grad_text: float32 [16, 64, 1536], P('dp', None, 'tensor')
- grad_norm1_gain: float32 [1536], P('dp')
- grad_norm1_bias: float32 [1536], P('dp')
- grad_self_query: float32 [1536, 1536], P('tensor', 'dp')
- grad_self_key: float32 [1536, 1536], P('tensor', 'dp')
- grad_self_value: float32 [1536, 1536], P('tensor', 'dp')
- grad_self_out: float32 [1536, 1536], P('dp', 'tensor')
- grad_norm2_gain: float32 [1536], P('dp')
- grad_norm2_bias: float32 [1536], P('dp')
- grad_cross_query: float32 [1536, 1536], P('tensor', 'dp')
- grad_cross_key: float32 [1536, 1536], P('tensor', 'dp')
- grad_cross_value: float32 [1536, 1536], P('tensor', 'dp')
- grad_cross_out: float32 [1536, 1536], P('dp', 'tensor')
- grad_norm3_gain: float32 [1536], P('dp')
- grad_norm3_bias: float32 [1536], P('dp')
- grad_hidden_up: float32 [6144, 1536], P('tensor', 'dp')
- grad_hidden_down: float32 [1536, 6144], P('dp', 'tensor')
All inputs are finite; a program needn't handle non-finite values.
Results may differ from a plain program's by a relative error of at most 0.025.
Values may be sent and summed in bfloat16 or wider, within the bound.
A program may use at most 384 MiB of HBM per device.

v0:
```python
import jax
import jax.numpy as jnp
from jax import lax
from jax.sharding import PartitionSpec as P

HEAD_DIM = 64


norm_eps = 1e-05
score_scale = 0.125


def layer_norm(values, gain, shift):
    centre = jnp.mean(values, axis=-1, keepdims=True)
    offset = values - centre
    spread = jnp.mean(offset * offset, axis=-1, keepdims=True)
    return offset * lax.rsqrt(spread + norm_eps) * gain + shift


def gelu_exact(values):
    return jax.nn.gelu(values, approximate=False)


def project(row_data, weight):
    return jnp.einsum("cli,oi->clo", row_data, weight, preferred_element_type=jnp.float32)


def split_heads(values):
    return values.reshape(values.shape[0], values.shape[1], -1, HEAD_DIM)


def flatten_heads(values):
    return values.reshape(values.shape[0], values.shape[1], -1)


def causal_keep(first_row, count, length):
    row_ids = first_row + lax.broadcasted_iota(jnp.int32, (count, length), 0)
    col_ids = lax.broadcasted_iota(jnp.int32, (count, length), 1)
    return col_ids <= row_ids


def block_scores(queries, key_rows, first_row, block_rows, key_end, causal):
    scores = (
        jnp.einsum(
            "cqhe,ckhe->chqk",
            queries[:, first_row : first_row + block_rows],
            key_rows[:, :key_end],
            preferred_element_type=jnp.float32,
        )
        * score_scale
    )
    if causal:
        scores = jnp.where(causal_keep(first_row, block_rows, key_end), scores, -1e30)
    return scores


def attend(queries, key_rows, val_rows, causal):
    length = queries.shape[1]
    block_rows = min(512, length)
    outputs = []
    log_sums = []
    for block_num in range(length // block_rows):
        first_row = block_num * block_rows
        key_end = first_row + block_rows if causal else key_rows.shape[1]
        scores = block_scores(queries, key_rows, first_row, block_rows, key_end, causal)
        row_peak = jnp.max(scores, axis=-1, keepdims=True)
        exp_scores = jnp.exp(scores - row_peak)
        row_total = jnp.sum(exp_scores, axis=-1, keepdims=True)
        soft_weights = (exp_scores / row_total).astype(jnp.bfloat16)
        outputs.append(
            jnp.einsum(
                "chqk,ckhe->cqhe",
                soft_weights,
                val_rows[:, :key_end],
                preferred_element_type=jnp.float32,
            ).astype(jnp.bfloat16)
        )
        log_sums.append((row_peak + jnp.log(row_total))[..., 0])
    return (jnp.concatenate(outputs, axis=1), jnp.concatenate(log_sums, axis=2))


def attend_back(queries, key_rows, val_rows, grad_out, log_sums, causal):
    length = queries.shape[1]
    block_rows = min(512, length)
    grad_keys = jnp.zeros(key_rows.shape, jnp.float32)
    grad_vals = jnp.zeros(val_rows.shape, jnp.float32)
    grad_queries = []
    for block_num in range(length // block_rows):
        first_row = block_num * block_rows
        key_end = first_row + block_rows if causal else key_rows.shape[1]
        query_blk = queries[:, first_row : first_row + block_rows]
        grad_blk = grad_out[:, first_row : first_row + block_rows]
        scores = block_scores(queries, key_rows, first_row, block_rows, key_end, causal)
        soft = jnp.exp(scores - log_sums[:, :, first_row : first_row + block_rows, None])
        grad_soft = jnp.einsum(
            "cqhe,ckhe->chqk", grad_blk, val_rows[:, :key_end], preferred_element_type=jnp.float32
        )
        grad_vals = grad_vals.at[:, :key_end].add(
            jnp.einsum(
                "chqk,cqhe->ckhe",
                soft.astype(jnp.bfloat16),
                grad_blk,
                preferred_element_type=jnp.float32,
            )
        )
        inner = jnp.sum(soft * grad_soft, axis=-1, keepdims=True)
        grad_scores = (soft * (grad_soft - inner)).astype(jnp.bfloat16)
        grad_queries.append(
            jnp.einsum(
                "chqk,ckhe->cqhe",
                grad_scores,
                key_rows[:, :key_end],
                preferred_element_type=jnp.float32,
            )
            * score_scale
        )
        grad_keys = grad_keys.at[:, :key_end].add(
            jnp.einsum(
                "chqk,cqhe->ckhe", grad_scores, query_blk, preferred_element_type=jnp.float32
            )
            * score_scale
        )
    return (jnp.concatenate(grad_queries, axis=1), grad_keys, grad_vals)


def gather_rows(values):
    return lax.all_gather(values, "tensor", axis=1, tiled=True)


def scatter_rows(values):
    return lax.psum_scatter(values, "tensor", scatter_dimension=1, tiled=True)


def gather_grads(values):
    return lax.all_gather(values, "tensor", axis=1, tiled=True)


def scatter_grads(values):
    return lax.psum_scatter(
        values.astype(jnp.bfloat16), "tensor", scatter_dimension=1, tiled=True
    ).astype(jnp.float32)


def heads_grads(grad_branch, attended, out_weight):
    grad_out_proj = jnp.einsum(
        "clo,cla->oa", grad_branch, flatten_heads(attended), preferred_element_type=jnp.float32
    )
    grad_attended = split_heads(
        jnp.einsum(
            "clo,oa->cla", grad_branch, out_weight, preferred_element_type=jnp.float32
        ).astype(jnp.bfloat16)
    )
    return (grad_out_proj, grad_attended)


def weight_grad(grad_rows, source_rows):
    return jnp.einsum("cla,cli->ai", grad_rows, source_rows, preferred_element_type=jnp.float32)


def input_grad(grad_rows, weight):
    return jnp.einsum("cla,ai->cli", grad_rows, weight, preferred_element_type=jnp.float32)


def local(
    hidden_in,
    text_states,
    norm1_gain,
    norm1_bias,
    self_query,
    self_key,
    self_value,
    self_out,
    norm2_gain,
    norm2_bias,
    cross_query,
    cross_key,
    cross_value,
    cross_out,
    norm3_gain,
    norm3_bias,
    hidden_up,
    hidden_down,
    cotangent,
):
    full_weights = (
        lax.all_gather(norm1_gain, "dp", axis=0, tiled=True),
        lax.all_gather(norm1_bias, "dp", axis=0, tiled=True),
        lax.all_gather(self_query, "dp", axis=1, tiled=True),
        lax.all_gather(self_key, "dp", axis=1, tiled=True),
        lax.all_gather(self_value, "dp", axis=1, tiled=True),
        lax.all_gather(self_out, "dp", axis=0, tiled=True),
        lax.all_gather(norm2_gain, "dp", axis=0, tiled=True),
        lax.all_gather(norm2_bias, "dp", axis=0, tiled=True),
        lax.all_gather(cross_query, "dp", axis=1, tiled=True),
        lax.all_gather(cross_key, "dp", axis=1, tiled=True),
        lax.all_gather(cross_value, "dp", axis=1, tiled=True),
        lax.all_gather(cross_out, "dp", axis=0, tiled=True),
        lax.all_gather(norm3_gain, "dp", axis=0, tiled=True),
        lax.all_gather(norm3_bias, "dp", axis=0, tiled=True),
        lax.all_gather(hidden_up, "dp", axis=1, tiled=True),
        lax.all_gather(hidden_down, "dp", axis=0, tiled=True),
    )
    gain_self = full_weights[0].astype(jnp.float32)
    bias_self = full_weights[1].astype(jnp.float32)
    gain_cross = full_weights[6].astype(jnp.float32)
    bias_cross = full_weights[7].astype(jnp.float32)
    gain_ffn = full_weights[12].astype(jnp.float32)
    bias_ffn = full_weights[13].astype(jnp.float32)
    stream_one = hidden_in.astype(jnp.float32)
    key_two = split_heads(project(text_states, full_weights[9]).astype(jnp.bfloat16))
    value_two = split_heads(project(text_states, full_weights[10]).astype(jnp.bfloat16))
    normed_one = gather_rows(layer_norm(stream_one, gain_self, bias_self).astype(jnp.bfloat16))
    query_one = split_heads(project(normed_one, full_weights[2]).astype(jnp.bfloat16))
    key_one = split_heads(project(normed_one, full_weights[3]).astype(jnp.bfloat16))
    value_one = split_heads(project(normed_one, full_weights[4]).astype(jnp.bfloat16))
    attended_one, logsum_one = attend(query_one, key_one, value_one, True)
    stream_two = stream_one + scatter_rows(project(flatten_heads(attended_one), full_weights[5]))
    normed_two = gather_rows(layer_norm(stream_two, gain_cross, bias_cross).astype(jnp.bfloat16))
    query_two = split_heads(project(normed_two, full_weights[8]).astype(jnp.bfloat16))
    attended_two, logsum_two = attend(query_two, key_two, value_two, False)
    stream_three = stream_two + scatter_rows(project(flatten_heads(attended_two), full_weights[11]))
    normed_three = gather_rows(layer_norm(stream_three, gain_ffn, bias_ffn).astype(jnp.bfloat16))
    upper = project(normed_three, full_weights[14])
    active = gelu_exact(upper).astype(jnp.bfloat16)
    layer_out = (stream_three + scatter_rows(project(active, full_weights[15]))).astype(
        jnp.bfloat16
    )
    grad_three = cotangent.astype(jnp.float32)
    grad_branch = gather_grads(grad_three.astype(jnp.bfloat16))
    grad_down = jnp.einsum("clo,clf->of", grad_branch, active, preferred_element_type=jnp.float32)
    grad_active = jnp.einsum(
        "clo,of->clf", grad_branch, full_weights[15], preferred_element_type=jnp.float32
    )
    grad_upper = jax.vjp(gelu_exact, upper)[1](grad_active)[0].astype(jnp.bfloat16)
    grad_up = weight_grad(grad_upper, normed_three)
    norm_back = jax.vjp(layer_norm, stream_three, gain_ffn, bias_ffn)[1]
    grad_stream, grad_gain_ffn, grad_bias_ffn = norm_back(
        scatter_grads(input_grad(grad_upper, full_weights[14]))
    )
    grad_two = grad_three + grad_stream
    grad_branch = gather_grads(grad_two.astype(jnp.bfloat16))
    grad_out_cross, grad_attended = heads_grads(grad_branch, attended_two, full_weights[11])
    grad_query, grad_key, grad_value = attend_back(
        query_two, key_two, value_two, grad_attended, logsum_two, False
    )
    grad_query = flatten_heads(grad_query).astype(jnp.bfloat16)
    grad_key = flatten_heads(grad_key).astype(jnp.bfloat16)
    grad_value = flatten_heads(grad_value).astype(jnp.bfloat16)
    grad_query_cross = weight_grad(grad_query, normed_two)
    grad_key_cross = weight_grad(grad_key, text_states)
    grad_value_cross = weight_grad(grad_value, text_states)
    text_part = input_grad(grad_key, full_weights[9]) + input_grad(grad_value, full_weights[10])
    grad_text = lax.psum_scatter(
        text_part.astype(jnp.bfloat16), "tensor", scatter_dimension=2, tiled=True
    ).astype(jnp.float32)
    norm_back = jax.vjp(layer_norm, stream_two, gain_cross, bias_cross)[1]
    grad_stream, grad_gain_cross, grad_bias_cross = norm_back(
        scatter_grads(input_grad(grad_query, full_weights[8]))
    )
    grad_one = grad_two + grad_stream
    grad_branch = gather_grads(grad_one.astype(jnp.bfloat16))
    grad_out_self, grad_attended = heads_grads(grad_branch, attended_one, full_weights[5])
    grad_query, grad_key, grad_value = attend_back(
        query_one, key_one, value_one, grad_attended, logsum_one, True
    )
    grad_query = flatten_heads(grad_query).astype(jnp.bfloat16)
    grad_key = flatten_heads(grad_key).astype(jnp.bfloat16)
    grad_value = flatten_heads(grad_value).astype(jnp.bfloat16)
    grad_query_self = weight_grad(grad_query, normed_one)
    grad_key_self = weight_grad(grad_key, normed_one)
    grad_value_self = weight_grad(grad_value, normed_one)
    grad_normed = (
        input_grad(grad_query, full_weights[2])
        + input_grad(grad_key, full_weights[3])
        + input_grad(grad_value, full_weights[4])
    )
    norm_back = jax.vjp(layer_norm, stream_one, gain_self, bias_self)[1]
    grad_stream, grad_gain_self, grad_bias_self = norm_back(scatter_grads(grad_normed))
    grad_input = grad_one + grad_stream
    summed = (
        lax.psum_scatter(
            grad_gain_self.astype(jnp.bfloat16), "dp", scatter_dimension=0, tiled=True
        ).astype(jnp.float32),
        lax.psum_scatter(
            grad_bias_self.astype(jnp.bfloat16), "dp", scatter_dimension=0, tiled=True
        ).astype(jnp.float32),
        lax.psum_scatter(
            grad_query_self.astype(jnp.bfloat16), "dp", scatter_dimension=1, tiled=True
        ).astype(jnp.float32),
        lax.psum_scatter(
            grad_key_self.astype(jnp.bfloat16), "dp", scatter_dimension=1, tiled=True
        ).astype(jnp.float32),
        lax.psum_scatter(
            grad_value_self.astype(jnp.bfloat16), "dp", scatter_dimension=1, tiled=True
        ).astype(jnp.float32),
        lax.psum_scatter(
            grad_out_self.astype(jnp.bfloat16), "dp", scatter_dimension=0, tiled=True
        ).astype(jnp.float32),
        lax.psum_scatter(
            grad_gain_cross.astype(jnp.bfloat16), "dp", scatter_dimension=0, tiled=True
        ).astype(jnp.float32),
        lax.psum_scatter(
            grad_bias_cross.astype(jnp.bfloat16), "dp", scatter_dimension=0, tiled=True
        ).astype(jnp.float32),
        lax.psum_scatter(
            grad_query_cross.astype(jnp.bfloat16), "dp", scatter_dimension=1, tiled=True
        ).astype(jnp.float32),
        lax.psum_scatter(
            grad_key_cross.astype(jnp.bfloat16), "dp", scatter_dimension=1, tiled=True
        ).astype(jnp.float32),
        lax.psum_scatter(
            grad_value_cross.astype(jnp.bfloat16), "dp", scatter_dimension=1, tiled=True
        ).astype(jnp.float32),
        lax.psum_scatter(
            grad_out_cross.astype(jnp.bfloat16), "dp", scatter_dimension=0, tiled=True
        ).astype(jnp.float32),
        lax.psum_scatter(
            grad_gain_ffn.astype(jnp.bfloat16), "dp", scatter_dimension=0, tiled=True
        ).astype(jnp.float32),
        lax.psum_scatter(
            grad_bias_ffn.astype(jnp.bfloat16), "dp", scatter_dimension=0, tiled=True
        ).astype(jnp.float32),
        lax.psum_scatter(
            grad_up.astype(jnp.bfloat16), "dp", scatter_dimension=1, tiled=True
        ).astype(jnp.float32),
        lax.psum_scatter(
            grad_down.astype(jnp.bfloat16), "dp", scatter_dimension=0, tiled=True
        ).astype(jnp.float32),
    )
    norm_sums = lax.psum(
        (summed[0], summed[1], summed[6], summed[7], summed[12], summed[13]), "tensor"
    )
    return (
        layer_out,
        grad_input,
        grad_text,
        norm_sums[0],
        norm_sums[1],
        summed[2],
        summed[3],
        summed[4],
        summed[5],
        norm_sums[2],
        norm_sums[3],
        summed[8],
        summed[9],
        summed[10],
        summed[11],
        norm_sums[4],
        norm_sums[5],
        summed[14],
        summed[15],
    )


def solution(mesh):
    placed = (
        P("dp", "tensor", None),
        P("dp", None, None),
        P("dp"),
        P("dp"),
        P("tensor", "dp"),
        P("tensor", "dp"),
        P("tensor", "dp"),
        P("dp", "tensor"),
        P("dp"),
        P("dp"),
        P("tensor", "dp"),
        P("tensor", "dp"),
        P("tensor", "dp"),
        P("dp", "tensor"),
        P("dp"),
        P("dp"),
        P("tensor", "dp"),
        P("dp", "tensor"),
        P("dp", "tensor", None),
    )
    return jax.shard_map(
        local,
        mesh=mesh,
        in_specs=placed,
        out_specs=(
            P("dp", "tensor", None),
            P("dp", "tensor", None),
            P("dp", None, "tensor"),
            P("dp"),
            P("dp"),
            P("tensor", "dp"),
            P("tensor", "dp"),
            P("tensor", "dp"),
            P("dp", "tensor"),
            P("dp"),
            P("dp"),
            P("tensor", "dp"),
            P("tensor", "dp"),
            P("tensor", "dp"),
            P("dp", "tensor"),
            P("dp"),
            P("dp"),
            P("tensor", "dp"),
            P("dp", "tensor"),
        ),
        check_vma=False,
    )
```

profile of v0, /device:TPU:0, one launch (start us, length us, event | category | flops | bytes accessed | tf_op | source)
XLA Modules:
  0.0 2638.0 jit_solution(2071661922912122973)
XLA Ops:
  14.5 78.5 %all-reduce.16 = (bf16[1536]{0:T(1024)(128)(2,1)S(1)}, bf16[1536]{0:T(1024)(128)(2,1)S(1)}, bf16[1536]{0:T(1024)(128)(2,1)S(1)}, bf16[1536]{0:T(1024)(128)(2,1)S...) all-reduce(bf16[1536]{0:T(1024)(128)(2,1)S(1)} %dynamic-update-slic, ...), channel_id=1, replica_groups=mesh['dp'=16,'tensor'=2] {'dp'}, use_global_device_ids=true, to_apply=%add.3 | all-reduce | flops 9216 | bytes 36864
  103.6 66.3 %all-gather.23.cloned.1.call-done = bf16[768,1536]{0,1:T(8,128)(2,1)} async-done(((bf16[768,96]{0,1:T(8,128)(2,1)}), bf16[768,1536]{0,1:T(8,128)(2,1)}) %all-gather.23.cloned.1.call-update) | async-done | bytes 2359312 | tf_op jit(solution)/shard_map/all_gather | solution.py:189
  175.1 58.7 %all-gather.21.cloned.1.call-done = bf16[768,1536]{0,1:T(8,128)(2,1)} async-done(((bf16[768,96]{0,1:T(8,128)(2,1)}), bf16[768,1536]{0,1:T(8,128)(2,1)}) %all-gather.21.cloned.1.call-update) | async-done | bytes 2359312 | tf_op jit(solution)/shard_map/all_gather | solution.py:188
  248.4 49.2 %all-gather.19.cloned.1.call-done = bf16[768,1536]{0,1:T(8,128)(2,1)} async-done(((bf16[768,96]{0,1:T(8,128)(2,1)}), bf16[768,1536]{0,1:T(8,128)(2,1)}) %all-gather.19.cloned.1.call-update) | async-done | bytes 2359312 | tf_op jit(solution)/shard_map/all_gather | solution.py:190
  307.3 10.6 fusion.15
  317.9 12.3 fusion
  333.5 8.5 fusion.110
  343.4 17.9 all-gather.25.cloned.1.call-done
  370.0 11.1 reduce-scatter.20.cloned.1.call-done
  388.7 59.1 %all-gather.33.cloned.1.call-done = bf16[768,1536]{0,1:T(8,128)(2,1)} async-done(((bf16[768,96]{0,1:T(8,128)(2,1)}), bf16[768,1536]{0,1:T(8,128)(2,1)}) %all-gather.33.cloned.1.call-update) | async-done | bytes 2359312 | tf_op jit(solution)/shard_map/all_gather | solution.py:195
  451.7 60.4 %all-gather.27.cloned.1.call-done = bf16[768,1536]{0,1:T(8,128)(2,1)} async-done(((bf16[768,96]{0,1:T(8,128)(2,1)}), bf16[768,1536]{0,1:T(8,128)(2,1)}) %all-gather.27.cloned.1.call-update) | async-done | bytes 2359312 | tf_op jit(solution)/shard_map/all_gather | solution.py:196
  516.7 59.7 %all-gather.31.cloned.1.call-done = bf16[768,1536]{0,1:T(8,128)(2,1)} async-done(((bf16[768,96]{0,1:T(8,128)(2,1)}), bf16[768,1536]{0,1:T(8,128)(2,1)}) %all-gather.31.cloned.1.call-update) | async-done | bytes 2359312 | tf_op jit(solution)/shard_map/all_gather | solution.py:194
  576.4 13.0 all-gather.29.cloned.1.call-done
  598.9 57.2 %all-gather.35.cloned.1.call-done = bf16[1536,768]{1,0:T(8,128)(2,1)} async-done(((bf16[96,768]{1,0:T(8,128)(2,1)}), bf16[1536,768]{1,0:T(8,128)(2,1)}) %all-gather.35.cloned.1.call-update) | async-done | bytes 2359312 | tf_op jit(solution)/shard_map/all_gather | solution.py:197
  656.1 7.5 convolution_bitcast_fusion.1
  664.5 12.6 reduce-scatter.22.cloned.1.call-done
  684.8 118.8 %all-gather.39.cloned.1.call-done = bf16[3072,1536]{0,1:T(8,128)(2,1)} async-done(((bf16[3072,96]{0,1:T(8,128)(2,1)}), bf16[3072,1536]{0,1:T(8,128)(2,1)}) %all-gather.39.cloned.1.call-update) | async-done | bytes 9437200 | tf_op jit(solution)/shard_map/all_gather | solution.py:200
  803.6 12.3 all-gather.37.cloned.1.call-done
  815.9 40.5 %multiply_convert_fusion.2 = (bf16[1024,3072]{1,0:T(8,128)(2,1)}, f32[1024,3072]{1,0:T(8,128)}, f32[1024,3072]{1,0:T(8,128)}) fusion(bf16[3072,1536]{0,1:T(8,128)(2,1)} %all-gather.39.cloned.1.call-done, bf16[1,1024,1536]{2,1,0:T(8,128)(2,1)} %all-gather.37.cloned.1.call-done), kind=kOutput, calls=%fused_computation.16 | convolution fusion | flops 9868148736 | bytes 44040192 | tf_op jit(solution)/shard_map/cli,oi->clo/dot_general | solution.py:25
  856.3 100.6 %all-gather.41.cloned.1.call-done = bf16[1536,3072]{1,0:T(8,128)(2,1)} async-done(((bf16[96,3072]{1,0:T(8,128)(2,1)}), bf16[1536,3072]{1,0:T(8,128)(2,1)}) %all-gather.41.cloned.1.call-update) | async-done | bytes 9437200 | tf_op jit(solution)/shard_map/all_gather | solution.py:201
  956.9 24.5 add_convert_fusion
  981.5 15.7 fusion.32
  997.2 15.5 convolution_bitcast_fusion
  1017.7 7.9 reduce-scatter.24.cloned.1.call-done
  1033.4 12.9 all-gather.45.cloned.1.call-done
  1061.8 12.2 reduce-scatter.28.cloned.1.call-done
  1090.2 16.1 fusion.13
  1106.2 12.7 copy.81
  1119.0 15.6 convolution_convert_fusion.1
  1164.8 7.1 fusion.101
  1171.9 12.1 fusion.43
  1189.2 13.7 multiply_reduce_fusion.1
  1202.9 18.6 multiply_reduce_fusion
  1221.6 13.9 multiply_convert_fusion.1
  1242.3 15.9 multiply_convert_fusion
  1258.2 8.9 multiply_convert_fusion.3
  1277.2 7.1 fusion.44
  1308.0 159.0 %reduce-scatter.50.cloned.1.call-done = bf16[3072,96]{0,1:T(8,128)(2,1)} async-done(((bf16[3072,1536]{0,1:T(8,128)(2,1)}), bf16[3072,96]{0,1:T(8,128)(2,1)}) %reduce-scatter.50.cloned.1.call-update) | async-done | bytes 589840 | tf_op jit(solution)/shard_map/reduce_scatter | solution.py:323
  1469.1 130.9 %reduce-scatter.48.cloned.1.call-done = bf16[96,768]{1,0:T(8,128)(2,1)} async-done(((bf16[1536,768]{1,0:T(8,128)(2,1)}), bf16[96,768]{1,0:T(8,128)(2,1)}) %reduce-scatter.48.cloned.1.call-update) | async-done | bytes 147472 | tf_op jit(solution)/shard_map/reduce_scatter | solution.py:314
  1601.7 130.7 %reduce-scatter.42.cloned.1.call-done = bf16[768,96]{0,1:T(8,128)(2,1)} async-done(((bf16[768,1536]{0,1:T(8,128)(2,1)}), bf16[768,96]{0,1:T(8,128)(2,1)}) %reduce-scatter.42.cloned.1.call-update) | async-done | bytes 147472 | tf_op jit(solution)/shard_map/reduce_scatter | solution.py:305
  1734.1 131.5 %reduce-scatter.46.cloned.1.call-done = bf16[768,96]{0,1:T(8,128)(2,1)} async-done(((bf16[768,1536]{0,1:T(8,128)(2,1)}), bf16[768,96]{0,1:T(8,128)(2,1)}) %reduce-scatter.46.cloned.1.call-update) | async-done | bytes 147472 | tf_op jit(solution)/shard_map/reduce_scatter | solution.py:311
  1867.2 130.9 %reduce-scatter.44.cloned.1.call-done = bf16[768,96]{0,1:T(8,128)(2,1)} async-done(((bf16[768,1536]{0,1:T(8,128)(2,1)}), bf16[768,96]{0,1:T(8,128)(2,1)}) %reduce-scatter.44.cloned.1.call-update) | async-done | bytes 147472 | tf_op jit(solution)/shard_map/reduce_scatter | solution.py:308
  2000.0 131.4 %reduce-scatter.40.cloned.1.call-done = bf16[96,768]{1,0:T(8,128)(2,1)} async-done(((bf16[1536,768]{1,0:T(8,128)(2,1)}), bf16[96,768]{1,0:T(8,128)(2,1)}) %reduce-scatter.40.cloned.1.call-update) | async-done | bytes 147472 | tf_op jit(solution)/shard_map/reduce_scatter | solution.py:296
  2133.1 130.7 %reduce-scatter.38.cloned.1.call-done = bf16[768,96]{0,1:T(8,128)(2,1)} async-done(((bf16[768,1536]{0,1:T(8,128)(2,1)}), bf16[768,96]{0,1:T(8,128)(2,1)}) %reduce-scatter.38.cloned.1.call-update) | async-done | bytes 147472 | tf_op jit(solution)/shard_map/reduce_scatter | solution.py:293
  2265.5 131.7 %reduce-scatter.34.cloned.1.call-done = bf16[768,96]{0,1:T(8,128)(2,1)} async-done(((bf16[768,1536]{0,1:T(8,128)(2,1)}), bf16[768,96]{0,1:T(8,128)(2,1)}) %reduce-scatter.34.cloned.1.call-update) | async-done | bytes 147472 | tf_op jit(solution)/shard_map/reduce_scatter | solution.py:287
  2398.8 130.9 %reduce-scatter.36.cloned.1.call-done = bf16[768,96]{0,1:T(8,128)(2,1)} async-done(((bf16[768,1536]{0,1:T(8,128)(2,1)}), bf16[768,96]{0,1:T(8,128)(2,1)}) %reduce-scatter.36.cloned.1.call-update) | async-done | bytes 147472 | tf_op jit(solution)/shard_map/reduce_scatter | solution.py:290
  2531.3 10.6 reduce-scatter.30.cloned.1.call-done
  2546.1 77.0 %all-reduce.15 = (bf16[1536]{0:T(1024)(128)(2,1)S(1)}, bf16[1536]{0:T(1024)(128)(2,1)S(1)}, bf16[1536]{0:T(1024)(128)(2,1)S(1)}, bf16[1536]{0:T(1024)(128)(2,1)S...) all-reduce(bf16[1536]{0:T(1024)(128)(2,1)S(1)} %get-tuple-element.2, ...), channel_id=9, replica_groups=mesh['dp'=16,'tensor'=2] {'dp'}, use_global_device_ids=true, to_apply=%region_32.33.clone | all-reduce | flops 9216 | bytes 36864
  (438 shorter events, 239.5 us)
Async XLA Ops:
  7.2 440.6 %copy-start = (bf16[1,64,1536]{2,1,0:T(8,128)(2,1)S(1)}, bf16[1,64,1536]{2,1,0:T(8,128)(2,1)}, u32[]{:S(2)}) copy-start(bf16[1,64,1536]{2,1,0:T(8,128)(2,1)} %param.48) | copy-start | bytes 589828
  7.2 86.4 %copy-start.8 = (bf16[1,512,1536]{2,1,0:T(8,128)(2,1)S(1)}, bf16[1,512,1536]{2,1,0:T(8,128)(2,1)}, u32[]{:S(2)}) copy-start(bf16[1,512,1536]{2,1,0:T(8,128)(2,1)} %param.47) | copy-start | bytes 4718596
  7.3 96.3 %all-gather.17.cloned.1.call-start = ((), (), s32[]{:S(2)}) async-start(), calls=%async_computation.17 | async-start | bytes 4718592 | tf_op jit(solution)/shard_map/all_gather | solution.py:127
  9.2 86.3 %copy-start.78 = (f32[512]{0:T(512)}, f32[512]{0:T(512)S(1)}, u32[]{:S(2)}) copy-start(f32[512]{0:T(512)S(1)} %broadcast_multiply_fusion.2) | copy-start | bytes 6148
  11.7 86.6 %copy-start.84 = (f32[512]{0:T(512)}, f32[512]{0:T(512)S(1)}, u32[]{:S(2)}) copy-start(f32[512]{0:T(512)S(1)} %fusion.137) | copy-start | bytes 6148
  95.4 74.4 %all-gather.23.cloned.1.call-start = ((), (), s32[]{:S(2)}) async-start(), calls=%async_computation.20 | async-start | bytes 2506752 | tf_op jit(solution)/shard_map/all_gather | solution.py:189
  96.2 137.6 %all-gather.21.cloned.1.call-start = ((), (), s32[]{:S(2)}) async-start(), calls=%async_computation.19 | async-start | bytes 2506752 | tf_op jit(solution)/shard_map/all_gather | solution.py:188
  96.9 200.7 %all-gather.19.cloned.1.call-start = ((), (), s32[]{:S(2)}) async-start(), calls=%async_computation.18 | async-start | bytes 2506752 | tf_op jit(solution)/shard_map/all_gather | solution.py:190
  97.5 263.9 %all-gather.25.cloned.1.call-start = ((), (), s32[]{:S(2)}) async-start(), calls=%async_computation.21 | async-start | bytes 2506752 | tf_op jit(solution)/shard_map/all_gather | solution.py:191
  98.1 283.0 %reduce-scatter.20.cloned.1.call-start = ((), (), s32[]{:S(2)}) async-start(), calls=%async_computation.22 | async-start | bytes 9437184 | tf_op jit(solution)/shard_map/reduce_scatter | solution.py:131
  98.4 204.9 %copy-start.36 = (pred[512,512]{0,1:T(8,128)(4,1)}, pred[512,512]{0,1:T(8,128)(4,1)S(1)}, u32[]{:S(2)}) copy-start(pred[512,512]{0,1:T(8,128)(4,1)S(1)} %iota_compare_fusion.1) | copy-start | bytes 786436
  98.8 231.5 %copy-start.26 = (pred[512,1024]{1,0:T(8,128)(4,1)}, pred[512,1024]{1,0:T(8,128)(4,1)S(1)}, u32[]{:S(2)}) copy-start(pred[512,1024]{1,0:T(8,128)(4,1)S(1)} %iota_compare_fusion) | copy-start | bytes 1572868
  175.1 132.2 %copy-start.21 = (bf16[1024,768]{0,1:T(8,128)(2,1)}, bf16[1024,768]{0,1:T(8,128)(2,1)S(1)}, u32[]{:S(2)}) copy-start(bf16[1024,768]{0,1:T(8,128)(2,1)S(1)} %fusion.83) | copy-start | bytes 4718596
  367.6 80.1 %all-gather.33.cloned.1.call-start = ((), (), s32[]{:S(2)}) async-start(), calls=%async_computation.26 | async-start | bytes 2506752 | tf_op jit(solution)/shard_map/all_gather | solution.py:195
  368.4 143.7 %all-gather.27.cloned.1.call-start = ((), (), s32[]{:S(2)}) async-start(), calls=%async_computation.23 | async-start | bytes 2506752 | tf_op jit(solution)/shard_map/all_gather | solution.py:196
  369.2 207.3 %all-gather.31.cloned.1.call-start = ((), (), s32[]{:S(2)}) async-start(), calls=%async_computation.25 | async-start | bytes 2506752 | tf_op jit(solution)/shard_map/all_gather | solution.py:194
  369.9 219.6 %all-gather.29.cloned.1.call-start = ((), (), s32[]{:S(2)}) async-start(), calls=%async_computation.24 | async-start | bytes 4718592 | tf_op jit(solution)/shard_map/all_gather | solution.py:127
  383.8 293.3 %copy-start.4 = (f32[1,512,1536]{2,1,0:T(8,128)}, f32[1,512,1536]{2,1,0:T(8,128)S(1)}, u32[]{:S(2)}) copy-start(f32[1,512,1536]{2,1,0:T(8,128)S(1)} %get-tuple-element.253) | copy-start | bytes 9437188
  387.5 268.6 %all-gather.35.cloned.1.call-start = ((), (), s32[]{:S(2)}) async-start(), calls=%async_computation.27 | async-start | bytes 2506752 | tf_op jit(solution)/shard_map/all_gather | solution.py:197
  388.3 288.9 %reduce-scatter.22.cloned.1.call-start = ((), (), s32[]{:S(2)}) async-start(), calls=%async_computation.28 | async-start | bytes 9437184 | tf_op jit(solution)/shard_map/reduce_scatter | solution.py:131
  451.7 143.8 %copy-start.41 = (bf16[64,768]{0,1:T(8,128)(2,1)}, bf16[64,768]{0,1:T(8,128)(2,1)S(1)}, u32[]{:S(2)}) copy-start(bf16[64,768]{0,1:T(8,128)(2,1)S(1)} %copy.83) | copy-start | bytes 294916
  663.6 139.9 %all-gather.39.cloned.1.call-start = ((), (), s32[]{:S(2)}) async-start(), calls=%async_computation.30 | async-start | bytes 10027008 | tf_op jit(solution)/shard_map/all_gather | solution.py:200
  664.4 151.5 %all-gather.37.cloned.1.call-start = ((), (), s32[]{:S(2)}) async-start(), calls=%async_computation.29 | async-start | bytes 4718592 | tf_op jit(solution)/shard_map/all_gather | solution.py:127
  683.4 173.0 %all-gather.43.cloned.1.call-start = ((), (), s32[]{:S(2)}) async-start(), calls=%async_computation.33 | async-start | bytes 4718592 | tf_op jit(solution)/shard_map/all_gather | solution.py:135
  684.0 273.0 %all-gather.41.cloned.1.call-start = ((), (), s32[]{:S(2)}) async-start(), calls=%async_computation.31 | async-start | bytes 10027008 | tf_op jit(solution)/shard_map/all_gather | solution.py:201
  684.5 328.3 %reduce-scatter.26.cloned.1.call-start = ((), (), s32[]{:S(2)}) async-start(), calls=%async_computation.34 | async-start | bytes 4718592 | tf_op jit(solution)/shard_map/reduce_scatter | solution.py:139
  997.2 28.5 %reduce-scatter.24.cloned.1.call-start = ((), (), s32[]{:S(2)}) async-start(), calls=%async_computation.32 | async-start | bytes 9437184 | tf_op jit(solution)/shard_map/reduce_scatter | solution.py:131
  1012.8 33.5 %all-gather.45.cloned.1.call-start = ((), (), s32[]{:S(2)}) async-start(), calls=%async_computation.35 | async-start | bytes 4718592 | tf_op jit(solution)/shard_map/all_gather | solution.py:135
  1032.9 41.1 %reduce-scatter.28.cloned.1.call-start = ((), (), s32[]{:S(2)}) async-start(), calls=%async_computation.36 | async-start | bytes 4718592 | tf_op jit(solution)/shard_map/reduce_scatter | solution.py:139
  1061.8 91.0 %all-gather.47.cloned.1.call-start = ((), (), s32[]{:S(2)}) async-start(), calls=%async_computation.37 | async-start | bytes 4718592 | tf_op jit(solution)/shard_map/all_gather | solution.py:135
  1081.5 222.0 %reduce-scatter.32.cloned.1.call-start = ((), (), s32[]{:S(2)}) async-start(), calls=%async_computation.39 | async-start | bytes 294912 | tf_op jit(solution)/shard_map/reduce_scatter | solution.py:253
  1090.0 215.2 %reduce-scatter.52.cloned.1.call-start = ((), (), s32[]{:S(2)}) async-start(), calls=%async_computation.49 | async-start | bytes 10027008
  1119.0 348.0 %reduce-scatter.50.cloned.1.call-start = ((), (), s32[]{:S(2)}) async-start(), calls=%async_computation.48 | async-start | bytes 10027008 | tf_op jit(solution)/shard_map/reduce_scatter | solution.py:323
  1134.7 465.4 %reduce-scatter.48.cloned.1.call-start = ((), (), s32[]{:S(2)}) async-start(), calls=%async_computation.47 | async-start | bytes 2506752 | tf_op jit(solution)/shard_map/reduce_scatter | solution.py:314
  1141.6 590.8 %reduce-scatter.42.cloned.1.call-start = ((), (), s32[]{:S(2)}) async-start(), calls=%async_computation.44 | async-start | bytes 2506752 | tf_op jit(solution)/shard_map/reduce_scatter | solution.py:305
  1147.8 717.7 %reduce-scatter.46.cloned.1.call-start = ((), (), s32[]{:S(2)}) async-start(), calls=%async_computation.46 | async-start | bytes 2506752 | tf_op jit(solution)/shard_map/reduce_scatter | solution.py:311
  1150.2 847.9 %reduce-scatter.44.cloned.1.call-start = ((), (), s32[]{:S(2)}) async-start(), calls=%async_computation.45 | async-start | bytes 2506752 | tf_op jit(solution)/shard_map/reduce_scatter | solution.py:308
  1152.6 978.8 %reduce-scatter.40.cloned.1.call-start = ((), (), s32[]{:S(2)}) async-start(), calls=%async_computation.43 | async-start | bytes 2506752 | tf_op jit(solution)/shard_map/reduce_scatter | solution.py:296
  1158.8 1105.0 %reduce-scatter.38.cloned.1.call-start = ((), (), s32[]{:S(2)}) async-start(), calls=%async_computation.42 | async-start | bytes 2506752 | tf_op jit(solution)/shard_map/reduce_scatter | solution.py:293
  1221.5 1175.6 %reduce-scatter.34.cloned.1.call-start = ((), (), s32[]{:S(2)}) async-start(), calls=%async_computation.40 | async-start | bytes 2506752 | tf_op jit(solution)/shard_map/reduce_scatter | solution.py:287
  1271.9 1257.7 %reduce-scatter.36.cloned.1.call-start = ((), (), s32[]{:S(2)}) async-start(), calls=%async_computation.41 | async-start | bytes 2506752 | tf_op jit(solution)/shard_map/reduce_scatter | solution.py:290
  1289.7 1252.3 %reduce-scatter.30.cloned.1.call-start = ((), (), s32[]{:S(2)}) async-start(), calls=%async_computation.38 | async-start | bytes 4718592 | tf_op jit(solution)/shard_map/reduce_scatter | solution.py:139
  1305.1 694.7 %copy-start.19 = (bf16[1,512,1536]{2,1,0:T(8,128)(2,1)S(1)}, bf16[1,512,1536]{2,1,0:T(8,128)(2,1)}, u32[]{:S(2)}) copy-start(bf16[1,512,1536]{2,1,0:T(8,128)(2,1)} %reduce-scatter.28.cloned.1.call-done) | copy-start | bytes 4718596
  1308.0 1234.0 %copy-start.9 = (bf16[1,512,1536]{2,1,0:T(8,128)(2,1)S(1)}, bf16[1,512,1536]{2,1,0:T(8,128)(2,1)}, u32[]{:S(2)}) copy-start(bf16[1,512,1536]{2,1,0:T(8,128)(2,1)} %param.47) | copy-start | bytes 4718596
  1308.0 1234.0 %copy-start.65 = (f32[1536]{0:T(1024)S(1)}, f32[1536]{0:T(1024)}, u32[]{:S(2)}) copy-start(f32[1536]{0:T(1024)} %copy-done.64) | copy-start | bytes 18436
  1308.0 1234.0 %copy-start.79 = (f32[512]{0:T(512)S(1)}, f32[512]{0:T(512)}, u32[]{:S(2)}) copy-start(f32[512]{0:T(512)} %copy-done.78) | copy-start | bytes 6148
  1999.8 544.5 %copy-start.91 = (f32[512]{0:T(512)S(1)}, f32[512]{0:T(512)}, u32[]{:S(2)}) copy-start(f32[512]{0:T(512)} %copy-done.90) | copy-start | bytes 6148
  1999.8 544.5 %copy-start.85 = (f32[512]{0:T(512)S(1)}, f32[512]{0:T(512)}, u32[]{:S(2)}) copy-start(f32[512]{0:T(512)} %copy-done.84) | copy-start | bytes 6148
  (105 other events, 708.8 us)
Sparse Core Ops, SparseCore 0:
  95.5 7.9 all-gather.16
  106.4 63.4 all-gather.22
  172.7 61.0 all-gather.20
  236.5 61.0 all-gather.18
  300.2 61.0 all-gather.24
  367.8 13.2 reduce-scatter.19
  384.3 63.4 all-gather.32
  451.0 61.0 all-gather.26
  515.3 61.0 all-gather.30
  578.5 10.9 all-gather.28
  592.6 63.4 all-gather.34
  663.8 13.3 reduce-scatter.21
  679.9 123.5 all-gather.38
  805.5 10.3 all-gather.36
  817.3 13.2 all-gather.42
  833.2 123.6 all-gather.40
  997.3 9.0 reduce-scatter.25
  1012.9 12.6 reduce-scatter.23
  1033.0 13.2 all-gather.44
  1061.9 12.0 reduce-scatter.27
  1081.6 13.2 all-gather.46
  1097.8 8.7 reduce-scatter.31
  1119.1 172.2 reduce-scatter.51
  1296.9 170.0 reduce-scatter.49
  1472.6 127.3 reduce-scatter.47
  1604.8 127.5 reduce-scatter.41
  1738.0 127.5 reduce-scatter.45
  1870.5 127.5 reduce-scatter.43
  2003.8 127.6 reduce-scatter.39
  2136.2 127.5 reduce-scatter.37
  2269.5 127.5 reduce-scatter.33
  2402.1 127.5 reduce-scatter.35
  2531.9 10.0 reduce-scatter.29
where the time goes:
time: 2640 us
  waiting for transfers between devices  1960 us (74%)
  matrix products  342 us (13%)
  blocking collectives  158 us (6%)
  other arithmetic  108 us (4%)
  local copies, waits for them, and re-layouts  47.7 us (2%)
    reduce_scatter x1, waiting for transfers between devices, local(): lax.psum_scatter(grad_up.astype(jnp.bfloat16), 'dp', scatter_dimension=1,...  159 us
    unnamed x2, blocking collectives  155 us
    reduce_scatter x1, waiting for transfers between devices, local(): lax.psum_scatter(grad_query_self.astype(jnp.bfloat16), 'dp', scatter_dime...  132 us
    reduce_scatter x1, waiting for transfers between devices, local(): lax.psum_scatter(grad_value_cross.astype(jnp.bfloat16), 'dp', scatter_dim...  131 us
    reduce_scatter x1, waiting for transfers between devices, local(): lax.psum_scatter(grad_out_self.astype(jnp.bfloat16), 'dp', scatter_dimens...  131 us
    reduce_scatter x1, waiting for transfers between devices, local(): lax.psum_scatter(grad_out_cross.astype(jnp.bfloat16), 'dp', scatter_dimen...  131 us
    reduce_scatter x1, waiting for transfers between devices, local(): lax.psum_scatter(grad_key_self.astype(jnp.bfloat16), 'dp', scatter_dimens...  131 us
    reduce_scatter x1, waiting for transfers between devices, local(): lax.psum_scatter(grad_key_cross.astype(jnp.bfloat16), 'dp', scatter_dimen...  131 us
  transfers between devices with their start and end apart: 33, of which 28 were waited for; matrix products, arithmetic and copies ran while one was open for 14% of the time, Pallas kernels for 0%

commit v1 on v0

--- a/solution.py
+++ b/solution.py
@@ -1,6 +1,10 @@
+import functools
+
 import jax
 import jax.numpy as jnp
 from jax import lax
+from jax.experimental import pallas as pl
+from jax.experimental.pallas import tpu as pltpu
 from jax.sharding import PartitionSpec as P
 
 HEAD_DIM = 64
@@ -161,7 +165,7 @@
     return jnp.einsum("cla,ai->cli", grad_rows, weight, preferred_element_type=jnp.float32)
 
 
-def local(
+def local_generic(
     hidden_in,
     text_states,
     norm1_gain,
@@ -353,6 +357,689 @@
     )
 
 
+MESH_IDS = pl.DeviceIdType.MESH
+BF16 = jnp.bfloat16
+F32 = jnp.float32
+VMEM_LIMIT = 60 * 2**20
+
+
+def my_place():
+    chip = lax.axis_index("dp")
+    core = lax.axis_index("tensor")
+    return (lax.rem(chip, 2), lax.rem(lax.div(chip, 2), 2), lax.div(chip, 4), core)
+
+
+def neighbours(x, y, z, core):
+    def device(zz, yy, xx):
+        return (zz * 4 + yy * 2 + xx, core)
+
+    return (device(z, y, 1 - x), device(z, 1 - y, x), device(z + 1, y, x), device(z - 1, y, x))
+
+
+def when(cond, fn):
+    if cond is None:
+        fn()
+    else:
+        pl.when(cond)(fn)
+
+
+def signal_neighbours(sems, near, has_up, has_down):
+    for sem, device, cond in zip(sems, near, (None, None, has_up, has_down), strict=True):
+        when(
+            cond,
+            functools.partial(
+                pl.semaphore_signal, sem, inc=1, device_id=device, device_id_type=MESH_IDS
+            ),
+        )
+
+
+def gather_kernel(count, chunks, *refs):
+    shards, outs = refs[:count], refs[count : 2 * count]
+    local_sem, send_sem, zs, xs, ys, ds = refs[2 * count :]
+    x, y, z, core = my_place()
+    xn, yn = 1 - x, 1 - y
+    near = neighbours(x, y, z, core)
+    right, across, up, down = near
+    has_up, has_down = z < 3, z > 0
+    barrier = pltpu.get_barrier_semaphore()
+    signal_neighbours([barrier] * 4, near, has_up, has_down)
+    pl.semaphore_wait(barrier, 2 + has_up.astype(jnp.int32) + has_down.astype(jnp.int32))
+    total = len(chunks)
+    pending = []
+
+    half_rows = shards[0].shape[0] // 2
+
+    def span(c):
+        _, first, width, _ = chunks[c]
+        return pl.ds(first, width)
+
+    def at(zz, yy, xx, c, half=None):
+        lines = slice(None) if half is None else pl.ds(half * half_rows, half_rows)
+        return outs[chunks[c][0]].at[zz, yy, xx, lines, span(c)]
+
+    def plane(zz, c):
+        return outs[chunks[c][0]].at[zz, :, :, :, span(c)]
+
+    def own(c):
+        return shards[chunks[c][0]].at[:, span(c)]
+
+    local = [pltpu.make_async_copy(own(c), at(z, y, x, c), local_sem.at[c]) for c in range(total)]
+
+    def remote(src, dst, sem, device):
+        return pltpu.make_async_remote_copy(
+            src_ref=src,
+            dst_ref=dst,
+            send_sem=send_sem,
+            recv_sem=sem,
+            device_id=device,
+            device_id_type=MESH_IDS,
+        )
+
+    def send(src, dst, sem, device, cond=None):
+        copy = remote(src, dst, sem, device)
+        when(cond, copy.start)
+        pending.append((cond, copy))
+
+    def wait(ref, sem, cond=None):
+        when(cond, remote(ref, ref, sem, right).wait_recv)
+
+    def lines(step):
+        for sign, device, more in ((-1, up, has_up), (1, down, has_down)):
+            block = z + sign * step
+            yield block, (block >= 0) if sign < 0 else (block <= 3), device, more
+
+    def stage_z(c, step):
+        if step == 0:
+            send(own(c), at(z, y, x, c), zs.at[c, z], up, has_up)
+            send(own(c), at(z, y, x, c), zs.at[c, z], down, has_down)
+            send(own(c), at(z, y, x, c), xs.at[c, z], right)
+            send(own(c), at(z, y, x, c), ys.at[c, z], across)
+            local[c].start()
+        if 1 <= step <= 3:
+            for block, exists, device, more in lines(step):
+                ref = at(block, y, x, c)
+                wait(ref, zs.at[c, block], exists)
+                if step < 3:
+                    send(ref, ref, zs.at[c, block], device, exists & more)
+                send(ref, ref, xs.at[c, block], right, exists)
+                send(ref, ref, ys.at[c, block], across, exists)
+        if 1 <= step <= 4:
+            for block, exists, _, _ in [(z, None, None, None)] if step == 1 else lines(step - 1):
+                wait(at(block, y, xn, c), xs.at[c, block], exists)
+                ref = at(block, y, xn, c, 0)
+                send(ref, ref, ds.at[c, block, 0], across, exists)
+                wait(at(block, yn, x, c), ys.at[c, block], exists)
+                ref = at(block, yn, x, c, 1)
+                send(ref, ref, ds.at[c, block, 1], right, exists)
+        if step == 5:
+            for block in range(4):
+                for half in range(2):
+                    wait(at(block, yn, xn, c, half), ds.at[c, block, half])
+            local[c].wait()
+
+    def stage_a(c, step):
+        if step == 0:
+            send(own(c), at(z, y, x, c), xs.at[c, z], right)
+            send(own(c), at(z, y, x, c), ys.at[c, z], across)
+            local[c].start()
+        if step == 1:
+            wait(at(z, y, xn, c), xs.at[c, z])
+            ref = at(z, y, xn, c, 0)
+            send(ref, ref, ds.at[c, z, 0], across)
+            wait(at(z, yn, x, c), ys.at[c, z])
+            ref = at(z, yn, x, c, 1)
+            send(ref, ref, ds.at[c, z, 1], right)
+        if step == 2:
+            for half in range(2):
+                wait(at(z, yn, xn, c, half), ds.at[c, z, half])
+            local[c].wait()
+            send(plane(z, c), plane(z, c), zs.at[c, z], up, has_up)
+            send(plane(z, c), plane(z, c), zs.at[c, z], down, has_down)
+        if step >= 3:
+            for block, exists, device, more in lines(step - 2):
+                wait(plane(block, c), zs.at[c, block], exists)
+                if step < 5:
+                    send(plane(block, c), plane(block, c), zs.at[c, block], device, exists & more)
+
+    stages = 6
+    for turn in range(total + stages - 1):
+        for step in range(stages):
+            c = turn - step
+            if 0 <= c < total:
+                (stage_z if chunks[c][3] == "Z" else stage_a)(c, step)
+    for cond, copy in pending:
+        when(cond, copy.wait_send)
+
+
+def gather_all(shards, chunks):
+    total, count = len(chunks), len(shards)
+    dma = pltpu.SemaphoreType.DMA
+    return pl.pallas_call(
+        functools.partial(gather_kernel, count, chunks),
+        out_shape=[jax.ShapeDtypeStruct((4, 2, 2) + s.shape, s.dtype) for s in shards],
+        in_specs=[pl.BlockSpec(memory_space=pl.ANY)] * count,
+        out_specs=[pl.BlockSpec(memory_space=pl.ANY)] * count,
+        scratch_shapes=[
+            dma((total,)),
+            dma,
+            dma((total, 4)),
+            dma((total, 4)),
+            dma((total, 4)),
+            dma((total, 4, 2)),
+        ],
+        compiler_params=pltpu.CompilerParams(collective_id=0, has_side_effects=True),
+        name="gather_weights",
+    )(*shards)
+
+
+def total_of(*parts):
+    value = parts[0].astype(F32)
+    for part in parts[1:]:
+        value = value + part.astype(F32)
+    return value
+
+
+XD, YD, XA, YA, XB, YB, UP, DOWN = range(8)
+
+
+def scatter_kernel(places, width_z, width_a, slots, *refs):
+    count = 1 + max(place[0] for place in places)
+    grads, out = refs[:count], refs[count]
+    gz, ga, xdz, ydz, xaz, yaz, xbz, ybz, upz, dnz = refs[count + 1 : count + 11]
+    xda, yda, xaa, yaa, xba, yba, upa, dna, oz, oa = refs[count + 11 : count + 21]
+    load_sem, out_sem, send_z, send_a, recv_z, recv_a, credit = refs[count + 21 :]
+    total, width = len(places), width_z + width_a
+    x, y, z, core = my_place()
+    xn, yn = 1 - x, 1 - y
+    near = neighbours(x, y, z, core)
+    right, across, up, down = near
+    has_up, has_down = z < 3, z > 0
+    degree = 2 + has_up.astype(jnp.int32) + has_down.astype(jnp.int32)
+    barrier = pltpu.get_barrier_semaphore()
+    signal_neighbours([barrier] * 4, near, has_up, has_down)
+    pl.semaphore_wait(barrier, degree)
+    rows = gz.shape[4]
+    low, high = pl.ds(0, rows // 2), pl.ds(rows // 2, rows // 2)
+
+    def remote(src, dst, send_sem, recv_sem, device):
+        return pltpu.make_async_remote_copy(
+            src_ref=src,
+            dst_ref=dst,
+            send_sem=send_sem,
+            recv_sem=recv_sem,
+            device_id=device,
+            device_id_type=MESH_IDS,
+        )
+
+    def arrived(ref, sem):
+        remote(ref, ref, send_z.at[0], sem, right).wait_recv()
+
+    def sent(ref, sem):
+        remote(ref, ref, sem, recv_z.at[0, 0], right).wait_send()
+
+    def load_copies(array, first, k):
+        grad = grads[array]
+        return (
+            pltpu.make_async_copy(
+                grad.at[:, :, :, :, pl.ds(first, width_z)], gz.at[k], load_sem.at[k, 0]
+            ),
+            pltpu.make_async_copy(
+                grad.at[:, :, :, :, pl.ds(first + width_z, width_a)], ga.at[k], load_sem.at[k, 1]
+            ),
+        )
+
+    def out_copies(c):
+        o = lax.rem(c, 2)
+        first = pl.multiple_of(c * width, 128)
+        return (
+            pltpu.make_async_copy(oz.at[o], out.at[:, pl.ds(first, width_z)], out_sem.at[o, 0]),
+            pltpu.make_async_copy(
+                oa.at[o], out.at[:, pl.ds(first + width_z, width_a)], out_sem.at[o, 1]
+            ),
+        )
+
+    def plane_first(own, k, bufs, send_sem, recv):
+        xd, yd, xa, ya = bufs
+        remote(own(yn, xn, low), xd.at[k], send_sem.at[k], recv.at[k, XD], right).start()
+        remote(own(yn, xn, high), yd.at[k], send_sem.at[k], recv.at[k, YD], across).start()
+        remote(own(y, xn, low), xa.at[k], send_sem.at[k], recv.at[k, XA], right).start()
+        remote(own(yn, x, high), ya.at[k], send_sem.at[k], recv.at[k, YA], across).start()
+
+    def plane_second(add, k, bufs, send_sem, recv):
+        xd, yd, xb, yb = bufs
+        arrived(xd.at[k], recv.at[k, XD])
+        add(xd, yn, x, low)
+        remote(xd.at[k], yb.at[k], send_sem.at[k], recv.at[k, YB], across).start()
+        arrived(yd.at[k], recv.at[k, YD])
+        add(yd, y, xn, high)
+        remote(yd.at[k], xb.at[k], send_sem.at[k], recv.at[k, XB], right).start()
+
+    def line_up(first, buf, add, k, send_sem, recv):
+        blocks = 4 - first
+        arrived(buf.at[k, pl.ds(first, blocks)], recv.at[k, UP])
+        if blocks > 1:
+            for block in range(first + 1, 4):
+                add(buf, block)
+            ref = buf.at[k, pl.ds(first + 1, blocks - 1)]
+            remote(ref, ref, send_sem.at[k], recv.at[k, UP], up).start()
+
+    def line_down(last, buf, add, k, send_sem, recv):
+        arrived(buf.at[k, pl.ds(0, last + 1)], recv.at[k, DOWN])
+        if last > 0:
+            for block in range(last):
+                add(buf, block)
+            ref = buf.at[k, pl.ds(0, last)]
+            remote(ref, ref, send_sem.at[k], recv.at[k, DOWN], down).start()
+
+    def add_a(k):
+        def add(buf, block):
+            for yy in range(2):
+                for xx in range(2):
+                    buf[k, block, yy, xx] = total_of(
+                        buf[k, block, yy, xx], ga[k, block, yy, xx]
+                    ).astype(BF16)
+
+        return add
+
+    def add_z(k):
+        def add(buf, block):
+            buf[k, block] = total_of(buf[k, block], gz[k, block, y, x]).astype(BF16)
+
+        return add
+
+    def start_load(c, k):
+        for index, (array, first) in enumerate(places):
+
+            @pl.when(c == index)
+            def _():
+                for copy in load_copies(array, first, k):
+                    copy.start()
+
+    def begin(c, k):
+        for copy in load_copies(0, 0, k):
+            copy.wait()
+
+        @pl.when(c >= slots)
+        def _():
+            pl.semaphore_wait(credit.at[0], 1)
+            pl.semaphore_wait(credit.at[1], 1)
+            pl.when(has_up)(lambda: pl.semaphore_wait(credit.at[2], 1))
+            pl.when(has_down)(lambda: pl.semaphore_wait(credit.at[3], 1))
+
+        plane_first(
+            lambda yy, xx, half: gz.at[k, :, yy, xx, half, :], k, (xdz, ydz, xaz, yaz), send_z, recv_z
+        )
+
+        @pl.when(z == 0)
+        def _():
+            ref = pl.ds(1, 3)
+            remote(ga.at[k, ref], upa.at[k, ref], send_a.at[k], recv_a.at[k, UP], up).start()
+
+        @pl.when(z == 3)
+        def _():
+            ref = pl.ds(0, 3)
+            remote(ga.at[k, ref], dna.at[k, ref], send_a.at[k], recv_a.at[k, DOWN], down).start()
+
+    def second(c, k):
+        def add(buf, yy, xx, half):
+            for block in range(4):
+                buf[k, block] = total_of(buf[k, block], gz[k, block, yy, xx, half, :]).astype(BF16)
+
+        plane_second(add, k, (xdz, ydz, xbz, ybz), send_z, recv_z)
+        pl.when(z == 1)(lambda: line_up(1, upa, add_a(k), k, send_a, recv_a))
+        pl.when(z == 2)(lambda: line_down(2, dna, add_a(k), k, send_a, recv_a))
+
+    def third(c, k):
+        for buf, kind in ((xaz, XA), (yaz, YA), (xbz, XB), (ybz, YB)):
+            arrived(buf.at[k], recv_z.at[k, kind])
+        for block in range(4):
+            for half, one, two in ((low, xaz, ybz), (high, yaz, xbz)):
+                gz[k, block, y, x, half, :] = total_of(
+                    gz[k, block, y, x, half, :], one[k, block], two[k, block]
+                ).astype(BF16)
+
+        @pl.when(z == 0)
+        def _():
+            ref = pl.ds(1, 3)
+            remote(
+                gz.at[k, ref, y, x], upz.at[k, ref], send_z.at[k], recv_z.at[k, UP], up
+            ).start()
+
+        @pl.when(z == 3)
+        def _():
+            ref = pl.ds(0, 3)
+            remote(
+                gz.at[k, ref, y, x], dnz.at[k, ref], send_z.at[k], recv_z.at[k, DOWN], down
+            ).start()
+
+        pl.when(z == 2)(lambda: line_up(2, upa, add_a(k), k, send_a, recv_a))
+        pl.when(z == 1)(lambda: line_down(1, dna, add_a(k), k, send_a, recv_a))
+
+    def fourth(c, k):
+        pl.when(z == 1)(lambda: line_up(1, upz, add_z(k), k, send_z, recv_z))
+        pl.when(z == 2)(lambda: line_down(2, dnz, add_z(k), k, send_z, recv_z))
+        pl.when(z == 3)(lambda: line_up(3, upa, None, k, send_a, recv_a))
+        pl.when(z == 0)(lambda: line_down(0, dna, None, k, send_a, recv_a))
+        for buf, exists in ((upa, has_down), (dna, has_up)):
+
+            @pl.when(exists)
+            def _():
+                for yy in range(2):
+                    for xx in range(2):
+                        ga[k, z, yy, xx] = total_of(ga[k, z, yy, xx], buf[k, z, yy, xx]).astype(BF16)
+
+        plane_first(
+            lambda yy, xx, half: ga.at[k, z, yy, xx, half, :], k, (xda, yda, xaa, yaa), send_a, recv_a
+        )
+
+    def fifth(c, k):
+        pl.when(z == 2)(lambda: line_up(2, upz, add_z(k), k, send_z, recv_z))
+        pl.when(z == 1)(lambda: line_down(1, dnz, add_z(k), k, send_z, recv_z))
+
+        def add(buf, yy, xx, half):
+            buf[k] = total_of(buf[k], ga[k, z, yy, xx, half, :]).astype(BF16)
+
+        plane_second(add, k, (xda, yda, xba, yba), send_a, recv_a)
+
+    def finish(c, k):
+        pl.when(z == 3)(lambda: line_up(3, upz, None, k, send_z, recv_z))
+        pl.when(z == 0)(lambda: line_down(0, dnz, None, k, send_z, recv_z))
+        o = lax.rem(c, 2)
+
+        @pl.when(c >= 2)
+        def _():
+            for copy in out_copies(c - 2):
+                copy.wait()
+
+        oz[o] = gz[k, z, y, x].astype(F32)
+        for buf, exists in ((upz, has_down), (dnz, has_up)):
+
+            @pl.when(exists)
+            def _():
+                oz[o] = oz[o] + buf[k, z].astype(F32)
+
+        for buf, kind in ((xaa, XA), (yaa, YA), (xba, XB), (yba, YB)):
+            arrived(buf.at[k], recv_a.at[k, kind])
+        oa[o, low, :] = total_of(ga[k, z, y, x, low, :], xaa[k], yba[k])
+        oa[o, high, :] = total_of(ga[k, z, y, x, high, :], yaa[k], xba[k])
+        for copy in out_copies(c):
+            copy.start()
+        for buf in (xdz, ydz, xaz, yaz, xbz, ybz):
+            sent(buf.at[k], send_z.at[k])
+        for buf in (xda, yda, xaa, yaa, xba, yba):
+            sent(buf.at[k], send_a.at[k])
+        for step in range(3):
+
+            @pl.when(z == step)
+            def _():
+                sent(upz.at[k, pl.ds(step + 1, 3 - step)], send_z.at[k])
+                sent(upa.at[k, pl.ds(step + 1, 3 - step)], send_a.at[k])
+
+            @pl.when(z == 3 - step)
+            def _():
+                sent(dnz.at[k, pl.ds(0, 3 - step)], send_z.at[k])
+                sent(dna.at[k, pl.ds(0, 3 - step)], send_a.at[k])
+
+        @pl.when(c < total - slots)
+        def _():
+            signal_neighbours([credit.at[i] for i in (0, 1, 3, 2)], near, has_up, has_down)
+
+    stages = (start_load, begin, second, third, fourth, fifth, finish)
+
+    def body(turn, carry):
+        for step, stage in enumerate(stages):
+            c = turn - step
+
+            @pl.when((c >= 0) & (c < total))
+            def _():
+                stage(c, lax.rem(c, slots))
+
+        return carry
+
+    lax.fori_loop(0, total + len(stages) - 1, body, 0)
+    for c in (total - 2, total - 1):
+        for copy in out_copies(jnp.int32(c)):
+            copy.wait()
+
+
+def scatter_all(grads, places, width_z, width_a, slots):
+    rows = grads[0].shape[3]
+    columns = len(places) * (width_z + width_a)
+    dma = pltpu.SemaphoreType.DMA
+
+    def buffer(*shape, dtype=BF16):
+        return pltpu.VMEM((slots,) + shape, dtype)
+
+    return pl.pallas_call(
+        functools.partial(scatter_kernel, places, width_z, width_a, slots),
+        out_shape=jax.ShapeDtypeStruct((rows, columns), F32),
+        in_specs=[pl.BlockSpec(memory_space=pl.ANY)] * len(grads),
+        out_specs=pl.BlockSpec(memory_space=pl.ANY),
+        scratch_shapes=[
+            buffer(4, 2, 2, rows, width_z),
+            buffer(4, 2, 2, rows, width_a),
+            *[buffer(4, rows // 2, width_z)] * 6,
+            *[buffer(4, rows, width_z)] * 2,
+            *[buffer(rows // 2, width_a)] * 6,
+            *[buffer(4, 2, 2, rows, width_a)] * 2,
+            pltpu.VMEM((2, rows, width_z), F32),
+            pltpu.VMEM((2, rows, width_a), F32),
+            dma((slots, 2)),
+            dma((2, 2)),
+            dma((slots,)),
+            dma((slots,)),
+            dma((slots, 8)),
+            dma((slots, 8)),
+            pltpu.SemaphoreType.REGULAR((4,)),
+        ],
+        compiler_params=pltpu.CompilerParams(
+            collective_id=1, has_side_effects=True, vmem_limit_bytes=VMEM_LIMIT
+        ),
+        name="scatter_gradients",
+    )(*grads)
+
+
+def sum_cores(values):
+    return values + lax.ppermute(values, "tensor", [(0, 1), (1, 0)])
+
+
+def weight_grad_t(source_rows, grad_rows):
+    return jnp.einsum(
+        "cli,cla->ia", source_rows, grad_rows, preferred_element_type=jnp.float32
+    ).astype(BF16)
+
+
+def project_t(row_data, weight):
+    return jnp.einsum("cli,io->clo", row_data, weight, preferred_element_type=jnp.float32)
+
+
+def input_grad_t(grad_rows, weight):
+    return jnp.einsum("cla,ia->cli", grad_rows, weight, preferred_element_type=jnp.float32)
+
+
+def gather_plan(columns):
+    chunks, since = [], 0
+    for array, width in enumerate(columns):
+        size = 768 if width % 768 == 0 else width
+        for first in range(0, width, size):
+            since += 1
+            family = "A" if since % 5 == 3 and size == 768 else "Z"
+            chunks.append((array, first, size, family))
+    return tuple(chunks)
+
+
+def scatter_plan(columns, width):
+    return tuple((array, first) for array, all_of in enumerate(columns) for first in range(0, all_of, width))
+
+
+def local_fast(
+    hidden_in,
+    text_states,
+    norm1_gain,
+    norm1_bias,
+    self_query,
+    self_key,
+    self_value,
+    self_out,
+    norm2_gain,
+    norm2_bias,
+    cross_query,
+    cross_key,
+    cross_value,
+    cross_out,
+    norm3_gain,
+    norm3_bias,
+    hidden_up,
+    hidden_down,
+    cotangent,
+):
+    width = norm1_gain.shape[0] * 16
+    norms = jnp.stack([norm1_gain, norm1_bias, norm2_gain, norm2_bias, norm3_gain, norm3_bias], axis=1)
+    norms = jnp.pad(norms, ((0, 0), (0, 122)))
+    shards = (
+        norms,
+        self_query.T,
+        self_key.T,
+        self_value.T,
+        self_out,
+        cross_query.T,
+        cross_key.T,
+        cross_value.T,
+        cross_out,
+        hidden_up.T,
+        hidden_down,
+    )
+    gathered = gather_all(shards, gather_plan([s.shape[1] for s in shards]))
+    gathered = [g.reshape(width, g.shape[-1]) for g in gathered]
+    norms = gathered[0][:, :6].T.astype(jnp.float32)
+    gain_self, bias_self, gain_cross, bias_cross, gain_ffn, bias_ffn = [norms[i] for i in range(6)]
+    w_q, w_k, w_v, w_o, w_cq, w_ck, w_cv, w_co, w_up, w_down = gathered[1:]
+    stream_one = hidden_in.astype(jnp.float32)
+    key_two = split_heads(project_t(text_states, w_ck).astype(jnp.bfloat16))
+    value_two = split_heads(project_t(text_states, w_cv).astype(jnp.bfloat16))
+    normed_one = gather_rows(layer_norm(stream_one, gain_self, bias_self).astype(jnp.bfloat16))
+    query_one = split_heads(project_t(normed_one, w_q).astype(jnp.bfloat16))
+    key_one = split_heads(project_t(normed_one, w_k).astype(jnp.bfloat16))
+    value_one = split_heads(project_t(normed_one, w_v).astype(jnp.bfloat16))
+    attended_one, logsum_one = attend(query_one, key_one, value_one, True)
+    stream_two = stream_one + scatter_rows(project(flatten_heads(attended_one), w_o))
+    normed_two = gather_rows(layer_norm(stream_two, gain_cross, bias_cross).astype(jnp.bfloat16))
+    query_two = split_heads(project_t(normed_two, w_cq).astype(jnp.bfloat16))
+    attended_two, logsum_two = attend(query_two, key_two, value_two, False)
+    stream_three = stream_two + scatter_rows(project(flatten_heads(attended_two), w_co))
+    normed_three = gather_rows(layer_norm(stream_three, gain_ffn, bias_ffn).astype(jnp.bfloat16))
+    upper = project_t(normed_three, w_up)
+    active = gelu_exact(upper).astype(jnp.bfloat16)
+    layer_out = (stream_three + scatter_rows(project(active, w_down))).astype(jnp.bfloat16)
+    grad_three = cotangent.astype(jnp.float32)
+    grad_branch = gather_grads(grad_three.astype(jnp.bfloat16))
+    grad_down = weight_grad_t(grad_branch, active)
+    grad_active = jnp.einsum("clo,of->clf", grad_branch, w_down, preferred_element_type=jnp.float32)
+    grad_upper = jax.vjp(gelu_exact, upper)[1](grad_active)[0].astype(jnp.bfloat16)
+    grad_up = weight_grad_t(normed_three, grad_upper)
+    norm_back = jax.vjp(layer_norm, stream_three, gain_ffn, bias_ffn)[1]
+    grad_stream, grad_gain_ffn, grad_bias_ffn = norm_back(
+        scatter_grads(input_grad_t(grad_upper, w_up))
+    )
+    grad_two = grad_three + grad_stream
+    grad_branch = gather_grads(grad_two.astype(jnp.bfloat16))
+    grad_out_cross, grad_attended = heads_grads(grad_branch, attended_two, w_co)
+    grad_query, grad_key, grad_value = attend_back(
+        query_two, key_two, value_two, grad_attended, logsum_two, False
+    )
+    grad_query = flatten_heads(grad_query).astype(jnp.bfloat16)
+    grad_key = flatten_heads(grad_key).astype(jnp.bfloat16)
+    grad_value = flatten_heads(grad_value).astype(jnp.bfloat16)
+    grad_query_cross = weight_grad_t(normed_two, grad_query)
+    grad_key_cross = weight_grad_t(text_states, grad_key)
+    grad_value_cross = weight_grad_t(text_states, grad_value)
+    text_part = input_grad_t(grad_key, w_ck) + input_grad_t(grad_value, w_cv)
+    grad_text = lax.psum_scatter(
+        text_part.astype(jnp.bfloat16), "tensor", scatter_dimension=2, tiled=True
+    ).astype(jnp.float32)
+    norm_back = jax.vjp(layer_norm, stream_two, gain_cross, bias_cross)[1]
+    grad_stream, grad_gain_cross, grad_bias_cross = norm_back(
+        scatter_grads(input_grad_t(grad_query, w_cq))
+    )
+    grad_one = grad_two + grad_stream
+    grad_branch = gather_grads(grad_one.astype(jnp.bfloat16))
+    grad_out_self, grad_attended = heads_grads(grad_branch, attended_one, w_o)
+    grad_query, grad_key, grad_value = attend_back(
+        query_one, key_one, value_one, grad_attended, logsum_one, True
+    )
+    grad_query = flatten_heads(grad_query).astype(jnp.bfloat16)
+    grad_key = flatten_heads(grad_key).astype(jnp.bfloat16)
+    grad_value = flatten_heads(grad_value).astype(jnp.bfloat16)
+    grad_query_self = weight_grad_t(normed_one, grad_query)
+    grad_key_self = weight_grad_t(normed_one, grad_key)
+    grad_value_self = weight_grad_t(normed_one, grad_value)
+    grad_normed = (
+        input_grad_t(grad_query, w_q) + input_grad_t(grad_key, w_k) + input_grad_t(grad_value, w_v)
+    )
+    norm_back = jax.vjp(layer_norm, stream_one, gain_self, bias_self)[1]
+    grad_stream, grad_gain_self, grad_bias_self = norm_back(scatter_grads(grad_normed))
+    grad_input = grad_one + grad_stream
+    norm_grads = jnp.stack(
+        [
+            grad_gain_self,
+            grad_bias_self,
+            grad_gain_cross,
+            grad_bias_cross,
+            grad_gain_ffn,
+            grad_bias_ffn,
+        ],
+        axis=1,
+    )
+    norm_grads = jnp.pad(norm_grads, ((0, 0), (0, 122)))
+    norm_sums = sum_cores(lax.psum_scatter(norm_grads, "dp", scatter_dimension=0, tiled=True)).T
+    grads = (
+        grad_down,
+        grad_up,
+        grad_out_cross.astype(BF16),
+        grad_query_cross,
+        grad_key_cross,
+        grad_value_cross,
+        grad_out_self.astype(BF16),
+        grad_query_self,
+        grad_key_self,
+        grad_value_self,
+    )
+    columns = [g.shape[1] for g in grads]
+    summed = scatter_all(
+        [g.reshape(4, 2, 2, width // 16, g.shape[1]) for g in grads],
+        scatter_plan(columns, 768),
+        640,
+        128,
+        8,
+    )
+    pieces, first = [], 0
+    for count in columns:
+        pieces.append(summed[:, first : first + count])
+        first += count
+    down, up, out_cross, query_cross, key_cross, value_cross, out_self, query, key, value = pieces
+    return (
+        layer_out,
+        grad_input,
+        grad_text,
+        norm_sums[0],
+        norm_sums[1],
+        query.T,
+        key.T,
+        value.T,
+        out_self,
+        norm_sums[2],
+        norm_sums[3],
+        query_cross.T,
+        key_cross.T,
+        value_cross.T,
+        out_cross,
+        norm_sums[4],
+        norm_sums[5],
+        up.T,
+        down,
+    )
+
+
 def solution(mesh):
     placed = (
         P("dp", "tensor", None),
@@ -375,8 +1062,9 @@
         P("dp", "tensor"),
         P("dp", "tensor", None),
     )
+    fast = dict(mesh.shape) == {"dp": 16, "tensor": 2}
     return jax.shard_map(
-        local,
+        local_fast if fast else local_generic,
         mesh=mesh,
         in_specs=placed,
         out_specs=(

time: 2640 us -> 1130 us (0.43)
  waiting for transfers between devices: 1960 us -> 100 us
  Pallas kernels: 0 us -> 572 us
  blocking collectives: 158 us -> 0 us
  matrix products: 342 us -> 315 us
    reduce_scatter x10 -> x1, waiting for transfers between devices: 1210 us -> 0.01 us  [local_fast(): lax.psum_scatter(text_part.astype(jnp.bfloat16), 'tensor', scatter_dimens...]
    all_gather x10 -> x0, waiting for transfers between devices: 648 us -> none  [the longest x1 119 us: local(): lax.all_gather(hidden_up, 'dp', axis=1, tiled=True)]
    pallas_call x0 -> x2, Pallas kernels: none -> 572 us  [the longest x1 297 us: scatter_all(): pl.pallas_call(functools.partial(scatter_kernel, places, width_z, width_a...]
    unnamed x2 -> x0, blocking collectives: 155 us -> none
    dot_general x10 -> x3, matrix products: 96.9 us -> 24.9 us  [project(): jnp.einsum('cli,oi->clo', row_data, weight, preferred_element_type=jnp.fl...]
    dot_general x16 -> x23, matrix products: 111 us -> 177 us  [the longest x7 66.9 us: project_t(): jnp.einsum('cli,io->clo', row_data, weight, preferred_element_type=jnp.fl...]
  transfers between devices with their start and end apart: 33 -> 15, of which waited for: 28 -> 9; matrix products, arithmetic and copies ran while one was open for 14% -> 23% of each run, Pallas kernels for 0% -> 26%
where the time goes in v1:
time: 1130 us
  Pallas kernels  572 us (51%)
  matrix products  315 us (28%)
  waiting for transfers between devices  100 us (9%)
  other arithmetic  83.7 us (7%)
  local copies, waits for them, and re-layouts  38.4 us (3%)
  between operations  15.9 us (1%)
    pallas_call x1, Pallas kernels, scatter_all(): pl.pallas_call(functools.partial(scatter_kernel, places, width_z, width_a...  297 us
    pallas_call x1, Pallas kernels, gather_all(): pl.pallas_call(functools.partial(gather_kernel, count, chunks), out_shape...  274 us
    dot_general x7, matrix products, project_t(): jnp.einsum('cli,io->clo', row_data, weight, preferred_element_type=jnp.fl...  66.9 us
    dot_general x8, matrix products, weight_grad_t(): jnp.einsum('cli,cla->ia', source_rows, grad_rows, preferred_element_type=...  53.4 us
    reduce_scatter x3, waiting for transfers between devices, scatter_rows(): return lax.psum_scatter(values, 'tensor', scatter_dimension=1, tiled=True)  42.5 us
    dot_general x7, matrix products, input_grad_t(): jnp.einsum('cla,ia->cli', grad_rows, weight, preferred_element_type=jnp.f...  31.7 us
    all_gather x3, waiting for transfers between devices, gather_rows(): return lax.all_gather(values, 'tensor', axis=1, tiled=True)  27.4 us
    dot_general x4, matrix products, attend_back(): jnp.einsum('cqhe,ckhe->chqk', grad_blk, val_rows[:, :key_end], preferred_...  25.6 us
  transfers between devices with their start and end apart: 15, of which 9 were waited for; matrix products, arithmetic and copies ran while one was open for 23% of the time, Pallas kernels for 26%

profile of v1, /device:TPU:0, one launch (start us, length us, event | category | flops | bytes accessed | tf_op | source)
XLA Modules:
  0.0 1127.4 jit_solution(7970885870763634759)
XLA Ops:
  12.4 274.5 %gather_weights.1 = (bf16[4,2,2,96,128]{4,3,2,1,0:T(8,128)(2,1)}, bf16[4,2,2,96,768]{4,3,2,1,0:T(8,128)(2,1)}, bf16[4,2,2,96,768]{4,3,2,1,0:T(8,128)(2,1)}, bf16...) custom-call(bf16[96,128]{1,0:T(8,128)(2,1)} %pad.32.refs_0_, ...), custom_call_target="tpu_custom_call" | custom-call | tf_op jit(solution)/shard_map/gather_weights/pallas_call | solution.py:517
  291.6 10.5 all-gather.7.cloned.1.call-done
  302.2 5.4 fusion.88
  315.1 7.2 fusion.82
  322.4 3.5 fusion.110
  326.0 10.8 fusion.21
  336.7 12.3 %fusion = f32[12,512]{1,0:T(8,128)S(1)} fusion(f32[12,512]{1,0:T(8,128)S(1)} %get-tuple-element.229, f32[12,512,1024]{2,1,0:T(8,128)} %get-tuple-element.230, pred[512,1024]{1,0:T(8,128)(4,1)S(1)} %iota_compare_fusion), kind=kLoop, calls=%fused_computation.6 | loop fusion | flops 25159680 | bytes 25739264 | tf_op jit(solution)/shard_map/reduce_sum | solution.py:72
  352.1 7.8 fusion.109
  362.2 4.7 convolution_bitcast_fusion.2
  367.0 15.8 %reduce-scatter.11.cloned.1.call-done = f32[1,512,1536]{2,1,0:T(8,128)} async-done(((f32[1,1024,1536]{2,1,0:T(8,128)}), f32[1,512,1536]{2,1,0:T(8,128)}) %reduce-scatter.11.cloned.1.call-update) | async-done | bytes 3145744 | tf_op jit(solution)/shard_map/reduce_scatter | solution.py:135
  396.7 4.5 all-gather.9.cloned.1.call-done
  401.2 5.3 fusion.91
  411.1 4.7 convolution_bitcast_fusion.1
  415.9 15.8 %reduce-scatter.13.cloned.1.call-done = f32[1,512,1536]{2,1,0:T(8,128)} async-done(((f32[1,1024,1536]{2,1,0:T(8,128)}), f32[1,512,1536]{2,1,0:T(8,128)}) %reduce-scatter.13.cloned.1.call-update) | async-done | bytes 3145744 | tf_op jit(solution)/shard_map/reduce_scatter | solution.py:135
  438.7 12.4 %all-gather.11.cloned.1.call-done = bf16[1,1024,1536]{2,1,0:T(8,128)(2,1)} async-done(((bf16[1,512,1536]{2,1,0:T(8,128)(2,1)}), bf16[1,1024,1536]{2,1,0:T(8,128)(2,1)}) %all-gather.11.cloned.1.call-update) | async-done | bytes 3145744 | tf_op jit(solution)/shard_map/all_gather | solution.py:131
  451.1 40.5 %multiply_convert_fusion.2 = (bf16[1024,3072]{1,0:T(8,128)(2,1)}, f32[1024,3072]{1,0:T(8,128)}, f32[1024,3072]{1,0:T(8,128)}) fusion(bf16[1536,3072]{1,0:T(8,128)(2,1)} %bitcast.439, bf16[1,1024,1536]{2,1,0:T(8,128)(2,1)} %all-gather.11.cloned.1.call-done), kind=kOutput, calls=%fused_computation.24 | convolution fusion | flops 9868148736 | bytes 44040192 | tf_op jit(solution)/shard_map/cli,io->clo/dot_general | solution.py:853
  491.6 24.5 %fusion.10 = bf16[1024,3072]{1,0:T(8,128)(2,1)} fusion(f32[1024,3072]{1,0:T(8,128)} %get-tuple-element.207, f32[1024,3072]{1,0:T(8,128)} %get-tuple-element.237, bf16[1536,3072]{1,0:T(8,128)(2,1)} %bitcast.437, bf16[1,1024,1536]{2,1,0:T(8,128)(2,1)} %all-gather.13.cloned.1.call-done), kind=kOutput, calls=%fused_computation.18 | convolution fusion | flops 9707716608 | bytes 44040192 | tf_op jit(solution)/shard_map/clo,of->clf/dot_general | solution.py:937
  516.1 15.7 %fusion.38 = bf16[1,1024,1536]{2,1,0:T(8,128)(2,1)} fusion(bf16[1024,3072]{1,0:T(8,128)(2,1)} %fusion.10, bf16[1536,3072]{1,0:T(8,128)(2,1)} %bitcast.440), kind=kOutput, calls=%fused_computation.91 | convolution fusion | flops 9665249280 | bytes 18874368 | tf_op jit(solution)/shard_map/cla,ia->cli/dot_general | solution.py:857
  531.9 15.6 %convolution_bitcast_fusion = f32[1,1024,1536]{2,1,0:T(8,128)} fusion(bf16[1024,3072]{1,0:T(8,128)(2,1)} %get-tuple-element.206, bf16[1536,3072]{1,0:T(8,128)(2,1)} %bitcast.438), kind=kOutput, calls=%fused_computation.71 | convolution fusion | flops 9663676416 | bytes 22020096 | tf_op jit(solution)/shard_map/cli,oi->clo/dot_general | solution.py:29
  552.4 10.9 reduce-scatter.15.cloned.1.call-done
  563.3 3.9 fusion.156
  570.9 13.1 %all-gather.15.cloned.1.call-done = bf16[1,1024,1536]{2,1,0:T(8,128)(2,1)} async-done(((bf16[1,512,1536]{2,1,0:T(8,128)(2,1)}), bf16[1,1024,1536]{2,1,0:T(8,128)(2,1)}) %all-gather.15.cloned.1.call-update) | async-done | bytes 3145744 | tf_op jit(solution)/shard_map/all_gather | solution.py:139
  583.9 5.3 fusion.94
  595.1 4.0 fusion.37
  599.2 12.2 %reduce-scatter.19.cloned.1.call-done = bf16[1,512,1536]{2,1,0:T(8,128)(2,1)} async-done(((bf16[1,1024,1536]{2,1,0:T(8,128)(2,1)}), bf16[1,512,1536]{2,1,0:T(8,128)(2,1)}) %reduce-scatter.19.cloned.1.call-update) | async-done | bytes 1572880 | tf_op jit(solution)/shard_map/reduce_scatter | solution.py:143
  628.8 4.4 all-gather.17.cloned.1.call-done
  633.2 4.7 fusion.97
  637.9 8.0 fusion.100
  646.0 6.9 multiply_reduce_fusion.1
  652.8 7.1 multiply_convert_fusion.1
  662.0 3.2 multiply_bitcast_fusion
  665.2 17.7 %multiply_reduce_fusion = (f32[12,512]{1,0:T(8,128)S(1)}, f32[12,512,1024]{2,1,0:T(8,128)}) fusion(f32[12,512]{1,0:T(8,128)S(1)} %log_add_fusion, f32[12,512,1024]{2,1,0:T(8,128)} %get-tuple-element.230, pred[512,1024]{1,0:T(8,128)(4,1)S(1)} %copy-done.25, bf16[1024,12,64]{0,2,1:T(8,128)(2,1)S(1)} %bitcast.394, bf16[1,1024,12,64]{1,3,2,0:T(8,128)(2,1)} %bitcast.411), kind=kOutput, calls=%fused_computation.1 | convolution fusion | flops 836757504 | bytes 53264384 | tf_op jit(solution)/shard_map/cqhe,ckhe->chqk/dot_general | solution.py:99
  682.9 13.7 %fusion.49 = bf16[1,1024,12,64]{1,3,2,0:T(8,128)(2,1)} fusion(f32[1,512,12,64]{1,3,2,0:T(8,128)} %fusion.100, f32[12,512]{1,0:T(8,128)S(1)} %log_add_fusion, f32[12,512,1024]{2,1,0:T(8,128)} %get-tuple-element.230, pred[512,1024]{1,0:T(8,128)(4,1)S(1)} %copy-done.25, bf16[1,1024,12,64]{1,3,2,0:T(8,128)(2,1)} %bitcast.412), kind=kOutput, calls=%fused_computation.103 | convolution fusion | flops 832045056 | bytes 29646848 | tf_op jit(solution)/shard_map/chqk,cqhe->ckhe/dot_general | solution.py:103
  696.6 16.8 %multiply_convert_fusion = bf16[12,512,1024]{2,1,0:T(8,128)(2,1)S(1)} fusion(f32[12,512,1024]{2,1,0:T(8,128)} %get-tuple-element.243, f32[12,512]{1,0:T(8,128)S(1)} %get-tuple-element.242, f32[12,512]{1,0:T(8,128)S(1)} %log_add_fusion, f32[12,512,1024]{2,1,0:T(8,128)} %get-tuple-element.230, pred[512,1024]{1,0:T(8,128)(4,1)S(1)} %copy-done.26), kind=kLoop, calls=%fused_computation | loop fusion | flops 37748736 | bytes 63488000 | tf_op jit(solution)/shard_map/convert_element_type | solution.py:111
  713.4 6.2 multiply_convert_fusion.3
  719.6 4.1 fusion.50
  729.2 4.3 fusion.39
  733.6 16.1 %convolution_convert_fusion.1 = bf16[3072,1536]{0,1:T(8,128)(2,1)} fusion(bf16[1024,3072]{1,0:T(8,128)(2,1)} %get-tuple-element.206, bf16[1,1024,1536]{2,1,0:T(8,128)(2,1)} %all-gather.13.cloned.1.call-done), kind=kOutput, calls=%fused_computation.43 | convolution fusion | flops 9668395008 | bytes 18874368 | tf_op jit(solution)/shard_map/cli,cla->ia/dot_general | solution.py:847
  749.7 15.1 %convolution_convert_fusion = bf16[1536,3072]{1,0:T(8,128)(2,1)} fusion(bf16[1024,3072]{1,0:T(8,128)(2,1)} %fusion.10, bf16[1,1024,1536]{2,1,0:T(8,128)(2,1)S(1)} %copy-done.112), kind=kOutput, calls=%fused_computation.42 | convolution fusion | flops 9668395008 | bytes 18874368 | tf_op jit(solution)/shard_map/cli,cla->ia/dot_general | solution.py:847
  771.8 6.3 convolution_convert_fusion.8
  778.1 4.0 convolution_convert_fusion.9
  783.8 6.1 convolution_convert_fusion.7
  789.9 3.9 convolution_convert_fusion.4
  793.8 4.1 convolution_convert_fusion.5
  805.5 6.4 convolution_convert_fusion.6
  811.9 297.1 %scatter_gradients.1 = f32[96,12288]{1,0:T(8,128)} custom-call(bf16[4,2,2,96,3072]{4,3,2,1,0:T(8,128)(2,1)} %bitcast.371, bf16[4,2,2,96,3072]{4,3,2,1,0:T(8,128)(2,1)} %bitcast.372, bf16[4,2,2,96,768]{4,3,2,1,0:T(8,128)(2,1)} %bitcast.400, bf16[4,2,2,96,768]{4,3,2,1,0:T(8,128)(2,1)} %bitcast.399, bf16[4,2,2,96,768]{4,3,2,1,0:T(8,128)(2,1)} %bitcast.374, ...), custom_call_target="tpu_custom_call" | custom-call | tf_op jit(solution)/shard_map/scatter_gradients/pallas_call | solution.py:813
  1109.1 3.2 fusion.161
  1115.5 4.6 add_add_fusion.3
  (379 shorter events, 106.7 us)
Async XLA Ops:
  7.2 380.8 %copy-start = (bf16[1,64,1536]{2,1,0:T(8,128)(2,1)S(1)}, bf16[1,64,1536]{2,1,0:T(8,128)(2,1)}, u32[]{:S(2)}) copy-start(bf16[1,64,1536]{2,1,0:T(8,128)(2,1)} %param.48) | copy-start | bytes 589828
  7.2 281.6 %copy-start.7 = (bf16[1,512,1536]{2,1,0:T(8,128)(2,1)S(1)}, bf16[1,512,1536]{2,1,0:T(8,128)(2,1)}, u32[]{:S(2)}) copy-start(bf16[1,512,1536]{2,1,0:T(8,128)(2,1)} %param.47) | copy-start | bytes 4718596
  7.3 294.9 %all-gather.7.cloned.1.call-start = ((), (), s32[]{:S(2)}) async-start(), calls=%async_computation.8 | async-start | bytes 4718592 | tf_op jit(solution)/shard_map/all_gather | solution.py:131
  9.1 281.5 %copy-start.82 = (f32[512]{0:T(512)}, f32[512]{0:T(512)S(1)}, u32[]{:S(2)}) copy-start(f32[512]{0:T(512)S(1)} %broadcast_multiply_fusion.2) | copy-start | bytes 6148
  11.1 279.5 %copy-start.90 = (f32[512]{0:T(512)}, f32[512]{0:T(512)S(1)}, u32[]{:S(2)}) copy-start(f32[512]{0:T(512)S(1)} %fusion.139) | copy-start | bytes 6148
  288.2 97.8 %copy-start.71 = (f32[1536]{0:T(1024)}, f32[1536]{0:T(1024)S(1)}, u32[]{:S(2)}) copy-start(f32[1536]{0:T(1024)S(1)} %get-tuple-element.199) | copy-start | bytes 18436
  288.2 147.1 %copy-start.73 = (f32[1536]{0:T(1024)}, f32[1536]{0:T(1024)S(1)}, u32[]{:S(2)}) copy-start(f32[1536]{0:T(1024)S(1)} %get-tuple-element.196) | copy-start | bytes 18436
  290.6 92.1 %reduce-scatter.11.cloned.1.call-start = ((), (), s32[]{:S(2)}) async-start(), calls=%async_computation.9 | async-start | bytes 9437184 | tf_op jit(solution)/shard_map/reduce_scatter | solution.py:135
  291.2 31.1 %copy-start.35 = (pred[512,512]{0,1:T(8,128)(4,1)}, pred[512,512]{0,1:T(8,128)(4,1)S(1)}, u32[]{:S(2)}) copy-start(pred[512,512]{0,1:T(8,128)(4,1)S(1)} %iota_compare_fusion.1) | copy-start | bytes 786436
  291.6 57.4 %copy-start.24 = (pred[512,1024]{1,0:T(8,128)(4,1)}, pred[512,1024]{1,0:T(8,128)(4,1)S(1)}, u32[]{:S(2)}) copy-start(pred[512,1024]{1,0:T(8,128)(4,1)S(1)} %iota_compare_fusion) | copy-start | bytes 1572868
  307.6 18.3 %copy-start.18 = (bf16[1024,768]{0,1:T(8,128)(2,1)}, bf16[1024,768]{0,1:T(8,128)(2,1)S(1)}, u32[]{:S(2)}) copy-start(bf16[1024,768]{0,1:T(8,128)(2,1)S(1)} %fusion.88) | copy-start | bytes 4718596
  312.5 9.8 copy-start.2
  312.5 9.8 copy-start.61
  325.9 23.1 %copy-start.43 = (bf16[1024,768]{0,1:T(8,128)(2,1)S(1)}, bf16[1024,768]{0,1:T(8,128)(2,1)}, u32[]{:S(2)}) copy-start(bf16[1024,768]{0,1:T(8,128)(2,1)} %copy-done.42) | copy-start | bytes 4718596
  336.7 12.4 %copy-start.63 = (f32[12,512]{1,0:T(8,128)}, f32[12,512]{1,0:T(8,128)S(1)}, u32[]{:S(2)}) copy-start(f32[12,512]{1,0:T(8,128)S(1)} %get-tuple-element.229) | copy-start | bytes 73732
  336.7 15.4 %copy-start.1 = (f32[12,512,1024]{2,1,0:T(8,128)S(1)}, f32[12,512,1024]{2,1,0:T(8,128)}, u32[]{:S(2)}) copy-start(f32[12,512,1024]{2,1,0:T(8,128)} %get-tuple-element.230) | copy-start | bytes 75497472
  349.0 10.9 copy-start.77
  366.9 34.3 %all-gather.9.cloned.1.call-start = ((), (), s32[]{:S(2)}) async-start(), calls=%async_computation.10 | async-start | bytes 4718592 | tf_op jit(solution)/shard_map/all_gather | solution.py:131
  385.5 46.2 %copy-start.3 = (f32[1,512,1536]{2,1,0:T(8,128)}, f32[1,512,1536]{2,1,0:T(8,128)S(1)}, u32[]{:S(2)}) copy-start(f32[1,512,1536]{2,1,0:T(8,128)S(1)} %get-tuple-element.211) | copy-start | bytes 9437188
  387.8 43.9 %reduce-scatter.13.cloned.1.call-start = ((), (), s32[]{:S(2)}) async-start(), calls=%async_computation.11 | async-start | bytes 9437184 | tf_op jit(solution)/shard_map/reduce_scatter | solution.py:135
  391.9 15.0 %copy-start.40 = (bf16[64,768]{0,1:T(8,128)(2,1)}, bf16[64,768]{0,1:T(8,128)(2,1)S(1)}, u32[]{:S(2)}) copy-start(bf16[64,768]{0,1:T(8,128)(2,1)S(1)} %copy.107) | copy-start | bytes 294916
  415.8 35.3 %all-gather.11.cloned.1.call-start = ((), (), s32[]{:S(2)}) async-start(), calls=%async_computation.12 | async-start | bytes 4718592 | tf_op jit(solution)/shard_map/all_gather | solution.py:131
  437.7 54.0 %all-gather.13.cloned.1.call-start = ((), (), s32[]{:S(2)}) async-start(), calls=%async_computation.14 | async-start | bytes 4718592 | tf_op jit(solution)/shard_map/all_gather | solution.py:139
  438.2 109.3 %reduce-scatter.17.cloned.1.call-start = ((), (), s32[]{:S(2)}) async-start(), calls=%async_computation.15 | async-start | bytes 4718592 | tf_op jit(solution)/shard_map/reduce_scatter | solution.py:143
  531.8 31.5 %reduce-scatter.15.cloned.1.call-start = ((), (), s32[]{:S(2)}) async-start(), calls=%async_computation.13 | async-start | bytes 9437184 | tf_op jit(solution)/shard_map/reduce_scatter | solution.py:135
  547.5 36.5 %all-gather.15.cloned.1.call-start = ((), (), s32[]{:S(2)}) async-start(), calls=%async_computation.16 | async-start | bytes 4718592 | tf_op jit(solution)/shard_map/all_gather | solution.py:139
  570.5 40.9 %reduce-scatter.19.cloned.1.call-start = ((), (), s32[]{:S(2)}) async-start(), calls=%async_computation.17 | async-start | bytes 4718592 | tf_op jit(solution)/shard_map/reduce_scatter | solution.py:143
  570.9 18.4 %copy-start.10 = (f32[12,512,64]{1,2,0:T(8,128)S(1)}, f32[12,512,64]{1,2,0:T(8,128)}, u32[]{:S(2)}) copy-start(f32[12,512,64]{1,2,0:T(8,128)} %copy-done.9) | copy-start | bytes 4718596
  570.9 18.4 %copy-start.51 = (bf16[64,12,64]{2,1,0:T(8,128)(2,1)S(1)}, bf16[64,12,64]{2,1,0:T(8,128)(2,1)}, u32[]{:S(2)}) copy-start(bf16[64,12,64]{2,1,0:T(8,128)(2,1)} %reshape.1238) | copy-start | bytes 294916
  595.1 16.3 %copy-start.72 = (f32[1536]{0:T(1024)S(1)}, f32[1536]{0:T(1024)}, u32[]{:S(2)}) copy-start(f32[1536]{0:T(1024)} %copy-done.71) | copy-start | bytes 18436
  599.1 12.3 %copy-start.4 = (f32[1,512,1536]{2,1,0:T(8,128)S(1)}, f32[1,512,1536]{2,1,0:T(8,128)}, u32[]{:S(2)}) copy-start(f32[1,512,1536]{2,1,0:T(8,128)} %copy-done.3) | copy-start | bytes 9437188
  599.1 12.3 %copy-start.85 = (f32[512]{0:T(512)S(1)}, f32[512]{0:T(512)}, u32[]{:S(2)}) copy-start(f32[512]{0:T(512)} %copy-done.84) | copy-start | bytes 6148
  599.2 15.2 %copy-start.101 = (f32[512]{0:T(512)S(1)}, f32[512]{0:T(512)}, u32[]{:S(2)}) copy-start(f32[512]{0:T(512)} %copy-done.100) | copy-start | bytes 6148
  599.2 15.2 %copy-start.93 = (f32[512]{0:T(512)S(1)}, f32[512]{0:T(512)}, u32[]{:S(2)}) copy-start(f32[512]{0:T(512)} %copy-done.92) | copy-start | bytes 6148
  599.2 34.0 %all-gather.17.cloned.1.call-start = ((), (), s32[]{:S(2)}) async-start(), calls=%async_computation.18 | async-start | bytes 4718592 | tf_op jit(solution)/shard_map/all_gather | solution.py:139
  619.8 162.4 %reduce-scatter.23.cloned.1.call-start = ((), (), s32[]{:S(2)}) async-start(), calls=%async_computation.20 | async-start | bytes 294912 | tf_op jit(solution)/shard_map/reduce_scatter | solution.py:957
  628.2 9.7 copy-start.36
  628.3 169.8 %reduce-scatter.21.cloned.1.call-start = ((), (), s32[]{:S(2)}) async-start(), calls=%async_computation.19 | async-start | bytes 4718592 | tf_op jit(solution)/shard_map/reduce_scatter | solution.py:143
  633.2 12.7 %slice-start = ((s8[12582912]{0:T(1024)(128)(4,1)}), s8[4194304]{0:T(1024)(128)(4,1)S(1)}, s32[]{:S(2)}) async-start(s8[12582912]{0:T(1024)(128)(4,1)} %bitcast.361), calls=%async_computation.22 | async-start | bytes 8388608
  633.2 12.7 %slice-start.1 = ((s8[12582912]{0:T(1024)(128)(4,1)}), s8[4194304]{0:T(1024)(128)(4,1)S(1)}, s32[]{:S(2)}) async-start(s8[12582912]{0:T(1024)(128)(4,1)} %bitcast.361), calls=%async_computation.23 | async-start | bytes 8388608
  637.9 8.0 copy-start.52
  682.9 13.7 %copy-start.26 = (pred[512,1024]{1,0:T(8,128)(4,1)S(1)}, pred[512,1024]{1,0:T(8,128)(4,1)}, u32[]{:S(2)}) copy-start(pred[512,1024]{1,0:T(8,128)(4,1)} %copy-done.24) | copy-start | bytes 1572868
  733.5 381.0 %reduce-scatter.25.cloned.1.call-start = ((), (), s32[]{:S(2)}) async-start(), calls=%async_computation.21 | async-start | bytes 835584
  733.6 16.1 %copy-start.112 = (bf16[1,1024,1536]{2,1,0:T(8,128)(2,1)S(1)}, bf16[1,1024,1536]{2,1,0:T(8,128)(2,1)}, u32[]{:S(2)}) copy-start(bf16[1,1024,1536]{2,1,0:T(8,128)(2,1)} %all-gather.11.cloned.1.call-done) | copy-start | bytes 9437188
  749.6 15.1 %copy-start.95 = (f32[1536]{0:T(1024)S(1)}, f32[1536]{0:T(1024)}, u32[]{:S(2)}) copy-start(f32[1536]{0:T(1024)} %get-tuple-element.187) | copy-start | bytes 18436
  749.6 15.1 %copy-start.94 = (f32[1536]{0:T(1024)S(1)}, f32[1536]{0:T(1024)}, u32[]{:S(2)}) copy-start(f32[1536]{0:T(1024)} %get-tuple-element.191) | copy-start | bytes 18436
  749.6 15.2 %copy-start.49 = (bf16[12,64,64]{2,1,0:T(8,128)(2,1)S(1)}, bf16[12,64,64]{2,1,0:T(8,128)(2,1)}, u32[]{:S(2)}) copy-start(bf16[12,64,64]{2,1,0:T(8,128)(2,1)} %copy-done.48) | copy-start | bytes 294916
  1115.4 4.7 collective-permute-start
  (94 other events, 286.0 us)
Sparse Core Ops, SparseCore 0:
  290.7 11.3 all-gather.6
  367.0 15.6 reduce-scatter.10
  387.9 13.2 all-gather.8
  415.9 15.6 reduce-scatter.12
  437.8 13.2 all-gather.10
  452.5 13.2 all-gather.12
  531.9 12.0 reduce-scatter.16
  547.6 15.6 reduce-scatter.14
  570.6 13.2 all-gather.14
  599.3 12.0 reduce-scatter.18
  619.9 13.2 all-gather.16
  635.9 8.7 reduce-scatter.22
  733.6 12.0 reduce-scatter.20
  805.6 125.9 reduce-scatter.24

commit v2 on v1

--- a/solution.py
+++ b/solution.py
@@ -542,13 +542,85 @@
 XD, YD, XA, YA, XB, YB, UP, DOWN = range(8)
 
 
-def scatter_kernel(places, width_z, width_a, slots, *refs):
-    count = 1 + max(place[0] for place in places)
-    grads, out = refs[:count], refs[count]
-    gz, ga, xdz, ydz, xaz, yaz, xbz, ybz, upz, dnz = refs[count + 1 : count + 11]
-    xda, yda, xaa, yaa, xba, yba, upa, dna, oz, oa = refs[count + 11 : count + 21]
-    load_sem, out_sem, send_z, send_a, recv_z, recv_a, credit = refs[count + 21 :]
-    total, width = len(places), width_z + width_a
+UNIT = 256
+WIDTH_Z, WIDTH_A, SLOTS = 384, 128, 8
+ROWS_L = 6
+FIRST_L = (0, 12, 24, 27, 36, 39)
+FIRST_R = ((0, 12), (12, 24), (24, 27), (27, 30), (36, 39))
+TEXT_UNITS = (30, 36)
+SELF_UNITS = (39, 48)
+UNITS = 48
+
+
+def dot_nt(left, right):
+    return lax.dot_general(left, right, (((1,), (1,)), ((), ())), preferred_element_type=F32)
+
+
+def dot_tn(left, right):
+    return lax.dot_general(left, right, (((0,), (0,)), ((), ())), preferred_element_type=F32)
+
+
+def dot_nn(left, right):
+    return jnp.dot(left, right, preferred_element_type=F32)
+
+
+def head_back(head, q_ref, k_ref, v_ref, do_ref, lse_ref, dqkv, acc_k, acc_v):
+    width = q_ref.shape[1]
+    pair, half = lax.div(head, 2), lax.rem(head, 2)
+    lanes = [pl.ds(pl.multiple_of(pair * 128 + n * width, 128), 128) for n in range(3)]
+    cols = lanes[0]
+    mine = lax.div(lax.broadcasted_iota(jnp.int32, (1, 128), 1), 64) == half
+    acc_k[...] = jnp.zeros_like(acc_k)
+    acc_v[...] = jnp.zeros_like(acc_v)
+    block = 256
+    keep = lax.broadcasted_iota(jnp.int32, (block, block), 0) <= lax.broadcasted_iota(
+        jnp.int32, (block, block), 1
+    )
+
+    def merged(rows, lane, value):
+        before = jnp.where(half == 0, 0.0, dqkv[rows, lane].astype(F32))
+        dqkv[rows, lane] = (before + value).astype(BF16)
+
+    for i in range(q_ref.shape[0] // block):
+        rows = pl.ds(i * block, block)
+        q = jnp.where(mine, q_ref[rows, cols].astype(F32), 0.0).astype(BF16)
+        do = jnp.where(mine, do_ref[rows, cols].astype(F32), 0.0).astype(BF16)
+        lse = lse_ref[pl.ds(head, 1), rows]
+        parts = [(i * block, block, True)]
+        if i:
+            parts.insert(0, (0, i * block, False))
+        held, inner = [], 0.0
+        for first, count, diagonal in parts:
+            keys = pl.ds(first, count)
+            soft = jnp.exp(dot_nt(k_ref[keys, cols], q) * score_scale - lse)
+            if diagonal:
+                soft = jnp.where(keep, soft, 0.0)
+            slope = dot_nt(v_ref[keys, cols], do)
+            inner = inner + jnp.sum(soft * slope, axis=0, keepdims=True)
+            held.append((keys, soft, slope))
+        grad_q = 0.0
+        for keys, soft, slope in held:
+            ds = (soft * (slope - inner)).astype(BF16)
+            acc_v[keys, :] += dot_nn(soft.astype(BF16), do)
+            acc_k[keys, :] += dot_nn(ds, q)
+            grad_q = grad_q + dot_tn(ds, k_ref[keys, cols])
+        merged(rows, lanes[0], jnp.where(mine, grad_q * score_scale, 0.0))
+    merged(slice(None), lanes[1], acc_k[...] * score_scale)
+    merged(slice(None), lanes[2], acc_v[...])
+
+
+def backward_kernel(*refs):
+    lefts, refs = refs[:ROWS_L], refs[ROWS_L:]
+    rights, refs = refs[:5], refs[5:]
+    text_h, dkv_h, q_h, k_h, v_h, do_h, lse_ref, out, dqkv_h = refs[:9]
+    refs = refs[9:]
+    gz, ga, xdz, ydz, xaz, yaz, xbz, ybz, upz, dnz = refs[:10]
+    xda, yda, xaa, yaa, xba, yba, upa, dna, oz, oa = refs[10:20]
+    lbuf, rbuf, text_v, dkv_v, q_v, k_v, v_v, do_v, dqkv, acc_k, acc_v = refs[20:31]
+    first_sem, l_sem, r_sem, dqkv_sem, out_sem, send_z, send_a, recv_z, recv_a, credit = refs[31:]
+    width_z, width_a, slots = WIDTH_Z, WIDTH_A, SLOTS
+    total, width = UNITS // 2, WIDTH_Z + WIDTH_A
+    heads = q_v.shape[1] // HEAD_DIM
     x, y, z, core = my_place()
     xn, yn = 1 - x, 1 - y
     near = neighbours(x, y, z, core)
@@ -577,16 +649,76 @@
     def sent(ref, sem):
         remote(ref, ref, sem, recv_z.at[0, 0], right).wait_send()
 
-    def load_copies(array, first, k):
-        grad = grads[array]
-        return (
-            pltpu.make_async_copy(
-                grad.at[:, :, :, :, pl.ds(first, width_z)], gz.at[k], load_sem.at[k, 0]
-            ),
-            pltpu.make_async_copy(
-                grad.at[:, :, :, :, pl.ds(first + width_z, width_a)], ga.at[k], load_sem.at[k, 1]
-            ),
+    firsts = [
+        pltpu.make_async_copy(src, dst, first_sem.at[n])
+        for n, (src, dst) in enumerate(
+            (
+                (text_h, text_v),
+                (dkv_h, dkv_v),
+                (q_h, q_v),
+                (k_h, k_v),
+                (v_h, v_v),
+                (do_h, do_v),
+            )
         )
+    ]
+
+    def left_copy(n):
+        return pltpu.make_async_copy(lefts[n], lbuf.at[n % 2], l_sem.at[n % 2])
+
+    def right_copies(c, which):
+        unit = 2 * c + which
+        place, sem = rbuf.at[lax.rem(c, 2), which], r_sem.at[lax.rem(c, 2), which]
+        for source, (lo, hi) in zip((*rights, dqkv), (*FIRST_R, SELF_UNITS), strict=True):
+            first = pl.multiple_of((unit - lo) * UNIT, UNIT)
+            yield (
+                (unit >= lo) & (unit < hi),
+                pltpu.make_async_copy(source.at[:, pl.ds(first, UNIT)], place, sem),
+            )
+
+    def start_rights(c):
+        for which in range(2):
+            for cond, copy in right_copies(c, which):
+                pl.when(cond)(copy.start)
+
+    def store_unit(which, k, i, value):
+        for yy in range(2):
+            for xx in range(2):
+                first = (yy * 2 + xx) * rows
+                block = value[first : first + rows, :].astype(BF16)
+                if which == 0:
+                    gz[k, i, yy, xx, :, pl.ds(0, UNIT)] = block
+                else:
+                    gz[k, i, yy, xx, :, pl.ds(UNIT, width_z - UNIT)] = block[:, : width_z - UNIT]
+                    ga[k, i, yy, xx] = block[:, width_z - UNIT :]
+
+    def compute(c, k):
+        for n in range(1, ROWS_L):
+            pl.when(c == FIRST_L[n] // 2)(left_copy(n).wait)
+        for which in range(2):
+            unit = 2 * c + which
+            text = (unit >= TEXT_UNITS[0]) & (unit < TEXT_UNITS[1])
+            slot = lax.rem(sum((unit >= first).astype(jnp.int32) for first in FIRST_L) + 1, 2)
+
+            @pl.when(text)
+            def _():
+                first = pl.multiple_of((unit - TEXT_UNITS[0]) * UNIT, UNIT)
+                right_part = dkv_v[:, pl.ds(first, UNIT)]
+                for i in range(4):
+                    store_unit(which, k, i, dot_tn(text_v[:, pl.ds(i * 4 * rows, 4 * rows)], right_part))
+
+            @pl.when(jnp.logical_not(text))
+            def _():
+                par = lax.rem(c, 2)
+                pltpu.make_async_copy(rbuf.at[par, which], rbuf.at[par, which], r_sem.at[par, which]).wait()
+                right_part = rbuf[par, which]
+                for i in range(4):
+                    left_part = lbuf[slot, :, pl.ds(i * 4 * rows, 4 * rows)]
+                    store_unit(which, k, i, dot_tn(left_part, right_part))
+
+        for n in range(2, ROWS_L):
+            pl.when(c == FIRST_L[n - 1] // 2)(left_copy(n).start)
+        pl.when(c + 1 < total)(lambda: start_rights(c + 1))
 
     def out_copies(c):
         o = lax.rem(c, 2)
@@ -647,18 +779,7 @@
 
         return add
 
-    def start_load(c, k):
-        for index, (array, first) in enumerate(places):
-
-            @pl.when(c == index)
-            def _():
-                for copy in load_copies(array, first, k):
-                    copy.start()
-
     def begin(c, k):
-        for copy in load_copies(0, 0, k):
-            copy.wait()
-
         @pl.when(c >= slots)
         def _():
             pl.semaphore_wait(credit.at[0], 1)
@@ -784,69 +905,132 @@
         def _():
             signal_neighbours([credit.at[i] for i in (0, 1, 3, 2)], near, has_up, has_down)
 
-    stages = (start_load, begin, second, third, fourth, fifth, finish)
+    stages = (begin, second, third, fourth, fifth, finish)
+    left_copy(0).start()
+    start_rights(jnp.int32(0))
+    left_copy(1).start()
+    for copy in firsts:
+        copy.start()
+    left_copy(0).wait()
+    for copy in firsts:
+        copy.wait()
+    dqkv_copy = pltpu.make_async_copy(dqkv, dqkv_h, dqkv_sem)
 
     def body(turn, carry):
         for step, stage in enumerate(stages):
-            c = turn - step
+            c = turn - step - 1
 
             @pl.when((c >= 0) & (c < total))
             def _():
                 stage(c, lax.rem(c, slots))
 
+        pl.when(turn < total)(lambda: compute(turn, lax.rem(turn, slots)))
+
+        @pl.when((turn >= 1) & (turn <= heads))
+        def _():
+            head_back(turn - 1, q_v, k_v, v_v, do_v, lse_ref, dqkv, acc_k, acc_v)
+
+        pl.when(turn == heads + 1)(dqkv_copy.start)
         return carry
 
-    lax.fori_loop(0, total + len(stages) - 1, body, 0)
+    lax.fori_loop(0, total + len(stages), body, 0)
     for c in (total - 2, total - 1):
         for copy in out_copies(jnp.int32(c)):
             copy.wait()
-
-
-def scatter_all(grads, places, width_z, width_a, slots):
-    rows = grads[0].shape[3]
-    columns = len(places) * (width_z + width_a)
+    dqkv_copy.wait()
+
+
+def backward_all(lefts, rights, text, grad_text_rows, heads_in, log_sums):
+    frames, width = lefts[0].shape
+    rows = width // 16
+    part = heads_in[0].shape[1]
     dma = pltpu.SemaphoreType.DMA
-
-    def buffer(*shape, dtype=BF16):
-        return pltpu.VMEM((slots,) + shape, dtype)
-
+    vmem = pltpu.VMEM
+
+    def buffer(*shape):
+        return vmem((SLOTS,) + shape, BF16)
+
+    anywhere = pl.BlockSpec(memory_space=pl.ANY)
+    inputs = (*lefts, *rights, text, grad_text_rows, *heads_in, log_sums)
     return pl.pallas_call(
-        functools.partial(scatter_kernel, places, width_z, width_a, slots),
-        out_shape=jax.ShapeDtypeStruct((rows, columns), F32),
-        in_specs=[pl.BlockSpec(memory_space=pl.ANY)] * len(grads),
-        out_specs=pl.BlockSpec(memory_space=pl.ANY),
+        backward_kernel,
+        out_shape=[
+            jax.ShapeDtypeStruct((rows, UNITS * UNIT), F32),
+            jax.ShapeDtypeStruct((frames, 3 * part), BF16),
+        ],
+        in_specs=[anywhere] * (len(inputs) - 1) + [pl.BlockSpec(memory_space=vmem)],
+        out_specs=[anywhere] * 2,
         scratch_shapes=[
-            buffer(4, 2, 2, rows, width_z),
-            buffer(4, 2, 2, rows, width_a),
-            *[buffer(4, rows // 2, width_z)] * 6,
-            *[buffer(4, rows, width_z)] * 2,
-            *[buffer(rows // 2, width_a)] * 6,
-            *[buffer(4, 2, 2, rows, width_a)] * 2,
-            pltpu.VMEM((2, rows, width_z), F32),
-            pltpu.VMEM((2, rows, width_a), F32),
-            dma((slots, 2)),
+            buffer(4, 2, 2, rows, WIDTH_Z),
+            buffer(4, 2, 2, rows, WIDTH_A),
+            *[buffer(4, rows // 2, WIDTH_Z)] * 6,
+            *[buffer(4, rows, WIDTH_Z)] * 2,
+            *[buffer(rows // 2, WIDTH_A)] * 6,
+            *[buffer(4, 2, 2, rows, WIDTH_A)] * 2,
+            vmem((2, rows, WIDTH_Z), F32),
+            vmem((2, rows, WIDTH_A), F32),
+            vmem((2, frames, width), BF16),
+            vmem((2, 2, frames, UNIT), BF16),
+            vmem(text.shape, BF16),
+            vmem(grad_text_rows.shape, BF16),
+            *[vmem((frames, part), BF16)] * 4,
+            vmem((frames, 3 * part), BF16),
+            *[vmem((frames, 128), F32)] * 2,
+            dma((6,)),
+            dma((2,)),
             dma((2, 2)),
-            dma((slots,)),
-            dma((slots,)),
-            dma((slots, 8)),
-            dma((slots, 8)),
+            dma,
+            dma((2, 2)),
+            dma((SLOTS,)),
+            dma((SLOTS,)),
+            dma((SLOTS, 8)),
+            dma((SLOTS, 8)),
             pltpu.SemaphoreType.REGULAR((4,)),
         ],
         compiler_params=pltpu.CompilerParams(
             collective_id=1, has_side_effects=True, vmem_limit_bytes=VMEM_LIMIT
         ),
-        name="scatter_gradients",
-    )(*grads)
-
-
-def sum_cores(values):
-    return values + lax.ppermute(values, "tensor", [(0, 1), (1, 0)])
-
-
-def weight_grad_t(source_rows, grad_rows):
-    return jnp.einsum(
-        "cli,cla->ia", source_rows, grad_rows, preferred_element_type=jnp.float32
-    ).astype(BF16)
+        name="backward",
+    )(*inputs)
+
+
+def sum_everywhere_kernel(values, out, got, send_sem, recv_sem):
+    chip, core = lax.axis_index("dp"), lax.axis_index("tensor")
+    partners = [(chip, 1 - core)]
+    for bit in (1, 2, 4, 8):
+        partners.append((chip + bit * (1 - 2 * lax.rem(lax.div(chip, bit), 2)), core))
+    barrier = pltpu.get_barrier_semaphore()
+    for device in partners:
+        pl.semaphore_signal(barrier, inc=1, device_id=device, device_id_type=MESH_IDS)
+    pl.semaphore_wait(barrier, len(partners))
+    got[0] = values[...]
+    for step, device in enumerate(partners):
+        copy = pltpu.make_async_remote_copy(
+            src_ref=got.at[2 * step],
+            dst_ref=got.at[2 * step + 1],
+            send_sem=send_sem.at[step],
+            recv_sem=recv_sem.at[step],
+            device_id=device,
+            device_id_type=MESH_IDS,
+        )
+        copy.start()
+        copy.wait()
+        got[2 * step + 2] = got[2 * step] + got[2 * step + 1]
+    out[...] = got[2 * len(partners)]
+
+
+def sum_everywhere(values):
+    dma = pltpu.SemaphoreType.DMA
+    vmem = pl.BlockSpec(memory_space=pltpu.VMEM)
+    return pl.pallas_call(
+        sum_everywhere_kernel,
+        out_shape=jax.ShapeDtypeStruct(values.shape, F32),
+        in_specs=[vmem],
+        out_specs=vmem,
+        scratch_shapes=[pltpu.VMEM((11,) + values.shape, F32), dma((5,)), dma((5,))],
+        compiler_params=pltpu.CompilerParams(collective_id=2, has_side_effects=True),
+        name="sum_norm_gradients",
+    )(values)
 
 
 def project_t(row_data, weight):
@@ -855,6 +1039,32 @@
 
 def input_grad_t(grad_rows, weight):
     return jnp.einsum("cla,ia->cli", grad_rows, weight, preferred_element_type=jnp.float32)
+
+
+def other_core(values):
+    return lax.ppermute(values, "tensor", [(0, 1), (1, 0)])
+
+
+def share_rows(values):
+    other = other_core(values)
+    first = lax.axis_index("tensor") == 0
+    return jnp.concatenate(
+        [jnp.where(first, values, other), jnp.where(first, other, values)], axis=1
+    )
+
+
+def sum_rows(rows, product):
+    core, half = lax.axis_index("tensor"), rows[0].shape[1] // 2
+    theirs = product(*[lax.dynamic_slice_in_dim(r, (1 - core) * half, half, 1) for r in rows])
+    arriving = other_core(theirs.astype(BF16))
+    mine = product(*[lax.dynamic_slice_in_dim(r, core * half, half, 1) for r in rows])
+    return mine + arriving.astype(F32)
+
+
+def gelu_parts(values):
+    below = 0.5 * (1.0 + lax.erf(values * (0.5**0.5)))
+    density = jnp.exp(-0.5 * values * values) * 0.3989422804014327
+    return (values * below).astype(BF16), (below + values * density).astype(BF16)
 
 
 def gather_plan(columns):
@@ -866,10 +1076,6 @@
             family = "A" if since % 5 == 3 and size == 768 else "Z"
             chunks.append((array, first, size, family))
     return tuple(chunks)
-
-
-def scatter_plan(columns, width):
-    return tuple((array, first) for array, all_of in enumerate(columns) for first in range(0, all_of, width))
 
 
 def local_fast(
@@ -907,77 +1113,97 @@
         cross_value.T,
         cross_out,
         hidden_up.T,
-        hidden_down,
-    )
+    )
+    w_down = lax.all_gather(hidden_down, "dp", axis=0, tiled=True)
     gathered = gather_all(shards, gather_plan([s.shape[1] for s in shards]))
     gathered = [g.reshape(width, g.shape[-1]) for g in gathered]
     norms = gathered[0][:, :6].T.astype(jnp.float32)
     gain_self, bias_self, gain_cross, bias_cross, gain_ffn, bias_ffn = [norms[i] for i in range(6)]
-    w_q, w_k, w_v, w_o, w_cq, w_ck, w_cv, w_co, w_up, w_down = gathered[1:]
+    w_q, w_k, w_v, w_o, w_cq, w_ck, w_cv, w_co, w_up = gathered[1:]
     stream_one = hidden_in.astype(jnp.float32)
     key_two = split_heads(project_t(text_states, w_ck).astype(jnp.bfloat16))
     value_two = split_heads(project_t(text_states, w_cv).astype(jnp.bfloat16))
-    normed_one = gather_rows(layer_norm(stream_one, gain_self, bias_self).astype(jnp.bfloat16))
+    normed_one = share_rows(layer_norm(stream_one, gain_self, bias_self).astype(jnp.bfloat16))
     query_one = split_heads(project_t(normed_one, w_q).astype(jnp.bfloat16))
     key_one = split_heads(project_t(normed_one, w_k).astype(jnp.bfloat16))
     value_one = split_heads(project_t(normed_one, w_v).astype(jnp.bfloat16))
     attended_one, logsum_one = attend(query_one, key_one, value_one, True)
-    stream_two = stream_one + scatter_rows(project(flatten_heads(attended_one), w_o))
-    normed_two = gather_rows(layer_norm(stream_two, gain_cross, bias_cross).astype(jnp.bfloat16))
+    stream_two = stream_one + sum_rows([flatten_heads(attended_one)], lambda r: project(r, w_o))
+    normed_two = share_rows(layer_norm(stream_two, gain_cross, bias_cross).astype(jnp.bfloat16))
     query_two = split_heads(project_t(normed_two, w_cq).astype(jnp.bfloat16))
     attended_two, logsum_two = attend(query_two, key_two, value_two, False)
-    stream_three = stream_two + scatter_rows(project(flatten_heads(attended_two), w_co))
-    normed_three = gather_rows(layer_norm(stream_three, gain_ffn, bias_ffn).astype(jnp.bfloat16))
+    stream_three = stream_two + sum_rows([flatten_heads(attended_two)], lambda r: project(r, w_co))
+    normed_three = share_rows(layer_norm(stream_three, gain_ffn, bias_ffn).astype(jnp.bfloat16))
     upper = project_t(normed_three, w_up)
-    active = gelu_exact(upper).astype(jnp.bfloat16)
-    layer_out = (stream_three + scatter_rows(project(active, w_down))).astype(jnp.bfloat16)
+    active, slope = gelu_parts(upper)
+    layer_out = (stream_three + sum_rows([active], lambda r: project(r, w_down))).astype(jnp.bfloat16)
     grad_three = cotangent.astype(jnp.float32)
-    grad_branch = gather_grads(grad_three.astype(jnp.bfloat16))
-    grad_down = weight_grad_t(grad_branch, active)
+    grad_branch = share_rows(grad_three.astype(jnp.bfloat16))
+    branch_three = grad_branch
     grad_active = jnp.einsum("clo,of->clf", grad_branch, w_down, preferred_element_type=jnp.float32)
-    grad_upper = jax.vjp(gelu_exact, upper)[1](grad_active)[0].astype(jnp.bfloat16)
-    grad_up = weight_grad_t(normed_three, grad_upper)
+    grad_upper = (grad_active * slope.astype(F32)).astype(jnp.bfloat16)
     norm_back = jax.vjp(layer_norm, stream_three, gain_ffn, bias_ffn)[1]
     grad_stream, grad_gain_ffn, grad_bias_ffn = norm_back(
-        scatter_grads(input_grad_t(grad_upper, w_up))
+        sum_rows([grad_upper], lambda r: input_grad_t(r, w_up))
     )
     grad_two = grad_three + grad_stream
-    grad_branch = gather_grads(grad_two.astype(jnp.bfloat16))
-    grad_out_cross, grad_attended = heads_grads(grad_branch, attended_two, w_co)
+    grad_branch = share_rows(grad_two.astype(jnp.bfloat16))
+    branch_two = grad_branch
+    grad_attended = split_heads(
+        jnp.einsum("clo,oa->cla", grad_branch, w_co, preferred_element_type=F32).astype(BF16)
+    )
     grad_query, grad_key, grad_value = attend_back(
         query_two, key_two, value_two, grad_attended, logsum_two, False
     )
     grad_query = flatten_heads(grad_query).astype(jnp.bfloat16)
     grad_key = flatten_heads(grad_key).astype(jnp.bfloat16)
     grad_value = flatten_heads(grad_value).astype(jnp.bfloat16)
-    grad_query_cross = weight_grad_t(normed_two, grad_query)
-    grad_key_cross = weight_grad_t(text_states, grad_key)
-    grad_value_cross = weight_grad_t(text_states, grad_value)
+    grad_query_two = grad_query
     text_part = input_grad_t(grad_key, w_ck) + input_grad_t(grad_value, w_cv)
-    grad_text = lax.psum_scatter(
-        text_part.astype(jnp.bfloat16), "tensor", scatter_dimension=2, tiled=True
-    ).astype(jnp.float32)
+    core, half = lax.axis_index("tensor"), width // 2
+    arriving = other_core(
+        lax.dynamic_slice_in_dim(text_part, (1 - core) * half, half, 2).astype(BF16)
+    )
+    grad_text = lax.dynamic_slice_in_dim(text_part, core * half, half, 2) + arriving.astype(F32)
     norm_back = jax.vjp(layer_norm, stream_two, gain_cross, bias_cross)[1]
     grad_stream, grad_gain_cross, grad_bias_cross = norm_back(
-        scatter_grads(input_grad_t(grad_query, w_cq))
+        sum_rows([grad_query], lambda r: input_grad_t(r, w_cq))
     )
     grad_one = grad_two + grad_stream
-    grad_branch = gather_grads(grad_one.astype(jnp.bfloat16))
-    grad_out_self, grad_attended = heads_grads(grad_branch, attended_one, w_o)
-    grad_query, grad_key, grad_value = attend_back(
-        query_one, key_one, value_one, grad_attended, logsum_one, True
-    )
-    grad_query = flatten_heads(grad_query).astype(jnp.bfloat16)
-    grad_key = flatten_heads(grad_key).astype(jnp.bfloat16)
-    grad_value = flatten_heads(grad_value).astype(jnp.bfloat16)
-    grad_query_self = weight_grad_t(normed_one, grad_query)
-    grad_key_self = weight_grad_t(normed_one, grad_key)
-    grad_value_self = weight_grad_t(normed_one, grad_value)
-    grad_normed = (
-        input_grad_t(grad_query, w_q) + input_grad_t(grad_key, w_k) + input_grad_t(grad_value, w_v)
+    grad_branch = share_rows(grad_one.astype(jnp.bfloat16))
+    grad_attended = jnp.einsum(
+        "clo,oa->cla", grad_branch, w_o, preferred_element_type=F32
+    ).astype(BF16)
+    part = grad_attended.shape[2]
+    summed, grad_heads = backward_all(
+        [
+            r[0]
+            for r in (branch_three, normed_three, branch_two, normed_two, grad_branch, normed_one)
+        ],
+        [
+            r[0]
+            for r in (
+                active,
+                grad_upper,
+                flatten_heads(attended_two),
+                grad_query_two,
+                flatten_heads(attended_one),
+            )
+        ],
+        text_states[0],
+        jnp.concatenate([grad_key[0], grad_value[0]], axis=1),
+        [flatten_heads(query_one)[0], flatten_heads(key_one)[0], flatten_heads(value_one)[0], grad_attended[0]],
+        jnp.pad(logsum_one[0], ((0, 4), (0, 0))),
+    )
+    grad_query, grad_key, grad_value = [
+        grad_heads[None, :, n * part : (n + 1) * part] for n in range(3)
+    ]
+    grad_normed = sum_rows(
+        [grad_query, grad_key, grad_value],
+        lambda q, k, v: input_grad_t(q, w_q) + input_grad_t(k, w_k) + input_grad_t(v, w_v),
     )
     norm_back = jax.vjp(layer_norm, stream_one, gain_self, bias_self)[1]
-    grad_stream, grad_gain_self, grad_bias_self = norm_back(scatter_grads(grad_normed))
+    grad_stream, grad_gain_self, grad_bias_self = norm_back(grad_normed)
     grad_input = grad_one + grad_stream
     norm_grads = jnp.stack(
         [
@@ -987,31 +1213,13 @@
             grad_bias_cross,
             grad_gain_ffn,
             grad_bias_ffn,
-        ],
-        axis=1,
-    )
-    norm_grads = jnp.pad(norm_grads, ((0, 0), (0, 122)))
-    norm_sums = sum_cores(lax.psum_scatter(norm_grads, "dp", scatter_dimension=0, tiled=True)).T
-    grads = (
-        grad_down,
-        grad_up,
-        grad_out_cross.astype(BF16),
-        grad_query_cross,
-        grad_key_cross,
-        grad_value_cross,
-        grad_out_self.astype(BF16),
-        grad_query_self,
-        grad_key_self,
-        grad_value_self,
-    )
-    columns = [g.shape[1] for g in grads]
-    summed = scatter_all(
-        [g.reshape(4, 2, 2, width // 16, g.shape[1]) for g in grads],
-        scatter_plan(columns, 768),
-        640,
-        128,
-        8,
-    )
+        ]
+    )
+    rows = width // 16
+    norm_sums = lax.dynamic_slice_in_dim(
+        sum_everywhere(jnp.pad(norm_grads, ((0, 2), (0, 0)))), lax.axis_index("dp") * rows, rows, 1
+    )
+    columns = [hidden_down.shape[1]] * 2 + [part] * 8
     pieces, first = [], 0
     for count in columns:
         pieces.append(summed[:, first : first + count])

time: 1130 us -> 853 us (0.75)
  matrix products: 315 us -> 171 us
  waiting for transfers between devices: 100 us -> 9.91 us
  Pallas kernels: 572 us -> 529 us
  other arithmetic: 83.7 us -> 63.1 us
  local copies, waits for them, and re-layouts: 38.4 us -> 55.6 us
    dot_general x12 -> x2, matrix products: 73.5 us -> 7.37 us  [the longest x1 4.63 us: local_fast(): jnp.einsum('clo,oa->cla', grad_branch, w_o, preferred_element_type=F32)]
    reduce_scatter x7 -> x0, waiting for transfers between devices: 54.7 us -> none  [the longest x3 42.5 us: scatter_rows(): return lax.psum_scatter(values, 'tensor', scatter_dimension=1, tiled=True)]
    pallas_call x1, Pallas kernels: 274 us -> 226 us  [gather_all(): pl.pallas_call(functools.partial(gather_kernel, count, chunks), out_shape...]
    all_gather x6 -> x1, waiting for transfers between devices: 44.9 us -> 0.01 us  [local_fast(): w_down = lax.all_gather(hidden_down, 'dp', axis=0, tiled=True)]
    dot_general x7, matrix products: 66.9 us -> 38 us  [project_t(): jnp.einsum('cli,io->clo', row_data, weight, preferred_element_type=jnp.fl...]
    dot_general x4 -> x2, matrix products: 25.6 us -> 1.09 us  [attend_back(): jnp.einsum('cqhe,ckhe->chqk', grad_blk, val_rows[:, :key_end], preferred_...]
    convert_element_type x4 -> x2, other arithmetic: 24.9 us -> 0.95 us  [attend_back(): grad_scores = (soft * (grad_soft - inner)).astype(jnp.bfloat16)]
    dot_general x4 -> x2, matrix products: 22.5 us -> 2.53 us  [attend_back(): jnp.einsum('chqk,cqhe->ckhe', soft.astype(jnp.bfloat16), grad_blk, prefer...]
  transfers between devices with their start and end apart: 15 -> 14, of which waited for: 9 -> 4; matrix products, arithmetic and copies ran while one was open for 23% -> 22% of each run, Pallas kernels for 26% -> 0%
where the time goes in v2:
time: 853 us; the launch traced here: 847 us
  Pallas kernels  529 us (62%)
  matrix products  171 us (20%)
  other arithmetic  63.1 us (7%)
  local copies, waits for them, and re-layouts  55.6 us (7%)
  between operations  15.7 us (2%)
  waiting for transfers between devices  9.91 us (1%)
    pallas_call x1, Pallas kernels, backward_all(): pl.pallas_call(backward_kernel, out_shape=[jax.ShapeDtypeStruct((rows, UN...  286 us
    pallas_call x1, Pallas kernels, gather_all(): pl.pallas_call(functools.partial(gather_kernel, count, chunks), out_shape...  226 us
    dot_general x12, matrix products, input_grad_t(): jnp.einsum('cla,ia->cli', grad_rows, weight, preferred_element_type=jnp.f...  41.4 us
    dot_general x7, matrix products, project_t(): jnp.einsum('cli,io->clo', row_data, weight, preferred_element_type=jnp.fl...  38 us
    dot_general x6, matrix products, project(): jnp.einsum('cli,oi->clo', row_data, weight, preferred_element_type=jnp.fl...  30 us
    unnamed x213, local copies, waits for them, and re-layouts  24.3 us
    dot_general x1, matrix products, local_fast(): jnp.einsum('clo,of->clf', grad_branch, w_down, preferred_element_type=jnp...  17.1 us
  transfers between devices with their start and end apart: 14, of which 4 were waited for; matrix products, arithmetic and copies ran while one was open for 22% of the time, Pallas kernels for 0%

profile of v2, /device:TPU:0, one launch (start us, length us, event | category | flops | bytes accessed | tf_op | source)
XLA Modules:
  0.0 847.1 jit_solution(11695078777756979929)
XLA Ops:
  8.9 226.4 %gather_weights.1 = (bf16[4,2,2,96,128]{4,3,2,1,0:T(8,128)(2,1)}, bf16[4,2,2,96,768]{4,3,2,1,0:T(8,128)(2,1)}, bf16[4,2,2,96,768]{4,3,2,1,0:T(8,128)(2,1)}, bf16...) custom-call(bf16[96,128]{1,0:T(8,128)(2,1)} %pad.24.refs_0_, ...), custom_call_target="tpu_custom_call" | custom-call | tf_op jit(solution)/shard_map/gather_weights/pallas_call | solution.py:517
  240.0 2.2 collective-permute-done
  242.2 2.5 broadcast_select_fusion.11
  246.4 4.8 convolution_convert_fusion.7.refs_13_
  251.2 2.8 copy.101
  253.9 5.7 convolution_convert_fusion.6.refs_14_
  261.6 5.9 convolution_convert_fusion.8.refs_15_
  267.5 2.9 copy.99
  270.4 2.1 fusion.8
  272.5 2.6 fusion.9
  275.1 2.0 copy-done.6
  277.1 11.9 %fusion = (f32[12,512]{1,0:T(8,128)S(1)}, f32[12,512,1024]{2,1,0:T(8,128)}) fusion(pred[512,1024]{1,0:T(8,128)(4,1)} %iota_compare_fusion, bf16[1024,12,64]{0,2,1:T(8,128)(2,1)S(1)} %bitcast.293, bf16[1,1024,12,64]{1,3,2,0:T(8,128)(2,1)S(1)} %bitcast.302), kind=kOutput, calls=%fused_computation.3 | convolution fusion | flops 824174592 | bytes 28073984 | tf_op jit(solution)/shard_map/cqhe,ckhe->chqk/dot_general | solution.py:48
  289.1 12.4 %fusion.1 = f32[12,512]{1,0:T(8,128)S(1)} fusion(f32[12,512,1024]{2,1,0:T(8,128)} %get-tuple-element.175, f32[12,512]{1,0:T(8,128)S(1)} %get-tuple-element.174, pred[512,1024]{1,0:T(8,128)(4,1)S(1)} %copy-done.48), kind=kLoop, calls=%fused_computation.4 | loop fusion | flops 25159680 | bytes 25739264 | tf_op jit(solution)/shard_map/reduce_sum | solution.py:72
  301.5 3.7 copy-done
  305.2 9.1 %fusion.57 = bf16[1,512,12,64]{1,3,2,0:T(8,128)(2,1)S(1)} fusion(bf16[1024,12,64]{0,2,1:T(8,128)(2,1)} %bitcast.334, f32[12,512,1024]{2,1,0:T(8,128)S(1)} %copy-done, f32[12,512]{1,0:T(8,128)S(1)} %fusion.1, f32[12,512]{1,0:T(8,128)S(1)} %get-tuple-element.174, pred[512,1024]{1,0:T(8,128)(4,1)S(1)} %copy-done.48), kind=kOutput, calls=%fused_computation.134 | convolution fusion | flops 837156864 | bytes 28098560 | tf_op jit(solution)/shard_map/chqk,ckhe->cqhe/dot_general | solution.py:75
  314.3 7.0 fusion.58
  321.5 2.0 copy-done.96
  325.1 3.5 collective-permute-done.1
  328.6 4.5 fusion.143
  338.0 2.8 fusion.64
  342.6 2.6 broadcast_select_fusion.9
  345.2 2.7 convolution_convert_fusion.5
  354.3 2.9 collective-permute-done.3
  360.5 1.8 broadcast_select_fusion.5
  366.3 14.9 %multiply_convert_fusion.1 = (bf16[1024,3072]{1,0:T(8,128)(2,1)}, f32[1024,3072]{1,0:T(8,128)}) fusion(bf16[1536,3072]{1,0:T(8,128)(2,1)S(1)} %bitcast.354, bf16[1,512,1536]{2,1,0:T(8,128)(2,1)S(1)} %get-tuple-element.163, bf16[1,512,1536]{2,1,0:T(8,128)(2,1)S(1)} %get-tuple-element.162), kind=kOutput, calls=%fused_computation.12 | convolution fusion | flops 9685696512 | bytes 31457280 | tf_op jit(solution)/shard_map/cli,io->clo/dot_general | solution.py:1037
  381.1 17.1 %multiply_convert_fusion.refs_7_ = bf16[1024,3072]{1,0:T(8,128)(2,1)S(1)} fusion(bf16[1536,3072]{1,0:T(8,128)(2,1)} %all-gather.2.cloned.1.call-done, f32[1024,3072]{1,0:T(8,128)} %get-tuple-element.187, bf16[1,512,1536]{2,1,0:T(8,128)(2,1)} %get-tuple-element.161, bf16[1,512,1536]{2,1,0:T(8,128)(2,1)} %get-tuple-element.160), kind=kOutput, calls=%fused_computation.11 | convolution fusion | flops 9707716608 | bytes 31457280 | tf_op jit(solution)/shard_map/clo,of->clf/dot_general | solution.py:1143
  398.3 11.3 %fusion.40 = bf16[1,512,1536]{2,1,0:T(8,128)(2,1)} fusion(bf16[1536,3072]{1,0:T(8,128)(2,1)} %bitcast.350, bf16[1024,3072]{1,0:T(8,128)(2,1)S(1)} %multiply_convert_fusion.refs_7_, s32[]{:T(128)S(6)} %select_n.97), kind=kOutput, calls=%fused_computation.83 | convolution fusion | flops 4832624640 | bytes 14155780 | tf_op jit(solution)/shard_map/cla,ia->cli/dot_general | solution.py:1041
  410.0 2.7 copy.119.refs_10_
  413.3 4.0 maximum_bitcast_fusion.3.refs_0_
  418.2 3.1 maximum_bitcast_fusion
  421.9 10.9 %multiply_reduce_fusion = (f32[1536]{0:T(1024)S(1)}, f32[512]{0:T(512)S(1)}, f32[1536]{0:T(1024)S(1)}, f32[1,512,1536]{2,1,0:T(8,128)S(1)}) fusion(f32[1,512,1536]{2,1,0:T(8,128)S(1)} %copy-done.2, f32[512]{0:T(512)S(1)} %fusion.127, f32[512]{0:T(512)S(1)} %broadcast_multiply_fusion, f32[1536]{0:T(1024)S(1)} %get-tuple-element.133, ...), kind=kOutput, calls=%fused_computation.55 | convolution fusion | flops 4839698944 | bytes 20471812 | tf_op jit(solution)/shard_map/cla,ia->cli/dot_general | solution.py:1041
  436.1 2.6 copy.117.refs_8_
  438.7 3.7 maximum_bitcast_fusion.2.refs_1_
  442.4 9.9 %fusion.43 = bf16[1,512,1536]{2,1,0:T(8,128)(2,1)S(1)} fusion(bf16[1536,3072]{1,0:T(8,128)(2,1)} %all-gather.2.cloned.1.call-done, bf16[1024,3072]{1,0:T(8,128)(2,1)} %get-tuple-element.186.refs_6_, s32[]{:T(128)S(6)} %select_n.97), kind=kOutput, calls=%fused_computation.84 | convolution fusion | flops 4832624640 | bytes 14155780 | tf_op jit(solution)/shard_map/cli,oi->clo/dot_general | solution.py:29
  453.3 2.2 broadcast_select_fusion.3
  455.9 2.7 convolution_convert_fusion.4
  463.7 2.6 fusion.48
  466.5 10.9 %add_convert_fusion = bf16[1,512,1536]{2,1,0:T(8,128)(2,1)} fusion(f32[1,512,1536]{2,1,0:T(8,128)S(1)} %copy-done.3, bf16[1,512,1536]{2,1,0:T(8,128)(2,1)} %collective-permute-done.5, bf16[1536,3072]{1,0:T(8,128)(2,1)} %all-gather.2.cloned.1.call-done, bf16[1024,3072]{1,0:T(8,128)(2,1)} %get-tuple-element.186.refs_6_, s32[]{:T(128)S(6)} %select_n.96), kind=kOutput, calls=%fused_computation.68 | convolution fusion | flops 4834983936 | bytes 18874372 | tf_op jit(solution)/shard_map/cli,oi->clo/dot_general | solution.py:29
  479.1 4.4 multiply_reduce_fusion.1
  492.4 2.5 fusion.147
  496.8 2.6 copy.118.refs_9_
  500.1 2.2 broadcast_select_fusion.1
  502.7 4.6 convolution_convert_fusion.3.refs_16_
  507.3 3.0 maximum_bitcast_fusion.4
  510.3 286.4 %backward.1 = (f32[96,12288]{1,0:T(8,128)}, bf16[1024,2304]{1,0:T(8,128)(2,1)}) custom-call(bf16[1024,1536]{1,0:T(8,128)(2,1)} %maximum_bitcast_fusion.3.refs_0_, bf16[1024,1536]{1,0:T(8,128)(2,1)} %maximum_bitcast_fusion.2.refs_1_, bf16[1024,1536]{1,0:T(8,128)(2,1)} %get-tuple-element.199.refs_2_, bf16[1024,1536]{1,0:T(8,128)(2,1)} %get-tuple-element.198.refs_3_, ...), custom_call_target="tpu_custom_call" | custom-call | tf_op jit(solution)/shard_map/backward/pallas_call | solution.py:955
  796.8 2.8 fusion.142
  816.6 16.2 %sum_norm_gradients.1 = f32[8,1536]{1,0:T(8,128)} custom-call(f32[8,1536]{1,0:T(8,128)} %pad.26.values), custom_call_target="tpu_custom_call" | custom-call | tf_op jit(solution)/shard_map/sum_norm_gradients/pallas_call | solution.py:1025
  834.2 5.8 add_add_fusion.3
  (326 shorter events, 75.4 us)
Async XLA Ops:
  7.2 229.9 %copy-start.4 = (bf16[1,512,1536]{2,1,0:T(8,128)(2,1)S(1)}, bf16[1,512,1536]{2,1,0:T(8,128)(2,1)}, u32[]{:S(2)}) copy-start(bf16[1,512,1536]{2,1,0:T(8,128)(2,1)} %param.35) | copy-start | bytes 4718596
  7.2 373.9 %all-gather.2.cloned.1.call-start = ((), (), s32[]{:S(2)}) async-start(), calls=%async_computation | async-start | bytes 10027008 | tf_op jit(solution)/shard_map/all_gather | solution.py:1117
  237.1 5.1 copy-start.59
  237.1 105.5 %copy-start.65 = (f32[1536]{0:T(1024)}, f32[1536]{0:T(1024)S(1)}, u32[]{:S(2)}) copy-start(f32[1536]{0:T(1024)S(1)} %get-tuple-element.136) | copy-start | bytes 18436
  237.4 7.3 copy-start.75
  237.9 6.8 copy-start.86
  238.0 6.8 copy-start.79
  238.6 3.6 collective-permute-start
  240.0 6.4 copy-start.94
  272.5 4.6 copy-start.6
  272.5 41.8 %copy-start.61 = (f32[12,512]{1,0:T(8,128)}, f32[12,512]{1,0:T(8,128)S(1)}, u32[]{:S(2)}) copy-start(f32[12,512]{1,0:T(8,128)S(1)} %get-tuple-element.176) | copy-start | bytes 73732
  277.1 37.2 %copy-start.67 = (f32[12,512]{1,0:T(8,128)}, f32[12,512]{1,0:T(8,128)S(1)}, u32[]{:S(2)}) copy-start(f32[12,512]{1,0:T(8,128)S(1)} %fusion.9) | copy-start | bytes 73732
  277.1 11.9 %copy-start.48 = (pred[512,1024]{1,0:T(8,128)(4,1)S(1)}, pred[512,1024]{1,0:T(8,128)(4,1)}, u32[]{:S(2)}) copy-start(pred[512,1024]{1,0:T(8,128)(4,1)} %iota_compare_fusion) | copy-start | bytes 1572868
  289.1 12.4 %copy-start.63 = (f32[12,512]{1,0:T(8,128)}, f32[12,512]{1,0:T(8,128)S(1)}, u32[]{:S(2)}) copy-start(f32[12,512]{1,0:T(8,128)S(1)} %get-tuple-element.174) | copy-start | bytes 73732
  289.1 16.1 %copy-start = (f32[12,512,1024]{2,1,0:T(8,128)S(1)}, f32[12,512,1024]{2,1,0:T(8,128)}, u32[]{:S(2)}) copy-start(f32[12,512,1024]{2,1,0:T(8,128)} %get-tuple-element.175) | copy-start | bytes 75497472
  301.5 12.8 %copy-start.69 = (f32[12,512]{1,0:T(8,128)}, f32[12,512]{1,0:T(8,128)S(1)}, u32[]{:S(2)}) copy-start(f32[12,512]{1,0:T(8,128)S(1)} %fusion.1) | copy-start | bytes 73732
  305.2 9.1 %copy-start.55 = (bf16[1024,768]{0,1:T(8,128)(2,1)S(1)}, bf16[1024,768]{0,1:T(8,128)(2,1)}, u32[]{:S(2)}) copy-start(bf16[1024,768]{0,1:T(8,128)(2,1)} %copy.99) | copy-start | bytes 4718596
  325.0 3.6 collective-permute-start.1
  335.6 7.1 collective-permute-start.2
  351.0 6.2 copy-start.20
  353.7 3.5 collective-permute-start.3
  354.1 6.4 collective-permute-start.6
  358.8 4.8 copy-start.1
  358.8 7.4 slice-start.2
  359.5 6.8 slice-start.3
  360.1 3.5 collective-permute-start.4
  398.2 11.3 %copy-start.47 = (bf16[1024,3072]{1,0:T(8,128)(2,1)}, bf16[1024,3072]{1,0:T(8,128)(2,1)S(1)}, u32[]{:S(2)}) copy-start(bf16[1024,3072]{1,0:T(8,128)(2,1)S(1)} %multiply_convert_fusion.refs_7_) | copy-start | bytes 18874372
  409.5 11.8 %collective-permute-start.7 = (bf16[1,512,1536]{2,1,0:T(8,128)(2,1)}, bf16[1,512,1536]{2,1,0:T(8,128)(2,1)}, u32[]{:S(2)}, u32[]{:S(2)}) collective-permute-start(bf16[1,512,1536]{2,1,0:T(8,128)(2,1)} %fusion.40), channel_id=1, source_target_pairs={{0,1},{1,0},{2,3},{3,2},{4,5},{5,4},{6,7},{7,6},{8,9},{9,8},{10,11... | collective-permute-start | bytes 4718600 | tf_op jit(solution)/shard_map/ppermute | solution.py:1045
  412.7 4.7 copy-start.74
  413.3 4.9 copy-start.34
  421.4 11.4 %copy-start.91 = (f32[512]{0:T(512)S(1)}, f32[512]{0:T(512)}, u32[]{:S(2)}) copy-start(f32[512]{0:T(512)} %copy-done.90) | copy-start | bytes 6148
  435.9 17.4 %collective-permute-start.8 = (bf16[1,512,1536]{2,1,0:T(8,128)(2,1)}, bf16[1,512,1536]{2,1,0:T(8,128)(2,1)}, u32[]{:S(2)}, u32[]{:S(2)}) collective-permute-start(bf16[1,512,1536]{2,1,0:T(8,128)(2,1)} %fusion.50), channel_id=1, source_target_pairs={{0,1},{1,0},{2,3},{3,2},{4,5},{5,4},{6,7},{7,6},{8,9},{9,8},{10,11... | collective-permute-start | bytes 4718600 | tf_op jit(solution)/shard_map/ppermute | solution.py:1045
  436.1 25.2 %copy-start.56 = (f32[12,512]{1,0:T(8,128)}, f32[12,512]{1,0:T(8,128)S(1)}, u32[]{:S(2)}) copy-start(f32[12,512]{1,0:T(8,128)S(1)} %log_add_fusion) | copy-start | bytes 73732
  452.3 14.2 %collective-permute-start.5 = (bf16[1,512,1536]{2,1,0:T(8,128)(2,1)S(1)}, bf16[1,512,1536]{2,1,0:T(8,128)(2,1)}, u32[]{:S(2)}, u32[]{:S(2)}) collective-permute-start(bf16[1,512,1536]{2,1,0:T(8,128)(2,1)S(1)} %fusion.43), channel_id=1, source_target_pairs={{0,1},{1,0},{2,3},{3,2},{4,5},{5,4},{6,7},{7,6},{8,9},{9,8},{10,11... | collective-permute-start | bytes 4718600 | tf_op jit(solution)/shard_map/ppermute | solution.py:1045
  458.7 19.1 %copy-start.42 = (bf16[1024,768]{0,1:T(8,128)(2,1)}, bf16[1024,768]{0,1:T(8,128)(2,1)S(1)}, u32[]{:S(2)}) copy-start(bf16[1024,768]{0,1:T(8,128)(2,1)S(1)} %convolution_convert_fusion.4) | copy-start | bytes 4718596
  462.3 16.7 %copy-start.44 = (bf16[1,1024,12,64]{1,3,2,0:T(8,128)(2,1)}, bf16[1,1024,12,64]{1,3,2,0:T(8,128)(2,1)S(1)}, u32[]{:S(2)}) copy-start(bf16[1,1024,12,64]{1,3,2,0:T(8,128)(2,1)S(1)} %maximum_convert_fusion) | copy-start | bytes 4718596
  466.3 11.1 %copy-start.46 = (bf16[1024,768]{0,1:T(8,128)(2,1)S(1)}, bf16[1024,768]{0,1:T(8,128)(2,1)}, u32[]{:S(2)}) copy-start(bf16[1024,768]{0,1:T(8,128)(2,1)} %copy-done.45) | copy-start | bytes 4718596
  466.3 12.6 %collective-permute-start.9 = (bf16[1,512,1536]{2,1,0:T(8,128)(2,1)}, bf16[1,512,1536]{2,1,0:T(8,128)(2,1)}, u32[]{:S(2)}, u32[]{:S(2)}) collective-permute-start(bf16[1,512,1536]{2,1,0:T(8,128)(2,1)} %fusion.48), channel_id=1, source_target_pairs={{0,1},{1,0},{2,3},{3,2},{4,5},{5,4},{6,7},{7,6},{8,9},{9,8},{10,11... | collective-permute-start | bytes 4718600 | tf_op jit(solution)/shard_map/ppermute | solution.py:1045
  478.9 4.6 copy-start.89
  488.7 11.4 %collective-permute-start.10 = (bf16[1,512,1536]{2,1,0:T(8,128)(2,1)}, bf16[1,512,1536]{2,1,0:T(8,128)(2,1)}, u32[]{:S(2)}, u32[]{:S(2)}) collective-permute-start(bf16[1,512,1536]{2,1,0:T(8,128)(2,1)} %fusion.136), channel_id=1, source_target_pairs={{0,1},{1,0},{2,3},{3,2},{4,5},{5,4},{6,7},{7,6},{8,9},{9,8},{10,11... | collective-permute-start | bytes 4718600 | tf_op jit(solution)/shard_map/ppermute | solution.py:1045
  495.0 5.1 copy-start.93
  495.0 5.1 copy-start.92
  495.9 3.5 collective-permute-start.12
  502.7 4.6 copy-start.37
  502.7 4.6 copy-start.39
  799.9 5.1 slice-start
  804.9 6.0 collective-permute-start.11
  813.0 21.2 %copy-start.19 = (bf16[1,512,1536]{2,1,0:T(8,128)(2,1)S(1)}, bf16[1,512,1536]{2,1,0:T(8,128)(2,1)}, u32[]{:S(2)}) copy-start(bf16[1,512,1536]{2,1,0:T(8,128)(2,1)} %param.53) | copy-start | bytes 4718596
  (72 other events, 173.7 us)
Sparse Core Ops, SparseCore 0:
  238.8 121.6 all-gather.1

commit v3 on v2

--- a/solution.py
+++ b/solution.py
@@ -393,9 +393,8 @@
         )
 
 
-def gather_kernel(count, chunks, *refs):
-    shards, outs = refs[:count], refs[count : 2 * count]
-    local_sem, send_sem, zs, xs, ys, ds = refs[2 * count :]
+def gather_engine(chunks, shards, outs, sems):
+    local_sem, send_sem, zs, xs, ys, ds = sems
     x, y, z, core = my_place()
     xn, yn = 1 - x, 1 - y
     near = neighbours(x, y, z, core)
@@ -403,19 +402,21 @@
     has_up, has_down = z < 3, z > 0
     barrier = pltpu.get_barrier_semaphore()
     signal_neighbours([barrier] * 4, near, has_up, has_down)
-    pl.semaphore_wait(barrier, 2 + has_up.astype(jnp.int32) + has_down.astype(jnp.int32))
+    pl.semaphore_signal(barrier, inc=1, device_id=(lax.axis_index("dp"), 1 - core), device_id_type=MESH_IDS)
+    pl.semaphore_wait(barrier, 3 + has_up.astype(jnp.int32) + has_down.astype(jnp.int32))
     total = len(chunks)
     pending = []
 
-    half_rows = shards[0].shape[0] // 2
 
     def span(c):
         _, first, width, _ = chunks[c]
         return pl.ds(first, width)
 
     def at(zz, yy, xx, c, half=None):
+        ref = outs[chunks[c][0]]
+        half_rows = ref.shape[3] // 2
         lines = slice(None) if half is None else pl.ds(half * half_rows, half_rows)
-        return outs[chunks[c][0]].at[zz, yy, xx, lines, span(c)]
+        return ref.at[zz, yy, xx, lines, span(c)]
 
     def plane(zz, c):
         return outs[chunks[c][0]].at[zz, :, :, :, span(c)]
@@ -502,23 +503,319 @@
                     send(plane(block, c), plane(block, c), zs.at[c, block], device, exists & more)
 
     stages = 6
-    for turn in range(total + stages - 1):
+
+    def turn(number):
         for step in range(stages):
-            c = turn - step
+            c = number - step
             if 0 <= c < total:
                 (stage_z if chunks[c][3] == "Z" else stage_a)(c, step)
-    for cond, copy in pending:
-        when(cond, copy.wait_send)
-
-
-def gather_all(shards, chunks):
+
+    def finish():
+        for cond, copy in pending:
+            when(cond, copy.wait_send)
+
+    return turn, finish
+
+
+def total_of(*parts):
+    value = parts[0].astype(F32)
+    for part in parts[1:]:
+        value = value + part.astype(F32)
+    return value
+
+
+def dot_nt(left, right):
+    return lax.dot_general(left, right, (((1,), (1,)), ((), ())), preferred_element_type=F32)
+
+
+def dot_tn(left, right):
+    return lax.dot_general(left, right, (((0,), (0,)), ((), ())), preferred_element_type=F32)
+
+
+def dot_nn(left, right):
+    return jnp.dot(left, right, preferred_element_type=F32)
+
+
+def project_rows(source, weight, store, rows=256, transposed=False):
+    def body(n, carry):
+        first = pl.multiple_of(n * rows, rows)
+        part = source[pl.ds(first, rows), :]
+        store(first, dot_nt(part, weight[...]) if transposed else dot_nn(part, weight[...]))
+        return carry
+
+    lax.fori_loop(0, source.shape[0] // rows, body, 0)
+
+
+def normalize(values, gain, shift):
+    offset = values - jnp.mean(values, axis=-1, keepdims=True)
+    spread = jnp.mean(offset * offset, axis=-1, keepdims=True)
+    return offset * lax.rsqrt(spread + norm_eps) * gain + shift
+
+
+def head_lanes(half):
+    return lax.div(lax.broadcasted_iota(jnp.int32, (1, 128), 1), 64) == half
+
+
+def only(mask, value):
+    return jnp.where(mask, value.astype(F32), 0.0).astype(BF16)
+
+
+def pair_forward(pair, q_ref, k_ref, v_ref, o_ref, lse_ref, causal):
+    cols = pl.ds(pl.multiple_of(pair * 128, 128), 128)
+    block = 256
+    keep = lax.broadcasted_iota(jnp.int32, (block, block), 0) <= lax.broadcasted_iota(
+        jnp.int32, (block, block), 1
+    )
+    for i in range(q_ref.shape[0] // block):
+        rows = pl.ds(i * block, block)
+        parts = [(0, k_ref.shape[0], False)]
+        if causal:
+            parts = [(0, i * block, False)] * (i > 0) + [(i * block, block, True)]
+        total = 0.0
+        for half in range(2):
+            mine = head_lanes(half)
+            q = only(mine, q_ref[rows, cols])
+            scores = []
+            for first, count, diagonal in parts:
+                part = dot_nt(k_ref[pl.ds(first, count), cols], q) * score_scale
+                scores.append(jnp.where(keep, part, -1e30) if diagonal else part)
+            peak = functools.reduce(
+                jnp.maximum, [jnp.max(part, axis=0, keepdims=True) for part in scores]
+            )
+            scores = [jnp.exp(part - peak) for part in scores]
+            weight = sum(jnp.sum(part, axis=0, keepdims=True) for part in scores)
+            lse_ref[pl.ds(2 * pair + half, 1), rows] = peak + jnp.log(weight)
+            share = 1.0 / weight
+            for (first, count, _), part in zip(parts, scores, strict=True):
+                v = only(mine, v_ref[pl.ds(first, count), cols])
+                total = total + dot_tn((part * share).astype(BF16), v)
+        o_ref[rows, cols] = total.astype(BF16)
+
+
+def forward_kernel(chunks, count, *refs):
+    shards, refs = refs[:count], refs[count:]
+    hidden_h, text_h, refs = refs[0], refs[1], refs[2:]
+    outs, refs = refs[:count], refs[count:]
+    results, refs = refs[:16], refs[16:]
+    sems, refs = refs[:6], refs[6:]
+    (h1, h2, h3, q1, k1, v1, o1, q2, k2, v2, o2, lse1, lse2, x2, x3), refs = refs[:15], refs[15:]
+    gathered_norms, norms, weights, hidden, text, mine, theirs, arrived = refs[:8]
+    norm_sem, weight_sem, load_sem, share_send, share_recv, result_sem = refs[8:]
+    names = dict(norms=0, q=1, k=2, v=3, o=4, ck=5, cv=6, cq=7, co=8, up=9, down=10)
+    turn, finish = gather_engine(chunks, shards, outs, sems)
+    chip, core = lax.axis_index("dp"), lax.axis_index("tensor")
+    frames, width = h1.shape
+    half = frames // 2
+    own = pl.ds(pl.multiple_of(core * half, half), half)
+    loads = [
+        pltpu.make_async_copy(hidden_h, hidden, load_sem.at[0]),
+        pltpu.make_async_copy(text_h, text, load_sem.at[1]),
+    ]
+    for copy in loads:
+        copy.start()
+    pending = []
+
+    def weight_copy(name, slot, first=0):
+        return [
+            pltpu.make_async_copy(
+                outs[names[name]].at[zz, yy, xx, :, pl.ds(first, weights.shape[2])],
+                weights.at[slot, pl.ds(((zz * 2 + yy) * 2 + xx) * rows, rows), :],
+                weight_sem.at[slot, (zz * 2 + yy) * 2 + xx],
+            )
+            for zz in range(4)
+            for yy in range(2)
+            for xx in range(2)
+        ]
+
+    rows = width // 16
+
+    def load_weight(name, slot, first=0):
+        for copy in weight_copy(name, slot, first):
+            copy.start()
+
+    def wait_weight(slot):
+        for copy in weight_copy("q", slot):
+            copy.wait()
+
+    def share(n, src, dst):
+        return pltpu.make_async_remote_copy(
+            src_ref=src,
+            dst_ref=dst,
+            send_sem=share_send.at[n],
+            recv_sem=share_recv.at[n],
+            device_id=(chip, 1 - core),
+            device_id_type=MESH_IDS,
+        )
+
+    def give(n, ref):
+        copy = pltpu.make_async_copy(ref, results[n], result_sem.at[n])
+        copy.start()
+        pending.append(copy)
+
+    def norm_share(n, values, kind, h):
+        step = 64
+
+        def body(i, carry):
+            first = pl.multiple_of(i * step, step)
+            h[pl.ds(pl.multiple_of(core * half + first, step), step), :] = normalize(
+                values(first, step), norms[2 * kind : 2 * kind + 1], norms[2 * kind + 1 : 2 * kind + 2]
+            ).astype(BF16)
+            return carry
+
+        lax.fori_loop(0, half // step, body, 0)
+        share(n, h.at[own], h.at[own]).start()
+
+    def get_share(n, h):
+        share(n, h.at[own], h.at[own]).wait()
+
+    def to(ref):
+        def store(first, value):
+            ref[pl.ds(first, value.shape[0]), :] = value.astype(BF16)
+
+        return store
+
+    def out_project(n, o, slot):
+        step = 256
+        for whose, ref in ((1 - core, theirs.at[n]), (core, mine)):
+            for first in range(0, half, step):
+                part = o[pl.ds(pl.multiple_of(whose * half + first, step), step), :]
+                ref[pl.ds(first, step), :] = dot_nt(part, weights[slot]).astype(ref.dtype)
+            if whose is not core:
+                share(3 + n, theirs.at[n], arrived.at[n]).start()
+
+    def add_stream(n, before, after):
+        def values(first, step):
+            lines = pl.ds(first, step)
+            total = before[lines, :].astype(F32) + (mine[lines, :] + arrived[n, lines, :].astype(F32))
+            after[lines, :] = total
+            return total
+
+        return values
+
+    def work(number):
+        if number == 5:
+            copy = pltpu.make_async_copy(outs[0], gathered_norms, norm_sem)
+            copy.start()
+            copy.wait()
+            for copy in loads:
+                copy.wait()
+            total = 0.0
+            lane = lax.broadcasted_iota(jnp.int32, (128, width), 0)
+            place = lax.broadcasted_iota(jnp.int32, (128, width), 1)
+            for n in range(16):
+                pick = (place == lane + n * rows) & (lane < rows)
+                total = total + dot_nn(
+                    gathered_norms[n // 4, n // 2 % 2, n % 2],
+                    jnp.where(pick, 1.0, 0.0).astype(BF16),
+                )
+            norms[...] = total
+            give(13, norms)
+            norm_share(0, lambda first, step: hidden[pl.ds(first, step), :].astype(F32), 0, h1)
+        if number == 6:
+            load_weight("q", 0)
+            get_share(0, h1)
+            give(0, h1)
+            wait_weight(0)
+            project_rows(h1, weights.at[0], to(q1))
+            give(3, q1)
+        if number == 7:
+            load_weight("k", 1)
+            wait_weight(1)
+            project_rows(h1, weights.at[1], to(k1))
+            give(4, k1)
+        if number == 8:
+            load_weight("v", 0)
+            wait_weight(0)
+            project_rows(h1, weights.at[0], to(v1))
+            give(5, v1)
+        if number in (9, 10, 11):
+            if number == 9:
+                load_weight("o", 1)
+            pairs = q1.shape[1] // 128
+            first = pairs * (number - 9) // 3
+            last = pairs * (number - 8) // 3
+
+            def body(pair, carry):
+                pair_forward(pair, q1, k1, v1, o1, lse1, True)
+                return carry
+
+            lax.fori_loop(first, last, body, 0)
+            if number == 11:
+                load_weight("cv", 0)
+        if number == 12:
+            give(6, o1)
+            give(11, lse1)
+            wait_weight(1)
+            out_project(0, o1, 1)
+            load_weight("ck", 1)
+            wait_weight(0)
+            v2[...] = dot_nn(text[...], weights[0]).astype(BF16)
+            give(9, v2)
+            load_weight("cq", 0)
+        if number == 13:
+            share(3, theirs.at[0], arrived.at[0]).wait()
+            norm_share(1, add_stream(0, hidden, x2), 1, h2)
+            give(14, x2)
+            wait_weight(1)
+            k2[...] = dot_nn(text[...], weights[1]).astype(BF16)
+            give(8, k2)
+            load_weight("co", 1)
+        if number == 14:
+            get_share(1, h2)
+            give(1, h2)
+            wait_weight(0)
+            project_rows(h2, weights.at[0], to(q2))
+            give(7, q2)
+        if number == 15:
+
+            def body(pair, carry):
+                pair_forward(pair, q2, k2, v2, o2, lse2, False)
+                return carry
+
+            lax.fori_loop(0, q2.shape[1] // 128, body, 0)
+            give(10, o2)
+            give(12, lse2)
+        if number == 16:
+            wait_weight(1)
+            out_project(1, o2, 1)
+        if number == 17:
+            share(4, theirs.at[1], arrived.at[1]).wait()
+            norm_share(2, add_stream(1, x2, x3), 2, h3)
+            give(15, x3)
+        if number == 18:
+            get_share(2, h3)
+            give(2, h3)
+
+    for number in range(len(chunks) + 5):
+        turn(number)
+        work(number)
+    finish()
+    for copy in pending:
+        copy.wait()
+
+
+def forward_all(shards, chunks, hidden, text):
     total, count = len(chunks), len(shards)
-    dma = pltpu.SemaphoreType.DMA
-    return pl.pallas_call(
-        functools.partial(gather_kernel, count, chunks),
-        out_shape=[jax.ShapeDtypeStruct((4, 2, 2) + s.shape, s.dtype) for s in shards],
-        in_specs=[pl.BlockSpec(memory_space=pl.ANY)] * count,
-        out_specs=[pl.BlockSpec(memory_space=pl.ANY)] * count,
+    dma, vmem = pltpu.SemaphoreType.DMA, pltpu.VMEM
+    half, width = hidden.shape
+    frames, part = 2 * half, shards[1].shape[1]
+    anywhere = pl.BlockSpec(memory_space=pl.ANY)
+    shape = jax.ShapeDtypeStruct
+    kept = [
+        *[((frames, width), BF16)] * 3,
+        *[((frames, part), BF16)] * 4,
+        ((frames, part), BF16),
+        *[((text.shape[0], part), BF16)] * 2,
+        ((frames, part), BF16),
+        *[((16, frames), F32)] * 2,
+    ]
+    given = [*kept, ((shards[0].shape[0], width), F32), ((half, width), F32), ((half, width), F32)]
+    held = [*kept, ((half, width), F32), ((half, width), F32)]
+    outs = pl.pallas_call(
+        functools.partial(forward_kernel, chunks, count),
+        out_shape=[shape((4, 2, 2) + s.shape, s.dtype) for s in shards] + [shape(*g) for g in given],
+        in_specs=[anywhere] * (count + 2),
+        out_specs=[anywhere] * (count + len(given)),
         scratch_shapes=[
             dma((total,)),
             dma,
@@ -526,17 +823,28 @@
             dma((total, 4)),
             dma((total, 4)),
             dma((total, 4, 2)),
+            *[vmem(*h) for h in held],
+            vmem((4, 2, 2) + shards[0].shape, BF16),
+            vmem((shards[0].shape[0], width), F32),
+            vmem((2, width, part), BF16),
+            vmem((half, width), BF16),
+            vmem(text.shape, BF16),
+            vmem((half, width), F32),
+            vmem((2, half, width), BF16),
+            vmem((2, half, width), BF16),
+            dma,
+            dma((2, 16)),
+            dma((2,)),
+            dma((5,)),
+            dma((5,)),
+            dma((16,)),
         ],
-        compiler_params=pltpu.CompilerParams(collective_id=0, has_side_effects=True),
-        name="gather_weights",
-    )(*shards)
-
-
-def total_of(*parts):
-    value = parts[0].astype(F32)
-    for part in parts[1:]:
-        value = value + part.astype(F32)
-    return value
+        compiler_params=pltpu.CompilerParams(
+            collective_id=0, has_side_effects=True, vmem_limit_bytes=VMEM_LIMIT
+        ),
+        name="forward",
+    )(*shards, hidden, text)
+    return outs[:count], outs[count:]
 
 
 XD, YD, XA, YA, XB, YB, UP, DOWN = range(8)
@@ -550,18 +858,6 @@
 TEXT_UNITS = (30, 36)
 SELF_UNITS = (39, 48)
 UNITS = 48
-
-
-def dot_nt(left, right):
-    return lax.dot_general(left, right, (((1,), (1,)), ((), ())), preferred_element_type=F32)
-
-
-def dot_tn(left, right):
-    return lax.dot_general(left, right, (((0,), (0,)), ((), ())), preferred_element_type=F32)
-
-
-def dot_nn(left, right):
-    return jnp.dot(left, right, preferred_element_type=F32)
 
 
 def head_back(head, q_ref, k_ref, v_ref, do_ref, lse_ref, dqkv, acc_k, acc_v):
@@ -1100,40 +1396,33 @@
     cotangent,
 ):
     width = norm1_gain.shape[0] * 16
-    norms = jnp.stack([norm1_gain, norm1_bias, norm2_gain, norm2_bias, norm3_gain, norm3_bias], axis=1)
-    norms = jnp.pad(norms, ((0, 0), (0, 122)))
+    norms = jnp.stack([norm1_gain, norm1_bias, norm2_gain, norm2_bias, norm3_gain, norm3_bias])
+    norms = jnp.pad(norms, ((0, 26), (0, 128 - norms.shape[1])))
     shards = (
         norms,
         self_query.T,
         self_key.T,
         self_value.T,
         self_out,
-        cross_query.T,
         cross_key.T,
         cross_value.T,
+        cross_query.T,
         cross_out,
         hidden_up.T,
-    )
-    w_down = lax.all_gather(hidden_down, "dp", axis=0, tiled=True)
-    gathered = gather_all(shards, gather_plan([s.shape[1] for s in shards]))
-    gathered = [g.reshape(width, g.shape[-1]) for g in gathered]
-    norms = gathered[0][:, :6].T.astype(jnp.float32)
-    gain_self, bias_self, gain_cross, bias_cross, gain_ffn, bias_ffn = [norms[i] for i in range(6)]
-    w_q, w_k, w_v, w_o, w_cq, w_ck, w_cv, w_co, w_up = gathered[1:]
-    stream_one = hidden_in.astype(jnp.float32)
-    key_two = split_heads(project_t(text_states, w_ck).astype(jnp.bfloat16))
-    value_two = split_heads(project_t(text_states, w_cv).astype(jnp.bfloat16))
-    normed_one = share_rows(layer_norm(stream_one, gain_self, bias_self).astype(jnp.bfloat16))
-    query_one = split_heads(project_t(normed_one, w_q).astype(jnp.bfloat16))
-    key_one = split_heads(project_t(normed_one, w_k).astype(jnp.bfloat16))
-    value_one = split_heads(project_t(normed_one, w_v).astype(jnp.bfloat16))
-    attended_one, logsum_one = attend(query_one, key_one, value_one, True)
-    stream_two = stream_one + sum_rows([flatten_heads(attended_one)], lambda r: project(r, w_o))
-    normed_two = share_rows(layer_norm(stream_two, gain_cross, bias_cross).astype(jnp.bfloat16))
-    query_two = split_heads(project_t(normed_two, w_cq).astype(jnp.bfloat16))
-    attended_two, logsum_two = attend(query_two, key_two, value_two, False)
-    stream_three = stream_two + sum_rows([flatten_heads(attended_two)], lambda r: project(r, w_co))
-    normed_three = share_rows(layer_norm(stream_three, gain_ffn, bias_ffn).astype(jnp.bfloat16))
+        hidden_down,
+    )
+    gathered, kept = forward_all(
+        shards, gather_plan([s.shape[1] for s in shards]), hidden_in[0], text_states[0]
+    )
+    w_q, w_k, w_v, w_o, w_ck, w_cv, w_cq, w_co, w_up, w_down = [
+        g.reshape(width, g.shape[-1]) for g in gathered[1:]
+    ]
+    normed_one, normed_two, normed_three = [k[None] for k in kept[:3]]
+    query_one, key_one, value_one, attended_one = kept[3:7]
+    query_two, key_two, value_two, attended_two = [split_heads(k[None]) for k in kept[7:11]]
+    logsum_one, logsum_two = kept[11], kept[12][None, :12]
+    gain_self, bias_self, gain_cross, bias_cross, gain_ffn, bias_ffn = [kept[13][i] for i in range(6)]
+    stream_one, stream_two, stream_three = hidden_in.astype(F32), kept[14][None], kept[15][None]
     upper = project_t(normed_three, w_up)
     active, slope = gelu_parts(upper)
     layer_out = (stream_three + sum_rows([active], lambda r: project(r, w_down))).astype(jnp.bfloat16)
@@ -1187,13 +1476,13 @@
                 grad_upper,
                 flatten_heads(attended_two),
                 grad_query_two,
-                flatten_heads(attended_one),
+                attended_one[None],
             )
         ],
         text_states[0],
         jnp.concatenate([grad_key[0], grad_value[0]], axis=1),
-        [flatten_heads(query_one)[0], flatten_heads(key_one)[0], flatten_heads(value_one)[0], grad_attended[0]],
-        jnp.pad(logsum_one[0], ((0, 4), (0, 0))),
+        [query_one, key_one, value_one, grad_attended[0]],
+        logsum_one,
     )
     grad_query, grad_key, grad_value = [
         grad_heads[None, :, n * part : (n + 1) * part] for n in range(3)

time: 853 us -> 764 us (0.90)
  matrix products: 171 us -> 112 us
  Pallas kernels: 529 us -> 577 us
  other arithmetic: 63.1 us -> 32.9 us
  local copies, waits for them, and re-layouts: 55.6 us -> 30.1 us
  between operations: 15.7 us -> 1.48 us
  waiting for transfers between devices: 9.91 us -> 0.02 us
    pallas_call x1, Pallas kernels: 226 us -> 274 us  [forward_all(): pl.pallas_call(functools.partial(forward_kernel, chunks, count), out_shap...]
    dot_general x7 -> x1, matrix products: 38 us -> 16.4 us  [project_t(): jnp.einsum('cli,io->clo', row_data, weight, preferred_element_type=jnp.fl...]
    dot_general x4 -> x0, matrix products: 16.9 us -> none  [attend(): jnp.einsum('chqk,ckhe->cqhe', soft_weights, val_rows[:, :key_end], prefer...]
    unnamed x213 -> x100, local copies, waits for them, and re-layouts: 24.3 us -> 7.83 us
    reduce_sum x4 -> x0, other arithmetic: 15.5 us -> none  [attend(): row_total = jnp.sum(exp_scores, axis=-1, keepdims=True)]
    dot_general x4 -> x2, matrix products: 14.9 us -> 1.09 us  [block_scores(): jnp.einsum('cqhe,ckhe->chqk', queries[:, first_row:first_row + block_rows...]
    dot_general x6 -> x2, matrix products: 30 us -> 20 us  [project(): jnp.einsum('cli,oi->clo', row_data, weight, preferred_element_type=jnp.fl...]
    ppermute x13 -> x8, waiting for transfers between devices: 9.9 us -> 0.02 us  [other_core(): return lax.ppermute(values, 'tensor', [(0, 1), (1, 0)])]
  transfers between devices with their start and end apart: 14 -> 8, of which waited for: 4 -> 0; matrix products, arithmetic and copies ran while one was open for 22% -> 13% of each run, Pallas kernels for 0% -> 36%
where the time goes in v3:
time: 764 us; the launch traced here: 756 us
  Pallas kernels  577 us (76%)
  matrix products  112 us (15%)
  other arithmetic  32.9 us (4%)
  local copies, waits for them, and re-layouts  30.1 us (4%)
    pallas_call x1, Pallas kernels, backward_all(): pl.pallas_call(backward_kernel, out_shape=[jax.ShapeDtypeStruct((rows, UN...  287 us
    pallas_call x1, Pallas kernels, forward_all(): pl.pallas_call(functools.partial(forward_kernel, chunks, count), out_shap...  274 us
    dot_general x12, matrix products, input_grad_t(): jnp.einsum('cla,ia->cli', grad_rows, weight, preferred_element_type=jnp.f...  43.6 us
    dot_general x2, matrix products, project(): jnp.einsum('cli,oi->clo', row_data, weight, preferred_element_type=jnp.fl...  20 us
    dot_general x1, matrix products, local_fast(): jnp.einsum('clo,of->clf', grad_branch, w_down, preferred_element_type=jnp...  18.8 us
    dot_general x1, matrix products, project_t(): jnp.einsum('cli,io->clo', row_data, weight, preferred_element_type=jnp.fl...  16.4 us
    pallas_call x1, Pallas kernels, sum_everywhere(): pl.pallas_call(sum_everywhere_kernel, out_shape=jax.ShapeDtypeStruct(valu...  15.8 us
  transfers between devices with their start and end apart: 8, of which 0 were waited for; matrix products, arithmetic and copies ran while one was open for 13% of the time, Pallas kernels for 36%

profile of v3, /device:TPU:0, one launch (start us, length us, event | category | flops | bytes accessed | tf_op | source)
XLA Modules:
  0.0 756.1 jit_solution(6891536915889000754)
XLA Ops:
  2.5 274.2 %forward.1 = (bf16[4,2,2,32,128]{4,3,2,1,0:T(8,128)(2,1)}, bf16[4,2,2,96,768]{4,3,2,1,0:T(8,128)(2,1)}, bf16[4,2,2,96,768]{4,3,2,1,0:T(8,128)(2,1)}, bf16[4,2,2,...) custom-call(bf16[32,128]{1,0:T(8,128)(2,1)} %pad.20.refs_0_, ...), custom_call_target="tpu_custom_call" | custom-call | tf_op jit(solution)/shard_map/forward/pallas_call | solution.py:814
  276.8 16.4 %multiply_convert_fusion.1 = (bf16[1024,3072]{1,0:T(8,128)(2,1)S(1)}, f32[1024,3072]{1,0:T(8,128)}) fusion(bf16[1024,1536]{1,0:T(8,128)(2,1)} %get-tuple-element.128.refs_1_, bf16[1536,3072]{1,0:T(8,128)(2,1)} %bitcast.239), kind=kOutput, calls=%fused_computation.7 | convolution fusion | flops 9679405056 | bytes 31457280 | tf_op jit(solution)/shard_map/cli,io->clo/dot_general | solution.py:1333
  293.4 1.3 copy-done.20
  295.2 18.8 %multiply_convert_fusion.refs_7_ = bf16[1024,3072]{1,0:T(8,128)(2,1)S(1)} fusion(bf16[1536,3072]{1,0:T(8,128)(2,1)} %bitcast.236, f32[1024,3072]{1,0:T(8,128)} %get-tuple-element.203, bf16[1,512,1536]{2,1,0:T(8,128)(2,1)S(1)} %get-tuple-element.191, bf16[1,512,1536]{2,1,0:T(8,128)(2,1)S(1)} %get-tuple-element.190), kind=kOutput, calls=%fused_computation.6 | convolution fusion | flops 9707716608 | bytes 31457280 | tf_op jit(solution)/shard_map/clo,of->clf/dot_general | solution.py:1432
  314.0 11.2 %fusion.36 = bf16[1,512,1536]{2,1,0:T(8,128)(2,1)} fusion(bf16[1536,3072]{1,0:T(8,128)(2,1)} %bitcast.240, bf16[1024,3072]{1,0:T(8,128)(2,1)S(1)} %multiply_convert_fusion.refs_7_, s32[]{:T(128)S(6)} %select_n.54), kind=kOutput, calls=%fused_computation.62 | convolution fusion | flops 4832624640 | bytes 14155780 | tf_op jit(solution)/shard_map/cla,ia->cli/dot_general | solution.py:1337
  325.3 9.0 %fusion.39 = bf16[1,512,1536]{2,1,0:T(8,128)(2,1)} fusion(bf16[1536,3072]{1,0:T(8,128)(2,1)} %bitcast.237, bf16[1024,3072]{1,0:T(8,128)(2,1)S(1)} %get-tuple-element.202.refs_6_, s32[]{:T(128)S(6)} %select_n.54), kind=kOutput, calls=%fused_computation.63 | convolution fusion | flops 4832624640 | bytes 14155780 | tf_op jit(solution)/shard_map/cli,oi->clo/dot_general | solution.py:29
  334.7 2.4 reduce_sum.175
  337.3 1.0 slice_reduce_fusion
  338.4 2.3 multiply_reduce_fusion.1
  340.8 11.8 %fusion.14 = (f32[1536]{0:T(1024)}, f32[512]{0:T(512)S(1)}, f32[1536]{0:T(1024)}, f32[1,512,1536]{2,1,0:T(8,128)S(1)}) fusion(f32[512,1536]{1,0:T(8,128)S(1)} %copy-done.2, f32[512]{0:T(512)S(1)} %fusion.87, f32[512]{0:T(512)S(1)} %broadcast_multiply_fusion.2, f32[1536]{0:T(1024)S(1)} %get-tuple-element.168, ...), kind=kOutput, calls=%fused_computation.35 | convolution fusion | flops 4839698944 | bytes 20471812 | tf_op jit(solution)/shard_map/cla,ia->cli/dot_general | solution.py:1337
  352.6 0.9 fusion.94
  354.0 1.6 fusion.44
  356.4 0.9 reshape.671
  357.2 2.6 copy.49
  360.0 0.9 copy.52
  360.9 2.5 multiply_reduce_fusion
  363.8 1.9 maximum_bitcast_fusion.refs_0_
  365.6 2.2 broadcast_select_fusion.3
  368.3 2.8 convolution_convert_fusion.2
  375.0 1.1 copy-done.46
  376.1 2.7 fusion.42
  378.8 11.0 %fusion.18 = bf16[1,512,1536]{2,1,0:T(8,128)(2,1)} fusion(f32[512,1536]{1,0:T(8,128)S(1)} %copy-done.4, bf16[1,512,1536]{2,1,0:T(8,128)(2,1)} %collective-permute-done, bf16[1536,3072]{1,0:T(8,128)(2,1)} %bitcast.238, bf16[1024,3072]{1,0:T(8,128)(2,1)} %copy-done.25, s32[]{:T(128)S(6)} %select_n.53), kind=kOutput, calls=%fused_computation.43 | convolution fusion | flops 4834983936 | bytes 18874372 | tf_op jit(solution)/shard_map/cli,oi->clo/dot_general | solution.py:29
  391.4 1.1 fusion.63
  392.5 5.2 fusion.15
  397.7 1.0 fusion.93
  399.2 1.9 fusion.91
  402.6 2.1 fusion.46
  405.5 2.6 fusion.98
  408.1 0.9 convolution_add_fusion.4
  411.1 2.6 copy.58.refs_9_
  413.7 1.6 bitcast_add_fusion.1
  416.8 2.2 broadcast_select_fusion.1
  419.6 2.9 maximum_bitcast_fusion.1
  422.5 4.6 convolution_convert_fusion.1.refs_16_
  427.1 287.0 %backward.1 = (f32[96,12288]{1,0:T(8,128)}, bf16[1024,2304]{1,0:T(8,128)(2,1)}) custom-call(bf16[1024,1536]{1,0:T(8,128)(2,1)} %maximum_bitcast_fusion.refs_0_, bf16[1024,1536]{1,0:T(8,128)(2,1)} %get-tuple-element.128.refs_1_, bf16[1024,1536]{1,0:T(8,128)(2,1)} %get-tuple-element.211.refs_2_, bf16[1024,1536]{1,0:T(8,128)(2,1)} %get-tuple-element.139.refs_3_, ...), custom_call_target="tpu_custom_call" | custom-call | tf_op jit(solution)/shard_map/backward/pallas_call | solution.py:1251
  714.1 2.8 fusion.97
  717.2 1.4 fusion.54
  718.9 1.4 convolution_add_fusion.1
  720.8 1.4 fusion.43
  722.3 1.4 fusion.96
  723.8 1.4 fusion.60
  725.2 1.4 convolution_add_fusion.3
  726.6 1.6 fusion.95
  728.6 2.1 fusion.92
  730.7 1.3 fusion.13
  733.1 15.8 %sum_norm_gradients.1 = f32[8,1536]{1,0:T(8,128)} custom-call(f32[8,1536]{1,0:T(8,128)} %pad.21.values), custom_call_target="tpu_custom_call" | custom-call | tf_op jit(solution)/shard_map/sum_norm_gradients/pallas_call | solution.py:1321
  748.9 0.8 constant_dynamic-slice_fusion
  750.2 5.7 add_add_fusion.3
  (158 shorter events, 20.8 us)
Async XLA Ops:
  0.7 292.5 %collective-permute-start.1 = (bf16[1,512,1536]{2,1,0:T(8,128)(2,1)}, bf16[1,512,1536]{2,1,0:T(8,128)(2,1)S(1)}, u32[]{:S(2)}, u32[]{:S(2)}) collective-permute-start(bf16[1,512,1536]{2,1,0:T(8,128)(2,1)} %param.53), channel_id=1, source_target_pairs={{0,1},{1,0},{2,3},{3,2},{4,5},{5,4},{6,7},{7,6},{8,9},{9,8},{10,11... | collective-permute-start | bytes 4718600 | tf_op jit(solution)/shard_map/ppermute | solution.py:1341
  276.8 16.4 %copy-start.8 = (bf16[1,512,1536]{2,1,0:T(8,128)(2,1)S(1)}, bf16[1,512,1536]{2,1,0:T(8,128)(2,1)}, u32[]{:S(2)}) copy-start(bf16[1,512,1536]{2,1,0:T(8,128)(2,1)} %param.53) | copy-start | bytes 4718596
  293.1 32.1 %copy-start.25 = (bf16[1024,3072]{1,0:T(8,128)(2,1)}, bf16[1024,3072]{1,0:T(8,128)(2,1)S(1)}, u32[]{:S(2)}) copy-start(bf16[1024,3072]{1,0:T(8,128)(2,1)S(1)} %get-tuple-element.202.refs_6_) | copy-start | bytes 18874372
  293.4 1.8 copy-start.22
  314.0 11.2 %copy-start.26 = (bf16[1024,3072]{1,0:T(8,128)(2,1)}, bf16[1024,3072]{1,0:T(8,128)(2,1)S(1)}, u32[]{:S(2)}) copy-start(bf16[1024,3072]{1,0:T(8,128)(2,1)S(1)} %multiply_convert_fusion.refs_7_) | copy-start | bytes 18874372
  325.3 15.5 %collective-permute-start.2 = (bf16[1,512,1536]{2,1,0:T(8,128)(2,1)}, bf16[1,512,1536]{2,1,0:T(8,128)(2,1)}, u32[]{:S(2)}, u32[]{:S(2)}) collective-permute-start(bf16[1,512,1536]{2,1,0:T(8,128)(2,1)} %fusion.36), channel_id=1, source_target_pairs={{0,1},{1,0},{2,3},{3,2},{4,5},{5,4},{6,7},{7,6},{8,9},{9,8},{10,11... | collective-permute-start | bytes 4718600 | tf_op jit(solution)/shard_map/ppermute | solution.py:1341
  334.2 2.9 copy-start
  334.2 44.6 %collective-permute-start = (bf16[1,512,1536]{2,1,0:T(8,128)(2,1)}, bf16[1,512,1536]{2,1,0:T(8,128)(2,1)}, u32[]{:S(2)}, u32[]{:S(2)}) collective-permute-start(bf16[1,512,1536]{2,1,0:T(8,128)(2,1)} %fusion.39), channel_id=1, source_target_pairs={{0,1},{1,0},{2,3},{3,2},{4,5},{5,4},{6,7},{7,6},{8,9},{9,8},{10,11... | collective-permute-start | bytes 4718600 | tf_op jit(solution)/shard_map/ppermute | solution.py:1341
  337.3 3.4 copy-start.2
  340.7 11.8 %copy-start.3 = (f32[512,1536]{1,0:T(8,128)S(1)}, f32[512,1536]{1,0:T(8,128)}, u32[]{:S(2)}) copy-start(f32[512,1536]{1,0:T(8,128)} %get-tuple-element.127) | copy-start | bytes 9437188
  354.0 2.1 copy-start.6
  354.0 2.4 copy-start.35
  355.6 4.3 copy-start.34
  355.6 10.1 %collective-permute-start.3 = (bf16[1,512,1536]{2,1,0:T(8,128)(2,1)}, bf16[1,512,1536]{2,1,0:T(8,128)(2,1)}, u32[]{:S(2)}, u32[]{:S(2)}) collective-permute-start(bf16[1,512,1536]{2,1,0:T(8,128)(2,1)} %fusion.44), channel_id=1, source_target_pairs={{0,1},{1,0},{2,3},{3,2},{4,5},{5,4},{6,7},{7,6},{8,9},{9,8},{10,11... | collective-permute-start | bytes 4718600 | tf_op jit(solution)/shard_map/ppermute | solution.py:1341
  360.0 3.4 copy-start.36
  360.9 2.6 copy-start.21
  360.9 2.8 copy-start.23
  365.6 2.6 copy-start.47
  367.9 3.1 copy-start.15
  367.9 3.1 copy-start.17
  368.2 2.8 copy-start.29
  368.2 3.2 copy-start.11
  371.0 20.4 %copy-start.24 = (bf16[1024,768]{0,1:T(8,128)(2,1)}, bf16[1024,768]{0,1:T(8,128)(2,1)S(1)}, u32[]{:S(2)}) copy-start(bf16[1024,768]{0,1:T(8,128)(2,1)S(1)} %convolution_convert_fusion.2) | copy-start | bytes 4718596
  374.2 1.9 copy-start.46
  375.0 17.6 %copy-start.19 = (bf16[1,1024,12,64]{1,3,2,0:T(8,128)(2,1)}, bf16[1,1024,12,64]{1,3,2,0:T(8,128)(2,1)S(1)}, u32[]{:S(2)}) copy-start(bf16[1,1024,12,64]{1,3,2,0:T(8,128)(2,1)S(1)} %maximum_convert_fusion) | copy-start | bytes 4718596
  376.1 2.7 copy-start.4
  378.8 11.1 %copy-start.42 = (f32[1536]{0:T(1024)S(1)}, f32[1536]{0:T(1024)}, u32[]{:S(2)}) copy-start(f32[1536]{0:T(1024)} %get-tuple-element.155) | copy-start | bytes 18436
  378.8 11.7 %copy-start.41 = (f32[1536]{0:T(1024)S(1)}, f32[1536]{0:T(1024)}, u32[]{:S(2)}) copy-start(f32[1536]{0:T(1024)} %get-tuple-element.161) | copy-start | bytes 18436
  378.8 13.8 %collective-permute-start.4 = (bf16[1,512,1536]{2,1,0:T(8,128)(2,1)}, bf16[1,512,1536]{2,1,0:T(8,128)(2,1)}, u32[]{:S(2)}, u32[]{:S(2)}) collective-permute-start(bf16[1,512,1536]{2,1,0:T(8,128)(2,1)} %fusion.42), channel_id=1, source_target_pairs={{0,1},{1,0},{2,3},{3,2},{4,5},{5,4},{6,7},{7,6},{8,9},{9,8},{10,11... | collective-permute-start | bytes 4718600 | tf_op jit(solution)/shard_map/ppermute | solution.py:1341
  389.8 2.7 copy-start.1
  398.7 2.3 copy-start.5
  398.8 2.3 copy-start.39
  401.0 15.7 %collective-permute-start.5 = (bf16[1,512,1536]{2,1,0:T(8,128)(2,1)}, bf16[1,512,1536]{2,1,0:T(8,128)(2,1)}, u32[]{:S(2)}, u32[]{:S(2)}) collective-permute-start(bf16[1,512,1536]{2,1,0:T(8,128)(2,1)} %fusion.91), channel_id=1, source_target_pairs={{0,1},{1,0},{2,3},{3,2},{4,5},{5,4},{6,7},{7,6},{8,9},{9,8},{10,11... | collective-permute-start | bytes 4718600 | tf_op jit(solution)/shard_map/ppermute | solution.py:1341
  405.5 2.7 copy-start.27
  405.5 5.0 copy-start.32
  405.5 5.0 copy-start.33
  410.4 3.3 copy-start.31
  410.4 3.3 collective-permute-start.7
  416.7 2.4 copy-start.16
  416.7 2.8 copy-start.18
  419.6 2.9 copy-start.45
  714.1 3.1 copy-start.44
  717.2 5.1 slice-start
  718.9 1.9 copy-start.43
  718.9 3.4 slice-start.1
  722.2 6.0 collective-permute-start.6
  726.6 2.0 copy-start.7
  730.7 19.5 %copy-start.40 = (f32[512]{0:T(512)S(1)}, f32[512]{0:T(512)}, u32[]{:S(2)}) copy-start(f32[512]{0:T(512)} %copy-done.39) | copy-start | bytes 6148
  (10 other events, 13.9 us)

commit v4 on v3

--- a/solution.py
+++ b/solution.py
@@ -360,7 +360,7 @@
 MESH_IDS = pl.DeviceIdType.MESH
 BF16 = jnp.bfloat16
 F32 = jnp.float32
-VMEM_LIMIT = 60 * 2**20
+VMEM_LIMIT = 63 * 2**20
 
 
 def my_place():
@@ -594,13 +594,13 @@
 
 def forward_kernel(chunks, count, *refs):
     shards, refs = refs[:count], refs[count:]
-    hidden_h, text_h, refs = refs[0], refs[1], refs[2:]
+    hidden_h, text_h, cotangent_h, refs = refs[0], refs[1], refs[2], refs[3:]
     outs, refs = refs[:count], refs[count:]
-    results, refs = refs[:16], refs[16:]
+    results, refs = refs[:19], refs[19:]
     sems, refs = refs[:6], refs[6:]
     (h1, h2, h3, q1, k1, v1, o1, q2, k2, v2, o2, lse1, lse2, x2, x3), refs = refs[:15], refs[15:]
-    gathered_norms, norms, weights, hidden, text, mine, theirs, arrived = refs[:8]
-    norm_sem, weight_sem, load_sem, share_send, share_recv, result_sem = refs[8:]
+    gathered_norms, norms, weights, hidden, text, mine, theirs, arrived, active, slopes = refs[:10]
+    norm_sem, weight_sem, load_sem, share_send, share_recv, result_sem = refs[10:]
     names = dict(norms=0, q=1, k=2, v=3, o=4, ck=5, cv=6, cq=7, co=8, up=9, down=10)
     turn, finish = gather_engine(chunks, shards, outs, sems)
     chip, core = lax.axis_index("dp"), lax.axis_index("tensor")
@@ -692,7 +692,39 @@
 
         return values
 
+    branch = results[16].at[own]
+    branch_copy = pltpu.make_async_copy(cotangent_h, branch, result_sem.at[16])
+
+    def active_copies(j):
+        lanes = pl.ds(j * active.shape[1], active.shape[1])
+        return (
+            pltpu.make_async_copy(active, results[17].at[:, lanes], result_sem.at[17]),
+            pltpu.make_async_copy(slopes, results[18].at[:, lanes], result_sem.at[18]),
+        )
+
+    def hidden_units(j):
+        wait_weight(j % 2)
+        if j < 3:
+            load_weight("up", (j + 1) % 2, (j + 1) * active.shape[1])
+        if j:
+            for copy in active_copies(j - 1):
+                copy.wait()
+
+        def store(first, value):
+            lines = pl.ds(first, value.shape[0])
+            below = 0.5 * (1.0 + lax.erf(value * (0.5**0.5)))
+            density = jnp.exp(-0.5 * value * value) * 0.3989422804014327
+            active[lines, :] = (value * below).astype(BF16)
+            slopes[lines, :] = (below + value * density).astype(BF16)
+
+        project_rows(h3, weights.at[j % 2], store)
+        for copy in active_copies(j):
+            copy.start()
+
     def work(number):
+        if number == 0:
+            share(5, cotangent_h, branch).start()
+            branch_copy.start()
         if number == 5:
             copy = pltpu.make_async_copy(outs[0], gathered_norms, norm_sem)
             copy.start()
@@ -782,19 +814,24 @@
             share(4, theirs.at[1], arrived.at[1]).wait()
             norm_share(2, add_stream(1, x2, x3), 2, h3)
             give(15, x3)
+            load_weight("up", 0)
         if number == 18:
             get_share(2, h3)
             give(2, h3)
+            share(5, cotangent_h, branch).wait()
+            branch_copy.wait()
+        if 18 <= number < 22:
+            hidden_units(number - 18)
 
     for number in range(len(chunks) + 5):
         turn(number)
         work(number)
     finish()
-    for copy in pending:
+    for copy in (*pending, *active_copies(3)):
         copy.wait()
 
 
-def forward_all(shards, chunks, hidden, text):
+def forward_all(shards, chunks, hidden, text, cotangent):
     total, count = len(chunks), len(shards)
     dma, vmem = pltpu.SemaphoreType.DMA, pltpu.VMEM
     half, width = hidden.shape
@@ -810,11 +847,12 @@
         *[((16, frames), F32)] * 2,
     ]
     given = [*kept, ((shards[0].shape[0], width), F32), ((half, width), F32), ((half, width), F32)]
+    given += [((frames, width), BF16), ((frames, 4 * part), BF16), ((frames, 4 * part), BF16)]
     held = [*kept, ((half, width), F32), ((half, width), F32)]
     outs = pl.pallas_call(
         functools.partial(forward_kernel, chunks, count),
         out_shape=[shape((4, 2, 2) + s.shape, s.dtype) for s in shards] + [shape(*g) for g in given],
-        in_specs=[anywhere] * (count + 2),
+        in_specs=[anywhere] * (count + 3),
         out_specs=[anywhere] * (count + len(given)),
         scratch_shapes=[
             dma((total,)),
@@ -832,18 +870,20 @@
             vmem((half, width), F32),
             vmem((2, half, width), BF16),
             vmem((2, half, width), BF16),
+            vmem((frames, part), BF16),
+            vmem((frames, part), BF16),
             dma,
             dma((2, 16)),
             dma((2,)),
-            dma((5,)),
-            dma((5,)),
-            dma((16,)),
+            dma((6,)),
+            dma((6,)),
+            dma((19,)),
         ],
         compiler_params=pltpu.CompilerParams(
             collective_id=0, has_side_effects=True, vmem_limit_bytes=VMEM_LIMIT
         ),
         name="forward",
-    )(*shards, hidden, text)
+    )(*shards, hidden, text, cotangent)
     return outs[:count], outs[count:]
 
 
@@ -851,40 +891,41 @@
 
 
 UNIT = 256
-WIDTH_Z, WIDTH_A, SLOTS = 384, 128, 8
+WIDTH_Z, WIDTH_A, SLOTS = 384, 128, 7
 ROWS_L = 6
 FIRST_L = (0, 12, 24, 27, 36, 39)
+LOAD_L = ((2, 10), (3, 11), (4, 14), (5, 15))
 FIRST_R = ((0, 12), (12, 24), (24, 27), (27, 30), (36, 39))
 TEXT_UNITS = (30, 36)
 SELF_UNITS = (39, 48)
 UNITS = 48
 
 
-def head_back(head, q_ref, k_ref, v_ref, do_ref, lse_ref, dqkv, acc_k, acc_v):
-    width = q_ref.shape[1]
+def head_back(head, q_ref, k_ref, v_ref, do_ref, lse_ref, dq_ref, dkv_ref, bases, acc_k, acc_v, causal):
     pair, half = lax.div(head, 2), lax.rem(head, 2)
-    lanes = [pl.ds(pl.multiple_of(pair * 128 + n * width, 128), 128) for n in range(3)]
-    cols = lanes[0]
-    mine = lax.div(lax.broadcasted_iota(jnp.int32, (1, 128), 1), 64) == half
-    acc_k[...] = jnp.zeros_like(acc_k)
-    acc_v[...] = jnp.zeros_like(acc_v)
+    cols = pl.ds(pl.multiple_of(pair * 128, 128), 128)
+    lanes = [pl.ds(pl.multiple_of(pair * 128 + base, 128), 128) for base in bases]
+    mine = head_lanes(half)
+    length = k_ref.shape[0]
+    acc_k[pl.ds(0, length), :] = jnp.zeros((length, 128), F32)
+    acc_v[pl.ds(0, length), :] = jnp.zeros((length, 128), F32)
     block = 256
     keep = lax.broadcasted_iota(jnp.int32, (block, block), 0) <= lax.broadcasted_iota(
         jnp.int32, (block, block), 1
     )
 
-    def merged(rows, lane, value):
-        before = jnp.where(half == 0, 0.0, dqkv[rows, lane].astype(F32))
-        dqkv[rows, lane] = (before + value).astype(BF16)
+    def merged(ref, rows, lane, value):
+        before = jnp.where(half == 0, 0.0, ref[rows, lane].astype(F32))
+        ref[rows, lane] = (before + value).astype(BF16)
 
     for i in range(q_ref.shape[0] // block):
         rows = pl.ds(i * block, block)
-        q = jnp.where(mine, q_ref[rows, cols].astype(F32), 0.0).astype(BF16)
-        do = jnp.where(mine, do_ref[rows, cols].astype(F32), 0.0).astype(BF16)
+        q = only(mine, q_ref[rows, cols])
+        do = only(mine, do_ref[rows, cols])
         lse = lse_ref[pl.ds(head, 1), rows]
-        parts = [(i * block, block, True)]
-        if i:
-            parts.insert(0, (0, i * block, False))
+        parts = [(0, length, False)]
+        if causal:
+            parts = [(0, i * block, False)] * (i > 0) + [(i * block, block, True)]
         held, inner = [], 0.0
         for first, count, diagonal in parts:
             keys = pl.ds(first, count)
@@ -900,32 +941,47 @@
             acc_v[keys, :] += dot_nn(soft.astype(BF16), do)
             acc_k[keys, :] += dot_nn(ds, q)
             grad_q = grad_q + dot_tn(ds, k_ref[keys, cols])
-        merged(rows, lanes[0], jnp.where(mine, grad_q * score_scale, 0.0))
-    merged(slice(None), lanes[1], acc_k[...] * score_scale)
-    merged(slice(None), lanes[2], acc_v[...])
+        merged(dq_ref, rows, lanes[0], jnp.where(mine, grad_q * score_scale, 0.0))
+    everything = pl.ds(0, length)
+    merged(dkv_ref, everything, lanes[1], acc_k[everything, :] * score_scale)
+    merged(dkv_ref, everything, lanes[2], acc_v[everything, :])
 
 
 def backward_kernel(*refs):
-    lefts, refs = refs[:ROWS_L], refs[ROWS_L:]
-    rights, refs = refs[:5], refs[5:]
-    text_h, dkv_h, q_h, k_h, v_h, do_h, lse_ref, out, dqkv_h = refs[:9]
-    refs = refs[9:]
-    gz, ga, xdz, ydz, xaz, yaz, xbz, ybz, upz, dnz = refs[:10]
-    xda, yda, xaa, yaa, xba, yba, upa, dna, oz, oa = refs[10:20]
-    lbuf, rbuf, text_v, dkv_v, q_v, k_v, v_v, do_v, dqkv, acc_k, acc_v = refs[20:31]
-    first_sem, l_sem, r_sem, dqkv_sem, out_sem, send_z, send_a, recv_z, recv_a, credit = refs[31:]
+    (e3_h, h3_h, h2_h, h1_h, a_h, slope_h, o2_h, o1_h, text_h), refs = refs[:9], refs[9:]
+    (q2_h, k2_h, v2_h, q1_h, k1_h, v1_h, x3_h, x2_h, x1_h), refs = refs[:9], refs[9:]
+    (w_q, w_k, w_v, w_o, w_ck, w_cv, w_cq, w_co, w_up, w_down), refs = refs[:10], refs[10:]
+    (lse2_ref, lse1_ref, norms), refs = refs[:3], refs[3:]
+    (out, layer_out, grad_input, grad_text, norm_out), refs = refs[:5], refs[5:]
+    (du_h, dq2_h, e2_h, e1_h), refs = refs[:4], refs[4:]
+    (gz, ga, xdz, ydz, xaz, yaz, xbz, ybz, lnz), refs = refs[:9], refs[9:]
+    (xda, yda, xaa, yaa, xba, yba, lna, oz, oa), refs = refs[:9], refs[9:]
+    (lbuf, rbuf, text_v, dkv_v, k2_v, v2_v, pool, dqkv, acc_k, acc_v), refs = refs[:10], refs[10:]
+    (acc, grad, xbuf, theirs, arrived, weights, text_part, text_send, text_got), refs = refs[:9], refs[9:]
+    (norm_grads, got), refs = refs[:2], refs[2:]
+    (first_sem, l_sem, r_sem, out_sem, send_z, send_a, recv_z, recv_a), refs = refs[:8], refs[8:]
+    (pool_sem, slope_sem, weight_sem, x_sem, keep_sem, share_send, share_recv, norm_send), refs = refs[:8], refs[8:]
+    norm_recv, credit = refs
+    lefts = (e3_h, h3_h, e2_h, h2_h, e1_h, h1_h)
+    rights = (a_h, du_h, o2_h, dq2_h, o1_h)
     width_z, width_a, slots = WIDTH_Z, WIDTH_A, SLOTS
     total, width = UNITS // 2, WIDTH_Z + WIDTH_A
-    heads = q_v.shape[1] // HEAD_DIM
     x, y, z, core = my_place()
     xn, yn = 1 - x, 1 - y
     near = neighbours(x, y, z, core)
     right, across, up, down = near
     has_up, has_down = z < 3, z > 0
     degree = 2 + has_up.astype(jnp.int32) + has_down.astype(jnp.int32)
+    chip = lax.axis_index("dp")
+    other = (chip, 1 - core)
+    partners = [other]
+    for bit in (1, 2, 4, 8):
+        partners.append((chip + bit * (1 - 2 * lax.rem(lax.div(chip, bit), 2)), core))
     barrier = pltpu.get_barrier_semaphore()
     signal_neighbours([barrier] * 4, near, has_up, has_down)
-    pl.semaphore_wait(barrier, degree)
+    for device in (other, partners[4]):
+        pl.semaphore_signal(barrier, inc=1, device_id=device, device_id_type=MESH_IDS)
+    pl.semaphore_wait(barrier, degree + 2)
     rows = gz.shape[4]
     low, high = pl.ds(0, rows // 2), pl.ds(rows // 2, rows // 2)
 
@@ -939,7 +995,7 @@
             device_id_type=MESH_IDS,
         )
 
-    def arrived(ref, sem):
+    def arrived_at(ref, sem):
         remote(ref, ref, send_z.at[0], sem, right).wait_recv()
 
     def sent(ref, sem):
@@ -947,16 +1003,7 @@
 
     firsts = [
         pltpu.make_async_copy(src, dst, first_sem.at[n])
-        for n, (src, dst) in enumerate(
-            (
-                (text_h, text_v),
-                (dkv_h, dkv_v),
-                (q_h, q_v),
-                (k_h, k_v),
-                (v_h, v_v),
-                (do_h, do_v),
-            )
-        )
+        for n, (src, dst) in enumerate(((text_h, text_v), (k2_h, k2_v), (v2_h, v2_v)))
     ]
 
     def left_copy(n):
@@ -1012,8 +1059,8 @@
                     left_part = lbuf[slot, :, pl.ds(i * 4 * rows, 4 * rows)]
                     store_unit(which, k, i, dot_tn(left_part, right_part))
 
-        for n in range(2, ROWS_L):
-            pl.when(c == FIRST_L[n - 1] // 2)(left_copy(n).start)
+        for n, at in LOAD_L:
+            pl.when(c == at)(left_copy(n).start)
         pl.when(c + 1 < total)(lambda: start_rights(c + 1))
 
     def out_copies(c):
@@ -1035,43 +1082,49 @@
 
     def plane_second(add, k, bufs, send_sem, recv):
         xd, yd, xb, yb = bufs
-        arrived(xd.at[k], recv.at[k, XD])
+        arrived_at(xd.at[k], recv.at[k, XD])
         add(xd, yn, x, low)
         remote(xd.at[k], yb.at[k], send_sem.at[k], recv.at[k, YB], across).start()
-        arrived(yd.at[k], recv.at[k, YD])
+        arrived_at(yd.at[k], recv.at[k, YD])
         add(yd, y, xn, high)
         remote(yd.at[k], xb.at[k], send_sem.at[k], recv.at[k, XB], right).start()
 
+    def above(buf, k, first, blocks):
+        return buf.at[k, pl.ds(first + 1, blocks)]
+
+    def below(buf, k, blocks):
+        return buf.at[k, pl.ds(0, blocks)]
+
     def line_up(first, buf, add, k, send_sem, recv):
         blocks = 4 - first
-        arrived(buf.at[k, pl.ds(first, blocks)], recv.at[k, UP])
+        arrived_at(above(buf, k, first, blocks), recv.at[k, UP])
         if blocks > 1:
             for block in range(first + 1, 4):
-                add(buf, block)
-            ref = buf.at[k, pl.ds(first + 1, blocks - 1)]
+                add(buf, block, block + 1)
+            ref = above(buf, k, first + 1, blocks - 1)
             remote(ref, ref, send_sem.at[k], recv.at[k, UP], up).start()
 
     def line_down(last, buf, add, k, send_sem, recv):
-        arrived(buf.at[k, pl.ds(0, last + 1)], recv.at[k, DOWN])
+        arrived_at(below(buf, k, last + 1), recv.at[k, DOWN])
         if last > 0:
             for block in range(last):
-                add(buf, block)
-            ref = buf.at[k, pl.ds(0, last)]
+                add(buf, block, block)
+            ref = below(buf, k, last)
             remote(ref, ref, send_sem.at[k], recv.at[k, DOWN], down).start()
 
     def add_a(k):
-        def add(buf, block):
+        def add(buf, block, at):
             for yy in range(2):
                 for xx in range(2):
-                    buf[k, block, yy, xx] = total_of(
-                        buf[k, block, yy, xx], ga[k, block, yy, xx]
+                    buf[k, at, yy, xx] = total_of(
+                        buf[k, at, yy, xx], ga[k, block, yy, xx]
                     ).astype(BF16)
 
         return add
 
     def add_z(k):
-        def add(buf, block):
-            buf[k, block] = total_of(buf[k, block], gz[k, block, y, x]).astype(BF16)
+        def add(buf, block, at):
+            buf[k, at] = total_of(buf[k, at], gz[k, block, y, x]).astype(BF16)
 
         return add
 
@@ -1090,12 +1143,12 @@
         @pl.when(z == 0)
         def _():
             ref = pl.ds(1, 3)
-            remote(ga.at[k, ref], upa.at[k, ref], send_a.at[k], recv_a.at[k, UP], up).start()
+            remote(ga.at[k, ref], above(lna, k, 1, 3), send_a.at[k], recv_a.at[k, UP], up).start()
 
         @pl.when(z == 3)
         def _():
             ref = pl.ds(0, 3)
-            remote(ga.at[k, ref], dna.at[k, ref], send_a.at[k], recv_a.at[k, DOWN], down).start()
+            remote(ga.at[k, ref], below(lna, k, 3), send_a.at[k], recv_a.at[k, DOWN], down).start()
 
     def second(c, k):
         def add(buf, yy, xx, half):
@@ -1103,12 +1156,12 @@
                 buf[k, block] = total_of(buf[k, block], gz[k, block, yy, xx, half, :]).astype(BF16)
 
         plane_second(add, k, (xdz, ydz, xbz, ybz), send_z, recv_z)
-        pl.when(z == 1)(lambda: line_up(1, upa, add_a(k), k, send_a, recv_a))
-        pl.when(z == 2)(lambda: line_down(2, dna, add_a(k), k, send_a, recv_a))
+        pl.when(z == 1)(lambda: line_up(1, lna, add_a(k), k, send_a, recv_a))
+        pl.when(z == 2)(lambda: line_down(2, lna, add_a(k), k, send_a, recv_a))
 
     def third(c, k):
         for buf, kind in ((xaz, XA), (yaz, YA), (xbz, XB), (ybz, YB)):
-            arrived(buf.at[k], recv_z.at[k, kind])
+            arrived_at(buf.at[k], recv_z.at[k, kind])
         for block in range(4):
             for half, one, two in ((low, xaz, ybz), (high, yaz, xbz)):
                 gz[k, block, y, x, half, :] = total_of(
@@ -1119,39 +1172,41 @@
         def _():
             ref = pl.ds(1, 3)
             remote(
-                gz.at[k, ref, y, x], upz.at[k, ref], send_z.at[k], recv_z.at[k, UP], up
+                gz.at[k, ref, y, x], above(lnz, k, 1, 3), send_z.at[k], recv_z.at[k, UP], up
             ).start()
 
         @pl.when(z == 3)
         def _():
             ref = pl.ds(0, 3)
             remote(
-                gz.at[k, ref, y, x], dnz.at[k, ref], send_z.at[k], recv_z.at[k, DOWN], down
+                gz.at[k, ref, y, x], below(lnz, k, 3), send_z.at[k], recv_z.at[k, DOWN], down
             ).start()
 
-        pl.when(z == 2)(lambda: line_up(2, upa, add_a(k), k, send_a, recv_a))
-        pl.when(z == 1)(lambda: line_down(1, dna, add_a(k), k, send_a, recv_a))
+        pl.when(z == 2)(lambda: line_up(2, lna, add_a(k), k, send_a, recv_a))
+        pl.when(z == 1)(lambda: line_down(1, lna, add_a(k), k, send_a, recv_a))
 
     def fourth(c, k):
-        pl.when(z == 1)(lambda: line_up(1, upz, add_z(k), k, send_z, recv_z))
-        pl.when(z == 2)(lambda: line_down(2, dnz, add_z(k), k, send_z, recv_z))
-        pl.when(z == 3)(lambda: line_up(3, upa, None, k, send_a, recv_a))
-        pl.when(z == 0)(lambda: line_down(0, dna, None, k, send_a, recv_a))
-        for buf, exists in ((upa, has_down), (dna, has_up)):
+        pl.when(z == 1)(lambda: line_up(1, lnz, add_z(k), k, send_z, recv_z))
+        pl.when(z == 2)(lambda: line_down(2, lnz, add_z(k), k, send_z, recv_z))
+        pl.when(z == 3)(lambda: line_up(3, lna, None, k, send_a, recv_a))
+        pl.when(z == 0)(lambda: line_down(0, lna, None, k, send_a, recv_a))
+        for shift, exists in ((1, has_down), (0, has_up)):
 
             @pl.when(exists)
             def _():
                 for yy in range(2):
                     for xx in range(2):
-                        ga[k, z, yy, xx] = total_of(ga[k, z, yy, xx], buf[k, z, yy, xx]).astype(BF16)
+                        ga[k, z, yy, xx] = total_of(
+                            ga[k, z, yy, xx], lna[k, z + shift, yy, xx]
+                        ).astype(BF16)
 
         plane_first(
             lambda yy, xx, half: ga.at[k, z, yy, xx, half, :], k, (xda, yda, xaa, yaa), send_a, recv_a
         )
 
     def fifth(c, k):
-        pl.when(z == 2)(lambda: line_up(2, upz, add_z(k), k, send_z, recv_z))
-        pl.when(z == 1)(lambda: line_down(1, dnz, add_z(k), k, send_z, recv_z))
+        pl.when(z == 2)(lambda: line_up(2, lnz, add_z(k), k, send_z, recv_z))
+        pl.when(z == 1)(lambda: line_down(1, lnz, add_z(k), k, send_z, recv_z))
 
         def add(buf, yy, xx, half):
             buf[k] = total_of(buf[k], ga[k, z, yy, xx, half, :]).astype(BF16)
@@ -1159,8 +1214,8 @@
         plane_second(add, k, (xda, yda, xba, yba), send_a, recv_a)
 
     def finish(c, k):
-        pl.when(z == 3)(lambda: line_up(3, upz, None, k, send_z, recv_z))
-        pl.when(z == 0)(lambda: line_down(0, dnz, None, k, send_z, recv_z))
+        pl.when(z == 3)(lambda: line_up(3, lnz, None, k, send_z, recv_z))
+        pl.when(z == 0)(lambda: line_down(0, lnz, None, k, send_z, recv_z))
         o = lax.rem(c, 2)
 
         @pl.when(c >= 2)
@@ -1169,14 +1224,14 @@
                 copy.wait()
 
         oz[o] = gz[k, z, y, x].astype(F32)
-        for buf, exists in ((upz, has_down), (dnz, has_up)):
+        for shift, exists in ((1, has_down), (0, has_up)):
 
             @pl.when(exists)
             def _():
-                oz[o] = oz[o] + buf[k, z].astype(F32)
+                oz[o] = oz[o] + lnz[k, z + shift].astype(F32)
 
         for buf, kind in ((xaa, XA), (yaa, YA), (xba, XB), (yba, YB)):
-            arrived(buf.at[k], recv_a.at[k, kind])
+            arrived_at(buf.at[k], recv_a.at[k, kind])
         oa[o, low, :] = total_of(ga[k, z, y, x, low, :], xaa[k], yba[k])
         oa[o, high, :] = total_of(ga[k, z, y, x, high, :], yaa[k], xba[k])
         for copy in out_copies(c):
@@ -1189,28 +1244,413 @@
 
             @pl.when(z == step)
             def _():
-                sent(upz.at[k, pl.ds(step + 1, 3 - step)], send_z.at[k])
-                sent(upa.at[k, pl.ds(step + 1, 3 - step)], send_a.at[k])
+                sent(above(lnz, k, step + 1, 3 - step), send_z.at[k])
+                sent(above(lna, k, step + 1, 3 - step), send_a.at[k])
 
             @pl.when(z == 3 - step)
             def _():
-                sent(dnz.at[k, pl.ds(0, 3 - step)], send_z.at[k])
-                sent(dna.at[k, pl.ds(0, 3 - step)], send_a.at[k])
+                sent(below(lnz, k, 3 - step), send_z.at[k])
+                sent(below(lna, k, 3 - step), send_a.at[k])
 
         @pl.when(c < total - slots)
         def _():
             signal_neighbours([credit.at[i] for i in (0, 1, 3, 2)], near, has_up, has_down)
 
+    frames, features = e3_h.shape
+    part, half_rows = pool.shape[2], frames // 2
+    heads = part // HEAD_DIM
+    own_rows = pl.ds(pl.multiple_of(core * half_rows, half_rows), half_rows)
+    wide = pl.ds(0, features)
+    slope = dqkv.at[:, pl.ds(features, part)]
+    block = 256
+
+    def columns(n):
+        return pl.ds(pl.multiple_of(n * part, part), part)
+
+    def weight_copy(slot, ref, n=0):
+        return pltpu.make_async_copy(ref.at[:, columns(n)], weights.at[slot], weight_sem.at[slot])
+
+    def use(slot):
+        weight_copy(slot, w_q).wait()
+
+    def pool_copy(n, ref, m=0):
+        return pltpu.make_async_copy(ref.at[:, columns(m)], pool.at[n], pool_sem.at[n])
+
+    def slope_copy(n):
+        return pltpu.make_async_copy(slope_h.at[:, columns(n)], slope, slope_sem)
+
+    def keep_copy(n, src, dst):
+        return pltpu.make_async_copy(src, dst, keep_sem.at[n])
+
+    def du_copy(n):
+        return keep_copy(0, pool.at[n], du_h.at[:, columns(n)])
+
+    def to_other(n, src, dst):
+        return remote(src, dst, share_send.at[n], share_recv.at[n], other)
+
+    def share_sum(n):
+        return to_other(n, theirs, arrived.at[n % 2])
+
+    def share_branch(n):
+        ref = dqkv.at[own_rows, wide]
+        return to_other(4 + n, ref, ref)
+
+    def multiply(whose, source, slot, fresh):
+        for first in range(0, half_rows, block):
+            rows_of = pl.ds(pl.multiple_of(whose * half_rows + first, block), block)
+            value = dot_nt(source(rows_of), weights[slot])
+            lines = pl.ds(first, block)
+            acc[lines, :] = value if fresh else acc[lines, :] + value
+
+    def pooled(n):
+        return lambda rows_of: pool[n, rows_of, :]
+
+    def headed(n):
+        return lambda rows_of: dqkv[rows_of, pl.ds(n * part, part)]
+
+    def send_sum(n):
+        for first in range(0, half_rows, block):
+            lines = pl.ds(first, block)
+            theirs[lines, :] = acc[lines, :].astype(BF16)
+        share_sum(n).start()
+
+    def norm_back(kind, n, load, before, store):
+        step = 64
+        gain = norms[2 * kind : 2 * kind + 1, :]
+
+        def body(i, sums):
+            first = pl.multiple_of(i * step, step)
+            lines = pl.ds(first, step)
+            value = load(i, lines)
+            offset = value - jnp.mean(value, axis=-1, keepdims=True)
+            scale = lax.rsqrt(jnp.mean(offset * offset, axis=-1, keepdims=True) + norm_eps)
+            unit = offset * scale
+            slope_in = acc[lines, :] + arrived[n % 2, lines, :].astype(F32)
+            scaled = slope_in * gain
+            inner = jnp.mean(scaled * unit, axis=-1, keepdims=True)
+            change = scale * (scaled - jnp.mean(scaled, axis=-1, keepdims=True) - unit * inner)
+            store(first, lines, before(first, lines) + change)
+            return (
+                sums[0] + jnp.sum(slope_in * unit, axis=0, keepdims=True),
+                sums[1] + jnp.sum(slope_in, axis=0, keepdims=True),
+            )
+
+        zero = jnp.zeros((1, features), F32)
+        gains, shifts = lax.fori_loop(0, half_rows // step, body, (zero, zero))
+        norm_grads[2 * kind : 2 * kind + 1, :] = gains
+        norm_grads[2 * kind + 1 : 2 * kind + 2, :] = shifts
+
+    def streamed(ref):
+        step = xbuf.shape[1]
+
+        def copy(i):
+            first = pl.multiple_of(i * step, step)
+            return pltpu.make_async_copy(
+                ref.at[pl.ds(first, step), :], xbuf.at[lax.rem(i, 2)], x_sem.at[lax.rem(i, 2)]
+            )
+
+        copy(jnp.int32(0)).start()
+
+        def load(i, lines):
+            copy(i).wait()
+            pl.when(i + 1 < half_rows // step)(copy(i + 1).start)
+            return xbuf[lax.rem(i, 2)]
+
+        return load
+
+    def store_branch(first, lines, value):
+        grad[lines, :] = value
+        dqkv[pl.ds(pl.multiple_of(core * half_rows + first, 64), 64), wide] = value.astype(BF16)
+
+    def project_to(n, slot):
+        for first in range(0, frames, block):
+            lines = pl.ds(first, block)
+            pool[n, lines, :] = dot_nn(dqkv[lines, wide], weights[slot]).astype(BF16)
+
+    def feed_forward(j):
+        use(0)
+        slope_copy(j).wait()
+        for first in range(0, frames, block):
+            lines = pl.ds(first, block)
+            value = dot_nn(lbuf[0, lines, :], weights[0])
+            pool[j, lines, :] = (
+                value * dqkv[lines, pl.ds(features, part)].astype(F32)
+            ).astype(BF16)
+
+        @pl.when(j > 0)
+        def _():
+            du_copy(j - 1).wait()
+
+        du_copy(j).start()
+
+        @pl.when(j < 3)
+        def _():
+            weight_copy(0, w_down, j + 1).start()
+            slope_copy(j + 1).start()
+
+        pl.when(j == 3)(lambda: weight_copy(0, w_up, 0).start())
+        use(1)
+        multiply(1 - core, pooled(j), 1, False)
+        pl.when(j < 3)(lambda: weight_copy(1, w_up, j + 1).start())
+        pl.when(j == 3)(lambda: send_sum(0))
+
+    def turn_4():
+        du_copy(3).wait()
+        multiply(core, pooled(3), 1, True)
+        weight_copy(1, w_up, 1).start()
+        use(0)
+        multiply(core, pooled(0), 0, False)
+        weight_copy(0, w_up, 2).start()
+
+    def turn_5():
+        use(1)
+        multiply(core, pooled(1), 1, False)
+        weight_copy(1, w_cq).start()
+        use(0)
+        multiply(core, pooled(2), 0, False)
+        weight_copy(0, w_co).start()
+
+    def turn_6():
+        pool_copy(0, q2_h).start()
+        share_sum(0).wait()
+        norm_back(
+            2,
+            0,
+            streamed(x3_h),
+            lambda first, lines: lbuf[
+                0, pl.ds(pl.multiple_of(core * half_rows + first, 64), 64), :
+            ].astype(F32),
+            store_branch,
+        )
+        share_branch(0).start()
+
+    def turn_7():
+        share_branch(0).wait()
+        keep_copy(1, dqkv.at[:, wide], e2_h).start()
+        use(0)
+        project_to(1, 0)
+        weight_copy(0, w_ck).start()
+
+    def turn_8():
+        pool_copy(0, q2_h).wait()
+        for copy in firsts:
+            copy.wait()
+
+        def body(head, carry):
+            head_back(
+                head,
+                pool.at[0],
+                k2_v,
+                v2_v,
+                pool.at[1],
+                lse2_ref,
+                pool.at[2],
+                dkv_v,
+                (0, 0, part),
+                acc_k,
+                acc_v,
+                False,
+            )
+            return carry
+
+        lax.fori_loop(0, heads, body, 0)
+        keep_copy(1, dqkv.at[:, wide], e2_h).wait()
+        keep_copy(0, pool.at[2], dq2_h).start()
+        use(0)
+        text_part[...] = dot_nt(dkv_v[:, pl.ds(0, part)], weights[0])
+        weight_copy(0, w_cv).start()
+
+    def text_columns(whose):
+        count = features // 2
+        return pl.ds(pl.multiple_of(whose * count, count), count)
+
+    def text_share():
+        return to_other(6, text_send, text_got)
+
+    def turn_9():
+        keep_copy(0, pool.at[2], dq2_h).wait()
+        use(0)
+        text_part[...] += dot_nt(dkv_v[:, pl.ds(part, part)], weights[0])
+        text_send[...] = text_part[:, text_columns(1 - core)].astype(BF16)
+        text_share().start()
+        weight_copy(0, w_o).start()
+        use(1)
+        multiply(1 - core, pooled(2), 1, True)
+        send_sum(1)
+
+    def turn_10():
+        multiply(core, pooled(2), 1, True)
+        for n, ref in enumerate((q1_h, k1_h, v1_h)):
+            pool_copy(n, ref).start()
+        share_sum(1).wait()
+        norm_back(1, 1, streamed(x2_h), lambda first, lines: grad[lines, :], store_branch)
+        share_branch(1).start()
+        text_share().wait()
+        text_part[:, pl.ds(0, features // 2)] = text_part[:, text_columns(core)] + text_got[
+            ...
+        ].astype(F32)
+        keep_copy(2, text_part.at[:, pl.ds(0, features // 2)], grad_text).start()
+
+    def turn_11():
+        share_branch(1).wait()
+        keep_copy(1, dqkv.at[:, wide], e1_h).start()
+        use(0)
+        project_to(3, 0)
+        weight_copy(0, w_q).start()
+        weight_copy(1, w_k).start()
+
+    def turn_12():
+        keep_copy(1, dqkv.at[:, wide], e1_h).wait()
+        for n, ref in enumerate((q1_h, k1_h, v1_h)):
+            pool_copy(n, ref).wait()
+
+    def self_head(head):
+        head_back(
+            head,
+            pool.at[0],
+            pool.at[1],
+            pool.at[2],
+            pool.at[3],
+            lse1_ref,
+            dqkv,
+            dqkv,
+            (0, part, 2 * part),
+            acc_k,
+            acc_v,
+            True,
+        )
+
+    def turn_18():
+        for n in range(4):
+            pool_copy(n, a_h, n).start()
+        use(0)
+        multiply(1 - core, headed(0), 0, True)
+        weight_copy(0, w_v).start()
+        use(1)
+        multiply(1 - core, headed(1), 1, False)
+
+    def turn_19():
+        use(0)
+        multiply(1 - core, headed(2), 0, False)
+        send_sum(2)
+        multiply(core, headed(2), 0, True)
+        weight_copy(0, w_down, 0).start()
+        multiply(core, headed(1), 1, False)
+        weight_copy(1, w_q).start()
+
+    def turn_20():
+        use(1)
+        multiply(core, headed(0), 1, False)
+        weight_copy(1, w_down, 1).start()
+
+    def turn_21():
+        share_sum(2).wait()
+        hidden = keep_copy(1, x1_h, theirs)
+        hidden.start()
+        hidden.wait()
+
+        def store(first, lines, value):
+            grad[lines, :] = value
+
+        norm_back(
+            0,
+            2,
+            lambda i, lines: theirs[lines, :].astype(F32),
+            lambda first, lines: grad[lines, :],
+            store,
+        )
+        keep_copy(3, grad, grad_input).start()
+
+    def turn_22():
+        for n in range(4):
+            pool_copy(n, a_h, n).wait()
+        use(0)
+        multiply(1 - core, pooled(0), 0, True)
+        weight_copy(0, w_down, 2).start()
+        use(1)
+        multiply(1 - core, pooled(1), 1, False)
+        weight_copy(1, w_down, 3).start()
+
+    def turn_23():
+        keep_copy(3, grad, grad_input).wait()
+        keep_copy(1, x3_h, grad).start()
+        use(0)
+        multiply(1 - core, pooled(2), 0, False)
+        use(1)
+        multiply(1 - core, pooled(3), 1, False)
+        send_sum(3)
+        multiply(core, pooled(2), 0, True)
+        weight_copy(0, w_down, 0).start()
+        multiply(core, pooled(3), 1, False)
+        weight_copy(1, w_down, 1).start()
+
+    def turn_24():
+        use(0)
+        multiply(core, pooled(0), 0, False)
+        use(1)
+        multiply(core, pooled(1), 1, False)
+
+    def turn_25():
+        share_sum(3).wait()
+        keep_copy(1, x3_h, grad).wait()
+        for first in range(0, half_rows, 64):
+            lines = pl.ds(first, 64)
+            theirs[lines, :] = (
+                grad[lines, :] + (acc[lines, :] + arrived[1, lines, :].astype(F32))
+            ).astype(BF16)
+        keep_copy(0, theirs, layer_out).start()
+
+    def norm_copy(step):
+        return remote(
+            got.at[2 * step],
+            got.at[2 * step + 1],
+            norm_send.at[step],
+            norm_recv.at[step],
+            partners[step],
+        )
+
+    def norm_sum(step):
+        if step == 0:
+            got[0] = norm_grads[...]
+        else:
+            norm_copy(step - 1).wait()
+            got[2 * step] = got[2 * step - 2] + got[2 * step - 1]
+        if step < len(partners):
+            norm_copy(step).start()
+        else:
+            keep_copy(1, got.at[2 * step], norm_out).start()
+
+    chain = {
+        4: turn_4,
+        5: turn_5,
+        6: turn_6,
+        7: turn_7,
+        8: turn_8,
+        9: turn_9,
+        10: turn_10,
+        11: turn_11,
+        18: turn_18,
+        19: turn_19,
+        20: turn_20,
+        21: turn_21,
+        22: turn_22,
+        23: turn_23,
+        24: turn_24,
+        25: turn_25,
+    }
     stages = (begin, second, third, fourth, fifth, finish)
     left_copy(0).start()
+    weight_copy(0, w_down, 0).start()
+    slope_copy(0).start()
     start_rights(jnp.int32(0))
+    weight_copy(1, w_up, 0).start()
     left_copy(1).start()
     for copy in firsts:
         copy.start()
+    for first in range(0, half_rows, block):
+        acc[pl.ds(first, block), :] = jnp.zeros((block, features), F32)
+    norm_grads[...] = jnp.zeros_like(norm_grads)
     left_copy(0).wait()
-    for copy in firsts:
-        copy.wait()
-    dqkv_copy = pltpu.make_async_copy(dqkv, dqkv_h, dqkv_sem)
 
     def body(turn, carry):
         for step, stage in enumerate(stages):
@@ -1221,146 +1661,108 @@
                 stage(c, lax.rem(c, slots))
 
         pl.when(turn < total)(lambda: compute(turn, lax.rem(turn, slots)))
-
-        @pl.when((turn >= 1) & (turn <= heads))
+        pl.when(turn < 4)(lambda: feed_forward(turn))
+        for number, fn in chain.items():
+            pl.when(turn == number)(fn)
+        pl.when(turn == 12)(turn_12)
+
+        @pl.when((turn >= 12) & (turn < 18))
         def _():
-            head_back(turn - 1, q_v, k_v, v_v, do_v, lse_ref, dqkv, acc_k, acc_v)
-
-        pl.when(turn == heads + 1)(dqkv_copy.start)
+            def both(head, carry):
+                self_head(head)
+                return carry
+
+            first = lax.div(heads, 6) * (turn - 12)
+            lax.fori_loop(first, first + heads // 6, both, 0)
+
+        for step in range(len(partners) + 1):
+            pl.when(turn == 22 + step)(functools.partial(norm_sum, step))
         return carry
 
     lax.fori_loop(0, total + len(stages), body, 0)
     for c in (total - 2, total - 1):
         for copy in out_copies(jnp.int32(c)):
             copy.wait()
-    dqkv_copy.wait()
-
-
-def backward_all(lefts, rights, text, grad_text_rows, heads_in, log_sums):
-    frames, width = lefts[0].shape
-    rows = width // 16
-    part = heads_in[0].shape[1]
-    dma = pltpu.SemaphoreType.DMA
-    vmem = pltpu.VMEM
-
-    def buffer(*shape):
-        return vmem((SLOTS,) + shape, BF16)
+    keep_copy(0, theirs, layer_out).wait()
+    keep_copy(1, got.at[2 * len(partners)], norm_out).wait()
+    keep_copy(2, text_part.at[:, pl.ds(0, features // 2)], grad_text).wait()
+
+
+def backward_all(arrays, small):
+    frames, width = arrays[0].shape
+    text = arrays[8]
+    rows, half, part = width // 16, frames // 2, arrays[9].shape[1]
+    dma, vmem, shape = pltpu.SemaphoreType.DMA, pltpu.VMEM, jax.ShapeDtypeStruct
+
+    def buffer(*dims):
+        return vmem((SLOTS,) + dims, BF16)
 
     anywhere = pl.BlockSpec(memory_space=pl.ANY)
-    inputs = (*lefts, *rights, text, grad_text_rows, *heads_in, log_sums)
     return pl.pallas_call(
         backward_kernel,
         out_shape=[
-            jax.ShapeDtypeStruct((rows, UNITS * UNIT), F32),
-            jax.ShapeDtypeStruct((frames, 3 * part), BF16),
+            shape((rows, UNITS * UNIT), F32),
+            shape((half, width), BF16),
+            shape((half, width), F32),
+            shape((text.shape[0], width // 2), F32),
+            shape((8, width), F32),
+            shape((frames, 4 * part), BF16),
+            shape((frames, part), BF16),
+            shape((frames, width), BF16),
+            shape((frames, width), BF16),
         ],
-        in_specs=[anywhere] * (len(inputs) - 1) + [pl.BlockSpec(memory_space=vmem)],
-        out_specs=[anywhere] * 2,
+        in_specs=[anywhere] * len(arrays) + [pl.BlockSpec(memory_space=vmem)] * len(small),
+        out_specs=[anywhere] * 9,
         scratch_shapes=[
             buffer(4, 2, 2, rows, WIDTH_Z),
             buffer(4, 2, 2, rows, WIDTH_A),
             *[buffer(4, rows // 2, WIDTH_Z)] * 6,
-            *[buffer(4, rows, WIDTH_Z)] * 2,
+            buffer(5, rows, WIDTH_Z),
             *[buffer(rows // 2, WIDTH_A)] * 6,
-            *[buffer(4, 2, 2, rows, WIDTH_A)] * 2,
+            buffer(5, 2, 2, rows, WIDTH_A),
             vmem((2, rows, WIDTH_Z), F32),
             vmem((2, rows, WIDTH_A), F32),
             vmem((2, frames, width), BF16),
             vmem((2, 2, frames, UNIT), BF16),
             vmem(text.shape, BF16),
-            vmem(grad_text_rows.shape, BF16),
-            *[vmem((frames, part), BF16)] * 4,
+            vmem((text.shape[0], 2 * part), BF16),
+            *[vmem((text.shape[0], part), BF16)] * 2,
+            vmem((4, frames, part), BF16),
             vmem((frames, 3 * part), BF16),
             *[vmem((frames, 128), F32)] * 2,
-            dma((6,)),
+            *[vmem((half, width), F32)] * 2,
+            vmem((2, 64, width), F32),
+            vmem((half, width), BF16),
+            vmem((2, half, width), BF16),
+            vmem((2, width, part), BF16),
+            vmem((text.shape[0], width), F32),
+            *[vmem((text.shape[0], width // 2), BF16)] * 2,
+            vmem((8, width), F32),
+            vmem((11, 8, width), F32),
+            dma((3,)),
             dma((2,)),
             dma((2, 2)),
-            dma,
             dma((2, 2)),
             dma((SLOTS,)),
             dma((SLOTS,)),
             dma((SLOTS, 8)),
             dma((SLOTS, 8)),
+            dma((4,)),
+            dma,
+            dma((2,)),
+            dma((2,)),
+            dma((4,)),
+            dma((7,)),
+            dma((7,)),
+            dma((5,)),
+            dma((5,)),
             pltpu.SemaphoreType.REGULAR((4,)),
         ],
         compiler_params=pltpu.CompilerParams(
             collective_id=1, has_side_effects=True, vmem_limit_bytes=VMEM_LIMIT
         ),
         name="backward",
-    )(*inputs)
-
-
-def sum_everywhere_kernel(values, out, got, send_sem, recv_sem):
-    chip, core = lax.axis_index("dp"), lax.axis_index("tensor")
-    partners = [(chip, 1 - core)]
-    for bit in (1, 2, 4, 8):
-        partners.append((chip + bit * (1 - 2 * lax.rem(lax.div(chip, bit), 2)), core))
-    barrier = pltpu.get_barrier_semaphore()
-    for device in partners:
-        pl.semaphore_signal(barrier, inc=1, device_id=device, device_id_type=MESH_IDS)
-    pl.semaphore_wait(barrier, len(partners))
-    got[0] = values[...]
-    for step, device in enumerate(partners):
-        copy = pltpu.make_async_remote_copy(
-            src_ref=got.at[2 * step],
-            dst_ref=got.at[2 * step + 1],
-            send_sem=send_sem.at[step],
-            recv_sem=recv_sem.at[step],
-            device_id=device,
-            device_id_type=MESH_IDS,
-        )
-        copy.start()
-        copy.wait()
-        got[2 * step + 2] = got[2 * step] + got[2 * step + 1]
-    out[...] = got[2 * len(partners)]
-
-
-def sum_everywhere(values):
-    dma = pltpu.SemaphoreType.DMA
-    vmem = pl.BlockSpec(memory_space=pltpu.VMEM)
-    return pl.pallas_call(
-        sum_everywhere_kernel,
-        out_shape=jax.ShapeDtypeStruct(values.shape, F32),
-        in_specs=[vmem],
-        out_specs=vmem,
-        scratch_shapes=[pltpu.VMEM((11,) + values.shape, F32), dma((5,)), dma((5,))],
-        compiler_params=pltpu.CompilerParams(collective_id=2, has_side_effects=True),
-        name="sum_norm_gradients",
-    )(values)
-
-
-def project_t(row_data, weight):
-    return jnp.einsum("cli,io->clo", row_data, weight, preferred_element_type=jnp.float32)
-
-
-def input_grad_t(grad_rows, weight):
-    return jnp.einsum("cla,ia->cli", grad_rows, weight, preferred_element_type=jnp.float32)
-
-
-def other_core(values):
-    return lax.ppermute(values, "tensor", [(0, 1), (1, 0)])
-
-
-def share_rows(values):
-    other = other_core(values)
-    first = lax.axis_index("tensor") == 0
-    return jnp.concatenate(
-        [jnp.where(first, values, other), jnp.where(first, other, values)], axis=1
-    )
-
-
-def sum_rows(rows, product):
-    core, half = lax.axis_index("tensor"), rows[0].shape[1] // 2
-    theirs = product(*[lax.dynamic_slice_in_dim(r, (1 - core) * half, half, 1) for r in rows])
-    arriving = other_core(theirs.astype(BF16))
-    mine = product(*[lax.dynamic_slice_in_dim(r, core * half, half, 1) for r in rows])
-    return mine + arriving.astype(F32)
-
-
-def gelu_parts(values):
-    below = 0.5 * (1.0 + lax.erf(values * (0.5**0.5)))
-    density = jnp.exp(-0.5 * values * values) * 0.3989422804014327
-    return (values * below).astype(BF16), (below + values * density).astype(BF16)
+    )(*arrays, *small)
 
 
 def gather_plan(columns):
@@ -1412,102 +1814,31 @@
         hidden_down,
     )
     gathered, kept = forward_all(
-        shards, gather_plan([s.shape[1] for s in shards]), hidden_in[0], text_states[0]
+        shards,
+        gather_plan([s.shape[1] for s in shards]),
+        hidden_in[0],
+        text_states[0],
+        cotangent[0],
     )
     w_q, w_k, w_v, w_o, w_ck, w_cv, w_cq, w_co, w_up, w_down = [
         g.reshape(width, g.shape[-1]) for g in gathered[1:]
     ]
-    normed_one, normed_two, normed_three = [k[None] for k in kept[:3]]
+    normed_one, normed_two, normed_three = kept[:3]
     query_one, key_one, value_one, attended_one = kept[3:7]
-    query_two, key_two, value_two, attended_two = [split_heads(k[None]) for k in kept[7:11]]
-    logsum_one, logsum_two = kept[11], kept[12][None, :12]
-    gain_self, bias_self, gain_cross, bias_cross, gain_ffn, bias_ffn = [kept[13][i] for i in range(6)]
-    stream_one, stream_two, stream_three = hidden_in.astype(F32), kept[14][None], kept[15][None]
-    upper = project_t(normed_three, w_up)
-    active, slope = gelu_parts(upper)
-    layer_out = (stream_three + sum_rows([active], lambda r: project(r, w_down))).astype(jnp.bfloat16)
-    grad_three = cotangent.astype(jnp.float32)
-    grad_branch = share_rows(grad_three.astype(jnp.bfloat16))
-    branch_three = grad_branch
-    grad_active = jnp.einsum("clo,of->clf", grad_branch, w_down, preferred_element_type=jnp.float32)
-    grad_upper = (grad_active * slope.astype(F32)).astype(jnp.bfloat16)
-    norm_back = jax.vjp(layer_norm, stream_three, gain_ffn, bias_ffn)[1]
-    grad_stream, grad_gain_ffn, grad_bias_ffn = norm_back(
-        sum_rows([grad_upper], lambda r: input_grad_t(r, w_up))
-    )
-    grad_two = grad_three + grad_stream
-    grad_branch = share_rows(grad_two.astype(jnp.bfloat16))
-    branch_two = grad_branch
-    grad_attended = split_heads(
-        jnp.einsum("clo,oa->cla", grad_branch, w_co, preferred_element_type=F32).astype(BF16)
-    )
-    grad_query, grad_key, grad_value = attend_back(
-        query_two, key_two, value_two, grad_attended, logsum_two, False
-    )
-    grad_query = flatten_heads(grad_query).astype(jnp.bfloat16)
-    grad_key = flatten_heads(grad_key).astype(jnp.bfloat16)
-    grad_value = flatten_heads(grad_value).astype(jnp.bfloat16)
-    grad_query_two = grad_query
-    text_part = input_grad_t(grad_key, w_ck) + input_grad_t(grad_value, w_cv)
-    core, half = lax.axis_index("tensor"), width // 2
-    arriving = other_core(
-        lax.dynamic_slice_in_dim(text_part, (1 - core) * half, half, 2).astype(BF16)
-    )
-    grad_text = lax.dynamic_slice_in_dim(text_part, core * half, half, 2) + arriving.astype(F32)
-    norm_back = jax.vjp(layer_norm, stream_two, gain_cross, bias_cross)[1]
-    grad_stream, grad_gain_cross, grad_bias_cross = norm_back(
-        sum_rows([grad_query], lambda r: input_grad_t(r, w_cq))
-    )
-    grad_one = grad_two + grad_stream
-    grad_branch = share_rows(grad_one.astype(jnp.bfloat16))
-    grad_attended = jnp.einsum(
-        "clo,oa->cla", grad_branch, w_o, preferred_element_type=F32
-    ).astype(BF16)
-    part = grad_attended.shape[2]
-    summed, grad_heads = backward_all(
-        [
-            r[0]
-            for r in (branch_three, normed_three, branch_two, normed_two, grad_branch, normed_one)
-        ],
-        [
-            r[0]
-            for r in (
-                active,
-                grad_upper,
-                flatten_heads(attended_two),
-                grad_query_two,
-                attended_one[None],
-            )
-        ],
-        text_states[0],
-        jnp.concatenate([grad_key[0], grad_value[0]], axis=1),
-        [query_one, key_one, value_one, grad_attended[0]],
-        logsum_one,
-    )
-    grad_query, grad_key, grad_value = [
-        grad_heads[None, :, n * part : (n + 1) * part] for n in range(3)
-    ]
-    grad_normed = sum_rows(
-        [grad_query, grad_key, grad_value],
-        lambda q, k, v: input_grad_t(q, w_q) + input_grad_t(k, w_k) + input_grad_t(v, w_v),
-    )
-    norm_back = jax.vjp(layer_norm, stream_one, gain_self, bias_self)[1]
-    grad_stream, grad_gain_self, grad_bias_self = norm_back(grad_normed)
-    grad_input = grad_one + grad_stream
-    norm_grads = jnp.stack(
-        [
-            grad_gain_self,
-            grad_bias_self,
-            grad_gain_cross,
-            grad_bias_cross,
-            grad_gain_ffn,
-            grad_bias_ffn,
-        ]
-    )
-    rows = width // 16
-    norm_sums = lax.dynamic_slice_in_dim(
-        sum_everywhere(jnp.pad(norm_grads, ((0, 2), (0, 0)))), lax.axis_index("dp") * rows, rows, 1
-    )
+    query_two, key_two, value_two, attended_two = kept[7:11]
+    logsum_one, logsum_two, norms, stream_two, stream_three, branch, active, slope = kept[11:]
+    summed, layer_out, grad_input, grad_text, norm_sums, *_ = backward_all(
+        (
+            *(branch, normed_three, normed_two, normed_one),
+            *(active, slope, attended_two, attended_one, text_states[0]),
+            *(query_two, key_two, value_two, query_one, key_one, value_one),
+            *(stream_three, stream_two, hidden_in[0]),
+            *(w_q, w_k, w_v, w_o, w_ck, w_cv, w_cq, w_co, w_up, w_down),
+        ),
+        (logsum_two, logsum_one, norms),
+    )
+    rows, part = width // 16, query_one.shape[1]
+    norm_sums = lax.dynamic_slice_in_dim(norm_sums, lax.axis_index("dp") * rows, rows, 1)
     columns = [hidden_down.shape[1]] * 2 + [part] * 8
     pieces, first = [], 0
     for count in columns:
@@ -1515,9 +1846,9 @@
         first += count
     down, up, out_cross, query_cross, key_cross, value_cross, out_self, query, key, value = pieces
     return (
-        layer_out,
-        grad_input,
-        grad_text,
+        layer_out[None],
+        grad_input[None],
+        grad_text[None],
         norm_sums[0],
         norm_sums[1],
         query.T,

time: 764 us -> 666 us (0.87)
  matrix products: 112 us -> 0 us
  Pallas kernels: 577 us -> 643 us
  other arithmetic: 32.9 us -> 0 us
  local copies, waits for them, and re-layouts: 30.1 us -> 13.3 us
    dot_general x28 -> x0, matrix products: 112 us -> none  [the longest x12 43.6 us: input_grad_t(): jnp.einsum('cla,ia->cli', grad_rows, weight, preferred_element_type=jnp.f...]
    pallas_call x1, Pallas kernels: 274 us -> 320 us  [forward_all(): pl.pallas_call(functools.partial(forward_kernel, chunks, count), out_shap...]
    pallas_call x2 -> x1, Pallas kernels: 303 us -> 324 us  [backward_all(): pl.pallas_call(backward_kernel, out_shape=[shape((rows, UNITS * UNIT), F3...]
    reduce_sum x8 -> x0, other arithmetic: 10.9 us -> none  [the longest x2 4.82 us: layer_norm(): spread = jnp.mean(offset * offset, axis=-1, keepdims=True)]
  transfers between devices with their start and end apart: 8 -> 0, of which waited for: 0 -> 0; matrix products, arithmetic and copies ran while one was open for 13% -> 0% of each run, Pallas kernels for 36% -> 0%
where the time goes in v4:
time: 666 us; the launch traced here: 658 us
  Pallas kernels  643 us (97%)
  local copies, waits for them, and re-layouts  13.3 us (2%)
    pallas_call x1, Pallas kernels, backward_all(): pl.pallas_call(backward_kernel, out_shape=[shape((rows, UNITS * UNIT), F3...  324 us
    pallas_call x1, Pallas kernels, forward_all(): pl.pallas_call(functools.partial(forward_kernel, chunks, count), out_shap...  320 us

profile of v4, /device:TPU:0, one launch (start us, length us, event | category | flops | bytes accessed | tf_op | source)
XLA Modules:
  0.0 657.6 jit_solution(3791324133310969680)
XLA Ops:
  0.7 0.8 stack.27
  1.4 0.6 pad.4.refs_0_
  2.0 319.8 %forward.1 = (bf16[4,2,2,32,128]{4,3,2,1,0:T(8,128)(2,1)}, bf16[4,2,2,96,768]{4,3,2,1,0:T(8,128)(2,1)}, bf16[4,2,2,96,768]{4,3,2,1,0:T(8,128)(2,1)}, bf16[4,2,2,...) custom-call(bf16[32,128]{1,0:T(8,128)(2,1)} %pad.4.refs_0_, ...), custom_call_target="tpu_custom_call" | custom-call | tf_op jit(solution)/shard_map/forward/pallas_call | solution.py:852
  321.9 323.6 %backward.1 = (f32[96,12288]{1,0:T(8,128)}, bf16[512,1536]{1,0:T(8,128)(2,1)}, f32[512,1536]{1,0:T(8,128)}, f32[64,768]{1,0:T(8,128)}, f32[8,1536]{1,0:T(8,128)}...) custom-call(bf16[1024,1536]{1,0:T(8,128)(2,1)} %get-tuple-element.53, ...), custom_call_target="tpu_custom_call" | custom-call | tf_op jit(solution)/shard_map/backward/pallas_call | solution.py:1701
  645.4 0.0 copy-start
  645.5 3.2 fusion.1
  648.6 0.7 copy-done
  649.4 1.6 fusion
  650.9 0.0 copy-start.1
  650.9 0.9 constant_dynamic-slice_fusion
  651.8 0.5 slice_bitcast_fusion.7
  652.4 2.7 copy.41
  655.0 0.0 copy-done.1
  655.0 0.0 copy-start.2
  655.0 1.7 copy.42
  656.7 0.0 copy-done.2
  656.7 0.7 copy.43
Async XLA Ops:
  645.4 3.9 copy-start
  650.9 4.1 copy-start.1
  655.0 1.7 copy-start.2

commit v5 on v4

--- a/solution.py
+++ b/solution.py
@@ -610,6 +610,7 @@
     loads = [
         pltpu.make_async_copy(hidden_h, hidden, load_sem.at[0]),
         pltpu.make_async_copy(text_h, text, load_sem.at[1]),
+        pltpu.make_async_copy(cotangent_h, theirs.at[1], load_sem.at[2]),
     ]
     for copy in loads:
         copy.start()
@@ -693,7 +694,7 @@
         return values
 
     branch = results[16].at[own]
-    branch_copy = pltpu.make_async_copy(cotangent_h, branch, result_sem.at[16])
+    branch_copy = pltpu.make_async_copy(theirs.at[1], branch, result_sem.at[16])
 
     def active_copies(j):
         lanes = pl.ds(j * active.shape[1], active.shape[1])
@@ -722,15 +723,14 @@
             copy.start()
 
     def work(number):
-        if number == 0:
-            share(5, cotangent_h, branch).start()
-            branch_copy.start()
         if number == 5:
             copy = pltpu.make_async_copy(outs[0], gathered_norms, norm_sem)
             copy.start()
             copy.wait()
             for copy in loads:
                 copy.wait()
+            share(5, theirs.at[1], branch).start()
+            branch_copy.start()
             total = 0.0
             lane = lax.broadcasted_iota(jnp.int32, (128, width), 0)
             place = lax.broadcasted_iota(jnp.int32, (128, width), 1)
@@ -775,6 +775,8 @@
             if number == 11:
                 load_weight("cv", 0)
         if number == 12:
+            share(5, theirs.at[1], branch).wait()
+            branch_copy.wait()
             give(6, o1)
             give(11, lse1)
             wait_weight(1)
@@ -818,8 +820,6 @@
         if number == 18:
             get_share(2, h3)
             give(2, h3)
-            share(5, cotangent_h, branch).wait()
-            branch_copy.wait()
         if 18 <= number < 22:
             hidden_units(number - 18)
 
@@ -852,7 +852,7 @@
     outs = pl.pallas_call(
         functools.partial(forward_kernel, chunks, count),
         out_shape=[shape((4, 2, 2) + s.shape, s.dtype) for s in shards] + [shape(*g) for g in given],
-        in_specs=[anywhere] * (count + 3),
+        in_specs=[pl.BlockSpec(memory_space=vmem)] * count + [anywhere] * 3,
         out_specs=[anywhere] * (count + len(given)),
         scratch_shapes=[
             dma((total,)),
@@ -874,7 +874,7 @@
             vmem((frames, part), BF16),
             dma,
             dma((2, 16)),
-            dma((2,)),
+            dma((3,)),
             dma((6,)),
             dma((6,)),
             dma((19,)),

time: 666 us -> 628 us (0.943)
  Pallas kernels: 643 us -> 605 us
    pallas_call x1, Pallas kernels: 320 us -> 283 us  [forward_all(): pl.pallas_call(functools.partial(forward_kernel, chunks, count), out_shap...]
where the time goes in v5:
time: 628 us; the launch traced here: 619 us
  Pallas kernels  605 us (96%)
  local copies, waits for them, and re-layouts  13.3 us (2%)
    pallas_call x1, Pallas kernels, backward_all(): pl.pallas_call(backward_kernel, out_shape=[shape((rows, UNITS * UNIT), F3...  322 us
    pallas_call x1, Pallas kernels, forward_all(): pl.pallas_call(functools.partial(forward_kernel, chunks, count), out_shap...  283 us

profile of v5, /device:TPU:0, one launch (start us, length us, event | category | flops | bytes accessed | tf_op | source)
XLA Modules:
  0.0 619.4 jit_solution(14060238448667459343)
XLA Ops:
  0.7 0.8 stack.27
  1.4 0.6 pad.4.refs_0_
  2.0 283.1 %forward.1 = (bf16[4,2,2,32,128]{4,3,2,1,0:T(8,128)(2,1)}, bf16[4,2,2,96,768]{4,3,2,1,0:T(8,128)(2,1)}, bf16[4,2,2,96,768]{4,3,2,1,0:T(8,128)(2,1)}, bf16[4,2,2,...) custom-call(bf16[32,128]{1,0:T(8,128)(2,1)} %pad.4.refs_0_, ...), custom_call_target="tpu_custom_call" | custom-call | tf_op jit(solution)/shard_map/forward/pallas_call | solution.py:852
  285.1 322.2 %backward.1 = (f32[96,12288]{1,0:T(8,128)}, bf16[512,1536]{1,0:T(8,128)(2,1)}, f32[512,1536]{1,0:T(8,128)}, f32[64,768]{1,0:T(8,128)}, f32[8,1536]{1,0:T(8,128)}...) custom-call(bf16[1024,1536]{1,0:T(8,128)(2,1)} %get-tuple-element.53, ...), custom_call_target="tpu_custom_call" | custom-call | tf_op jit(solution)/shard_map/backward/pallas_call | solution.py:1701
  607.3 0.0 copy-start
  607.3 3.2 fusion.1
  610.5 0.7 copy-done
  611.2 1.6 fusion
  612.8 0.0 copy-start.1
  612.8 0.9 constant_dynamic-slice_fusion
  613.7 0.5 slice_bitcast_fusion.7
  614.2 2.7 copy.41
  616.9 0.0 copy-done.1
  616.9 0.0 copy-start.2
  616.9 1.7 copy.42
  618.6 0.0 copy-done.2
  618.6 0.7 copy.43
Async XLA Ops:
  607.3 3.9 copy-start
  612.8 4.1 copy-start.1
  616.9 1.7 copy-start.2

commit v6 on v5

--- a/solution.py
+++ b/solution.py
@@ -599,8 +599,8 @@
     results, refs = refs[:19], refs[19:]
     sems, refs = refs[:6], refs[6:]
     (h1, h2, h3, q1, k1, v1, o1, q2, k2, v2, o2, lse1, lse2, x2, x3), refs = refs[:15], refs[15:]
-    gathered_norms, norms, weights, hidden, text, mine, theirs, arrived, active, slopes = refs[:10]
-    norm_sem, weight_sem, load_sem, share_send, share_recv, result_sem = refs[10:]
+    gathered_norms, norms, weights, hidden, text, mine, theirs, arrived, active, slopes, x2_parts = refs[:11]
+    norm_sem, weight_sem, load_sem, share_send, share_recv, result_sem = refs[11:]
     names = dict(norms=0, q=1, k=2, v=3, o=4, ck=5, cv=6, cq=7, co=8, up=9, down=10)
     turn, finish = gather_engine(chunks, shards, outs, sems)
     chip, core = lax.axis_index("dp"), lax.axis_index("tensor")
@@ -684,11 +684,16 @@
             if whose is not core:
                 share(3 + n, theirs.at[n], arrived.at[n]).start()
 
-    def add_stream(n, before, after):
+    def add_stream(n, before, after, parts=None):
         def values(first, step):
             lines = pl.ds(first, step)
             total = before[lines, :].astype(F32) + (mine[lines, :] + arrived[n, lines, :].astype(F32))
             after[lines, :] = total
+            if parts is not None:
+                high = total.astype(BF16)
+                parts[lines, :] = high
+                low = total - high.astype(F32)
+                parts[pl.ds(pl.multiple_of(half + first, step), step), :] = low.astype(BF16)
             return total
 
         return values
@@ -788,8 +793,8 @@
             load_weight("cq", 0)
         if number == 13:
             share(3, theirs.at[0], arrived.at[0]).wait()
-            norm_share(1, add_stream(0, hidden, x2), 1, h2)
-            give(14, x2)
+            norm_share(1, add_stream(0, hidden, x2, x2_parts), 1, h2)
+            give(14, x2_parts)
             wait_weight(1)
             k2[...] = dot_nn(text[...], weights[1]).astype(BF16)
             give(8, k2)
@@ -846,7 +851,7 @@
         ((frames, part), BF16),
         *[((16, frames), F32)] * 2,
     ]
-    given = [*kept, ((shards[0].shape[0], width), F32), ((half, width), F32), ((half, width), F32)]
+    given = [*kept, ((shards[0].shape[0], width), F32), ((frames, width), BF16), ((half, width), F32)]
     given += [((frames, width), BF16), ((frames, 4 * part), BF16), ((frames, 4 * part), BF16)]
     held = [*kept, ((half, width), F32), ((half, width), F32)]
     outs = pl.pallas_call(
@@ -872,6 +877,7 @@
             vmem((2, half, width), BF16),
             vmem((frames, part), BF16),
             vmem((frames, part), BF16),
+            vmem((frames, width), BF16),
             dma,
             dma((2, 16)),
             dma((3,)),
@@ -894,7 +900,7 @@
 WIDTH_Z, WIDTH_A, SLOTS = 384, 128, 7
 ROWS_L = 6
 FIRST_L = (0, 12, 24, 27, 36, 39)
-LOAD_L = ((2, 10), (3, 11), (4, 14), (5, 15))
+LOAD_L = ((2, 11), (3, 11), (4, 14), (5, 15))
 FIRST_R = ((0, 12), (12, 24), (24, 27), (27, 30), (36, 39))
 TEXT_UNITS = (30, 36)
 SELF_UNITS = (39, 48)
@@ -909,10 +915,11 @@
     length = k_ref.shape[0]
     acc_k[pl.ds(0, length), :] = jnp.zeros((length, 128), F32)
     acc_v[pl.ds(0, length), :] = jnp.zeros((length, 128), F32)
-    block = 256
-    keep = lax.broadcasted_iota(jnp.int32, (block, block), 0) <= lax.broadcasted_iota(
-        jnp.int32, (block, block), 1
-    )
+    block = 256 if causal else q_ref.shape[0]
+    if causal:
+        keep = lax.broadcasted_iota(jnp.int32, (block, block), 0) <= lax.broadcasted_iota(
+            jnp.int32, (block, block), 1
+        )
 
     def merged(ref, rows, lane, value):
         before = jnp.where(half == 0, 0.0, ref[rows, lane].astype(F32))
@@ -957,7 +964,7 @@
     (gz, ga, xdz, ydz, xaz, yaz, xbz, ybz, lnz), refs = refs[:9], refs[9:]
     (xda, yda, xaa, yaa, xba, yba, lna, oz, oa), refs = refs[:9], refs[9:]
     (lbuf, rbuf, text_v, dkv_v, k2_v, v2_v, pool, dqkv, acc_k, acc_v), refs = refs[:10], refs[10:]
-    (acc, grad, xbuf, theirs, arrived, weights, text_part, text_send, text_got), refs = refs[:9], refs[9:]
+    (acc, grad, theirs, arrived, weights, text_part, text_send, text_got), refs = refs[:8], refs[8:]
     (norm_grads, got), refs = refs[:2], refs[2:]
     (first_sem, l_sem, r_sem, out_sem, send_z, send_a, recv_z, recv_a), refs = refs[:8], refs[8:]
     (pool_sem, slope_sem, weight_sem, x_sem, keep_sem, share_send, share_recv, norm_send), refs = refs[:8], refs[8:]
@@ -1288,6 +1295,10 @@
     def to_other(n, src, dst):
         return remote(src, dst, share_send.at[n], share_recv.at[n], other)
 
+    def active_copy(whose, n):
+        lines = pl.ds(pl.multiple_of(whose * half_rows, half_rows), half_rows)
+        return keep_copy(0, a_h.at[lines, pl.ds(n * 2 * part, 2 * part)], theirs)
+
     def share_sum(n):
         return to_other(n, theirs, arrived.at[n % 2])
 
@@ -1340,23 +1351,7 @@
         norm_grads[2 * kind : 2 * kind + 1, :] = gains
         norm_grads[2 * kind + 1 : 2 * kind + 2, :] = shifts
 
-    def streamed(ref):
-        step = xbuf.shape[1]
-
-        def copy(i):
-            first = pl.multiple_of(i * step, step)
-            return pltpu.make_async_copy(
-                ref.at[pl.ds(first, step), :], xbuf.at[lax.rem(i, 2)], x_sem.at[lax.rem(i, 2)]
-            )
-
-        copy(jnp.int32(0)).start()
-
-        def load(i, lines):
-            copy(i).wait()
-            pl.when(i + 1 < half_rows // step)(copy(i + 1).start)
-            return xbuf[lax.rem(i, 2)]
-
-        return load
+    x2_copy = pltpu.make_async_copy(x2_h, lbuf.at[0], x_sem)
 
     def store_branch(first, lines, value):
         grad[lines, :] = value
@@ -1396,6 +1391,7 @@
 
     def turn_4():
         du_copy(3).wait()
+        keep_copy(3, x3_h, grad).start()
         multiply(core, pooled(3), 1, True)
         weight_copy(1, w_up, 1).start()
         use(0)
@@ -1413,10 +1409,11 @@
     def turn_6():
         pool_copy(0, q2_h).start()
         share_sum(0).wait()
+        keep_copy(3, x3_h, grad).wait()
         norm_back(
             2,
             0,
-            streamed(x3_h),
+            lambda i, lines: grad[lines, :],
             lambda first, lines: lbuf[
                 0, pl.ds(pl.multiple_of(core * half_rows + first, 64), 64), :
             ].astype(F32),
@@ -1426,6 +1423,7 @@
 
     def turn_7():
         share_branch(0).wait()
+        x2_copy.start()
         keep_copy(1, dqkv.at[:, wide], e2_h).start()
         use(0)
         project_to(1, 0)
@@ -1453,7 +1451,7 @@
             )
             return carry
 
-        lax.fori_loop(0, heads, body, 0)
+        lax.fori_loop(0, heads, body, 0, unroll=2)
         keep_copy(1, dqkv.at[:, wide], e2_h).wait()
         keep_copy(0, pool.at[2], dq2_h).start()
         use(0)
@@ -1483,7 +1481,15 @@
         for n, ref in enumerate((q1_h, k1_h, v1_h)):
             pool_copy(n, ref).start()
         share_sum(1).wait()
-        norm_back(1, 1, streamed(x2_h), lambda first, lines: grad[lines, :], store_branch)
+        x2_copy.wait()
+        norm_back(
+            1,
+            1,
+            lambda i, lines: lbuf[0, lines, :].astype(F32)
+            + lbuf[0, pl.ds(pl.multiple_of(half_rows + i * 64, 64), 64), :].astype(F32),
+            lambda first, lines: grad[lines, :],
+            store_branch,
+        )
         share_branch(1).start()
         text_share().wait()
         text_part[:, pl.ds(0, features // 2)] = text_part[:, text_columns(core)] + text_got[
@@ -1496,8 +1502,9 @@
         keep_copy(1, dqkv.at[:, wide], e1_h).start()
         use(0)
         project_to(3, 0)
-        weight_copy(0, w_q).start()
-        weight_copy(1, w_k).start()
+        weight_copy(0, w_down, 0).start()
+        weight_copy(1, w_down, 1).start()
+        active_copy(1 - core, 0).start()
 
     def turn_12():
         keep_copy(1, dqkv.at[:, wide], e1_h).wait()
@@ -1520,9 +1527,60 @@
             True,
         )
 
+    def held(n):
+        return lambda rows_of: theirs[rows_of, pl.ds(n * part, part)]
+
+    def turn_13():
+        active_copy(core, 0).wait()
+        use(0)
+        multiply(0, held(0), 0, True)
+        weight_copy(0, w_down, 2).start()
+        use(1)
+        multiply(0, held(1), 1, False)
+        weight_copy(1, w_down, 3).start()
+        active_copy(1 - core, 1).start()
+
+    def turn_14():
+        active_copy(core, 0).wait()
+        use(0)
+        multiply(0, held(0), 0, False)
+        use(1)
+        multiply(0, held(1), 1, False)
+        send_sum(3)
+
+    def turn_15():
+        share_sum(3).wait()
+        keep_copy(3, x3_h, acc).start()
+        active_copy(core, 1).start()
+
+    def turn_16():
+        active_copy(core, 0).wait()
+        keep_copy(3, x3_h, acc).wait()
+        multiply(0, held(0), 0, False)
+        weight_copy(0, w_down, 0).start()
+        multiply(0, held(1), 1, False)
+        weight_copy(1, w_down, 1).start()
+        active_copy(core, 0).start()
+
+    def turn_17():
+        active_copy(core, 0).wait()
+        use(0)
+        multiply(0, held(0), 0, False)
+        weight_copy(0, w_q).start()
+        use(1)
+        multiply(0, held(1), 1, False)
+        weight_copy(1, w_k).start()
+
+        def body(i, carry):
+            lines = pl.ds(pl.multiple_of(i * 64, 64), 64)
+            theirs[lines, :] = (acc[lines, :] + arrived[1, lines, :].astype(F32)).astype(BF16)
+            return carry
+
+        lax.fori_loop(0, half_rows // 64, body, 0)
+        keep_copy(0, theirs, layer_out).start()
+
     def turn_18():
-        for n in range(4):
-            pool_copy(n, a_h, n).start()
+        keep_copy(0, theirs, layer_out).wait()
         use(0)
         multiply(1 - core, headed(0), 0, True)
         weight_copy(0, w_v).start()
@@ -1534,20 +1592,17 @@
         multiply(1 - core, headed(2), 0, False)
         send_sum(2)
         multiply(core, headed(2), 0, True)
-        weight_copy(0, w_down, 0).start()
         multiply(core, headed(1), 1, False)
         weight_copy(1, w_q).start()
 
     def turn_20():
         use(1)
         multiply(core, headed(0), 1, False)
-        weight_copy(1, w_down, 1).start()
+        share_sum(2).wait()
+        keep_copy(1, x1_h, theirs).start()
 
     def turn_21():
-        share_sum(2).wait()
-        hidden = keep_copy(1, x1_h, theirs)
-        hidden.start()
-        hidden.wait()
+        keep_copy(1, x1_h, theirs).wait()
 
         def store(first, lines, value):
             grad[lines, :] = value
@@ -1560,45 +1615,6 @@
             store,
         )
         keep_copy(3, grad, grad_input).start()
-
-    def turn_22():
-        for n in range(4):
-            pool_copy(n, a_h, n).wait()
-        use(0)
-        multiply(1 - core, pooled(0), 0, True)
-        weight_copy(0, w_down, 2).start()
-        use(1)
-        multiply(1 - core, pooled(1), 1, False)
-        weight_copy(1, w_down, 3).start()
-
-    def turn_23():
-        keep_copy(3, grad, grad_input).wait()
-        keep_copy(1, x3_h, grad).start()
-        use(0)
-        multiply(1 - core, pooled(2), 0, False)
-        use(1)
-        multiply(1 - core, pooled(3), 1, False)
-        send_sum(3)
-        multiply(core, pooled(2), 0, True)
-        weight_copy(0, w_down, 0).start()
-        multiply(core, pooled(3), 1, False)
-        weight_copy(1, w_down, 1).start()
-
-    def turn_24():
-        use(0)
-        multiply(core, pooled(0), 0, False)
-        use(1)
-        multiply(core, pooled(1), 1, False)
-
-    def turn_25():
-        share_sum(3).wait()
-        keep_copy(1, x3_h, grad).wait()
-        for first in range(0, half_rows, 64):
-            lines = pl.ds(first, 64)
-            theirs[lines, :] = (
-                grad[lines, :] + (acc[lines, :] + arrived[1, lines, :].astype(F32))
-            ).astype(BF16)
-        keep_copy(0, theirs, layer_out).start()
 
     def norm_copy(step):
         return remote(
@@ -1629,14 +1645,15 @@
         9: turn_9,
         10: turn_10,
         11: turn_11,
+        13: turn_13,
+        14: turn_14,
+        15: turn_15,
+        16: turn_16,
+        17: turn_17,
         18: turn_18,
         19: turn_19,
         20: turn_20,
         21: turn_21,
-        22: turn_22,
-        23: turn_23,
-        24: turn_24,
-        25: turn_25,
     }
     stages = (begin, second, third, fourth, fifth, finish)
     left_copy(0).start()
@@ -1683,7 +1700,7 @@
     for c in (total - 2, total - 1):
         for copy in out_copies(jnp.int32(c)):
             copy.wait()
-    keep_copy(0, theirs, layer_out).wait()
+    keep_copy(3, grad, grad_input).wait()
     keep_copy(1, got.at[2 * len(partners)], norm_out).wait()
     keep_copy(2, text_part.at[:, pl.ds(0, features // 2)], grad_text).wait()
 
@@ -1731,7 +1748,6 @@
             vmem((frames, 3 * part), BF16),
             *[vmem((frames, 128), F32)] * 2,
             *[vmem((half, width), F32)] * 2,
-            vmem((2, 64, width), F32),
             vmem((half, width), BF16),
             vmem((2, half, width), BF16),
             vmem((2, width, part), BF16),
@@ -1750,7 +1766,7 @@
             dma((4,)),
             dma,
             dma((2,)),
-            dma((2,)),
+            dma,
             dma((4,)),
             dma((7,)),
             dma((7,)),

time: 628 us -> 620 us (0.987)
  no operation moved by 1% of the time
where the time goes in v6:
time: 620 us; the launch traced here: 613 us
  Pallas kernels  599 us (97%)
  local copies, waits for them, and re-layouts  13.3 us (2%)
    pallas_call x1, Pallas kernels, backward_all(): pl.pallas_call(backward_kernel, out_shape=[shape((rows, UNITS * UNIT), F3...  316 us
    pallas_call x1, Pallas kernels, forward_all(): pl.pallas_call(functools.partial(forward_kernel, chunks, count), out_shap...  283 us

profile of v6, /device:TPU:0, one launch (start us, length us, event | category | flops | bytes accessed | tf_op | source)
XLA Modules:
  0.0 612.9 jit_solution(6799135028736892288)
XLA Ops:
  0.7 0.8 stack.27
  1.4 0.6 pad.4.refs_0_
  2.0 282.6 %forward.1 = (bf16[4,2,2,32,128]{4,3,2,1,0:T(8,128)(2,1)}, bf16[4,2,2,96,768]{4,3,2,1,0:T(8,128)(2,1)}, bf16[4,2,2,96,768]{4,3,2,1,0:T(8,128)(2,1)}, bf16[4,2,2,...) custom-call(bf16[32,128]{1,0:T(8,128)(2,1)} %pad.4.refs_0_, ...), custom_call_target="tpu_custom_call" | custom-call | tf_op jit(solution)/shard_map/forward/pallas_call | solution.py:857
  284.6 316.2 %backward.1 = (f32[96,12288]{1,0:T(8,128)}, bf16[512,1536]{1,0:T(8,128)(2,1)}, f32[512,1536]{1,0:T(8,128)}, f32[64,768]{1,0:T(8,128)}, f32[8,1536]{1,0:T(8,128)}...) custom-call(bf16[1024,1536]{1,0:T(8,128)(2,1)} %get-tuple-element.53, ...), custom_call_target="tpu_custom_call" | custom-call | tf_op jit(solution)/shard_map/backward/pallas_call | solution.py:1718
  600.8 0.0 copy-start
  600.8 3.2 fusion.1
  604.0 0.7 copy-done
  604.7 1.6 fusion
  606.3 0.0 copy-start.1
  606.3 0.9 constant_dynamic-slice_fusion
  607.2 0.5 slice_bitcast_fusion.7
  607.7 2.7 copy.41
  610.4 0.0 copy-done.1
  610.4 0.0 copy-start.2
  610.4 1.7 copy.42
  612.1 0.0 copy-done.2
  612.1 0.7 copy.43
Async XLA Ops:
  600.8 3.9 copy-start
  606.3 4.1 copy-start.1
  610.4 1.7 copy-start.2

commit v7 on v6

--- a/solution.py
+++ b/solution.py
@@ -805,7 +805,6 @@
             wait_weight(0)
             project_rows(h2, weights.at[0], to(q2))
             give(7, q2)
-        if number == 15:
 
             def body(pair, carry):
                 pair_forward(pair, q2, k2, v2, o2, lse2, False)
@@ -814,19 +813,19 @@
             lax.fori_loop(0, q2.shape[1] // 128, body, 0)
             give(10, o2)
             give(12, lse2)
-        if number == 16:
+        if number == 15:
             wait_weight(1)
             out_project(1, o2, 1)
-        if number == 17:
+        if number == 16:
             share(4, theirs.at[1], arrived.at[1]).wait()
             norm_share(2, add_stream(1, x2, x3), 2, h3)
             give(15, x3)
             load_weight("up", 0)
-        if number == 18:
+        if number == 17:
             get_share(2, h3)
             give(2, h3)
-        if 18 <= number < 22:
-            hidden_units(number - 18)
+        for j in {17: (0,), 18: (1, 2), 19: (3,)}.get(number, ()):
+            hidden_units(j)
 
     for number in range(len(chunks) + 5):
         turn(number)

time: 620 us -> 613 us (0.989)
  Pallas kernels: 599 us -> 591 us
where the time goes in v7:
time: 613 us; the launch traced here: 605 us
  Pallas kernels  591 us (96%)
  local copies, waits for them, and re-layouts  13.3 us (2%)
    pallas_call x1, Pallas kernels, backward_all(): pl.pallas_call(backward_kernel, out_shape=[shape((rows, UNITS * UNIT), F3...  315 us
    pallas_call x1, Pallas kernels, forward_all(): pl.pallas_call(functools.partial(forward_kernel, chunks, count), out_shap...  276 us

profile of v7, /device:TPU:0, one launch (start us, length us, event | category | flops | bytes accessed | tf_op | source)
XLA Modules:
  0.0 605.5 jit_solution(16595584943094596156)
XLA Ops:
  0.7 0.8 stack.27
  1.4 0.6 pad.4.refs_0_
  2.0 276.5 %forward.1 = (bf16[4,2,2,32,128]{4,3,2,1,0:T(8,128)(2,1)}, bf16[4,2,2,96,768]{4,3,2,1,0:T(8,128)(2,1)}, bf16[4,2,2,96,768]{4,3,2,1,0:T(8,128)(2,1)}, bf16[4,2,2,...) custom-call(bf16[32,128]{1,0:T(8,128)(2,1)} %pad.4.refs_0_, ...), custom_call_target="tpu_custom_call" | custom-call | tf_op jit(solution)/shard_map/forward/pallas_call | solution.py:856
  278.5 314.8 %backward.1 = (f32[96,12288]{1,0:T(8,128)}, bf16[512,1536]{1,0:T(8,128)(2,1)}, f32[512,1536]{1,0:T(8,128)}, f32[64,768]{1,0:T(8,128)}, f32[8,1536]{1,0:T(8,128)}...) custom-call(bf16[1024,1536]{1,0:T(8,128)(2,1)} %get-tuple-element.53, ...), custom_call_target="tpu_custom_call" | custom-call | tf_op jit(solution)/shard_map/backward/pallas_call | solution.py:1717
  593.3 0.0 copy-start
  593.4 3.2 fusion.1
  596.5 0.7 copy-done
  597.3 1.6 fusion
  598.8 0.0 copy-start.1
  598.8 0.9 constant_dynamic-slice_fusion
  599.7 0.5 slice_bitcast_fusion.7
  600.3 2.7 copy.41
  602.9 0.0 copy-done.1
  602.9 0.0 copy-start.2
  602.9 1.7 copy.42
  604.6 0.0 copy-done.2
  604.6 0.7 copy.43
Async XLA Ops:
  593.3 3.9 copy-start
  598.8 4.1 copy-start.1
  602.9 1.7 copy-start.2

commit v8 on v7

--- a/solution.py
+++ b/solution.py
@@ -1669,14 +1669,14 @@
     left_copy(0).wait()
 
     def body(turn, carry):
+        pl.when(turn < total)(lambda: compute(turn, lax.rem(turn, slots)))
         for step, stage in enumerate(stages):
-            c = turn - step - 1
+            c = turn - step
 
             @pl.when((c >= 0) & (c < total))
             def _():
                 stage(c, lax.rem(c, slots))
 
-        pl.when(turn < total)(lambda: compute(turn, lax.rem(turn, slots)))
         pl.when(turn < 4)(lambda: feed_forward(turn))
         for number, fn in chain.items():
             pl.when(turn == number)(fn)
@@ -1695,7 +1695,7 @@
             pl.when(turn == 22 + step)(functools.partial(norm_sum, step))
         return carry
 
-    lax.fori_loop(0, total + len(stages), body, 0)
+    lax.fori_loop(0, total + len(stages) - 1, body, 0)
     for c in (total - 2, total - 1):
         for copy in out_copies(jnp.int32(c)):
             copy.wait()

time: 613 us -> 608 us (level)
  no operation moved by 1% of the time
where the time goes in v8:
time: 608 us; the launch traced here: 600 us
  Pallas kernels  586 us (96%)
  local copies, waits for them, and re-layouts  13.3 us (2%)
    pallas_call x1, Pallas kernels, backward_all(): pl.pallas_call(backward_kernel, out_shape=[shape((rows, UNITS * UNIT), F3...  310 us
    pallas_call x1, Pallas kernels, forward_all(): pl.pallas_call(functools.partial(forward_kernel, chunks, count), out_shap...  276 us

profile of v8, /device:TPU:0, one launch (start us, length us, event | category | flops | bytes accessed | tf_op | source)
XLA Modules:
  0.0 600.3 jit_solution(12493800341389088989)
XLA Ops:
  0.7 0.8 stack.27
  1.4 0.6 pad.4.refs_0_
  2.0 276.5 %forward.1 = (bf16[4,2,2,32,128]{4,3,2,1,0:T(8,128)(2,1)}, bf16[4,2,2,96,768]{4,3,2,1,0:T(8,128)(2,1)}, bf16[4,2,2,96,768]{4,3,2,1,0:T(8,128)(2,1)}, bf16[4,2,2,...) custom-call(bf16[32,128]{1,0:T(8,128)(2,1)} %pad.4.refs_0_, ...), custom_call_target="tpu_custom_call" | custom-call | tf_op jit(solution)/shard_map/forward/pallas_call | solution.py:856
  278.5 309.7 %backward.1 = (f32[96,12288]{1,0:T(8,128)}, bf16[512,1536]{1,0:T(8,128)(2,1)}, f32[512,1536]{1,0:T(8,128)}, f32[64,768]{1,0:T(8,128)}, f32[8,1536]{1,0:T(8,128)}...) custom-call(bf16[1024,1536]{1,0:T(8,128)(2,1)} %get-tuple-element.53, ...), custom_call_target="tpu_custom_call" | custom-call | tf_op jit(solution)/shard_map/backward/pallas_call | solution.py:1717
  588.2 0.0 copy-start
  588.2 3.2 fusion.1
  591.4 0.7 copy-done
  592.1 1.6 fusion
  593.7 0.0 copy-start.1
  593.7 0.9 constant_dynamic-slice_fusion
  594.6 0.5 slice_bitcast_fusion.7
  595.2 2.7 copy.41
  597.8 0.0 copy-done.1
  597.8 0.0 copy-start.2
  597.8 1.7 copy.42
  599.5 0.0 copy-done.2
  599.5 0.7 copy.43
Async XLA Ops:
  588.2 3.9 copy-start
  593.7 4.1 copy-start.1
  597.8 1.7 copy-start.2
